TPU v7x, 128 devices: a whole 4x4x4 slice. The times are simulated.
128 devices in a mesh: tm: 64 (over z, y, x), space: 2 (over core).
Axes of the slice: x: 4, y: 4, z: 4, core: 2. Of those that a mesh axis runs over, the one named last changes fastest.
Arguments:
- coeffs: float32 [4, 8, 2, 512, 1024], P(None, None, 'space', 'tm'), may hold values from -2.5 to 2.5
Outputs:
- wilson: float32 [2, 3, 3, 2, 512, 1024], P(None, None, None, 'space', 'tm')
All inputs are finite; a program needn't handle non-finite values.
Results may differ from a plain program's by a relative error of at most 0.000088.
Values sent between devices are 32-bit elements; how exact they have to be, the bound alone decides.
No kernel may reach another device: no remote copies, remote signals or barrier semaphores. Data moves between devices by JAX's collectives and lax.ppermute only.
A program may use at most 64 MiB of HBM per device.

v0:
```python
import jax
import jax.numpy as jnp
from jax import lax
from jax.experimental import pallas as pl
from jax.experimental.pallas import tpu as pltpu
from jax.sharding import PartitionSpec as P

ZDIM = 32
LANES = 128
ROWS = 8
NT_LOCAL = 8
SMEAR = 0.1
ROOT_THIRD = 1.0 / 3.0**0.5
VMEM_LIMIT = 48 * 1024 * 1024
WHOLE = pl.BlockSpec(memory_space=pltpu.VMEM)


def read(ref, *index):
    re = [[ref[(*index, 3 * i + j)] for j in range(3)] for i in range(3)]
    im = [[ref[(*index, 9 + 3 * i + j)] for j in range(3)] for i in range(3)]
    return re, im


def write(ref, matrix, *index):
    for part in range(2):
        for i in range(3):
            for j in range(3):
                ref[(*index, 9 * part + 3 * i + j)] = matrix[part][i][j]


def dagger(matrix):
    re, im = matrix
    return (
        [[re[j][i] for j in range(3)] for i in range(3)],
        [[-im[j][i] for j in range(3)] for i in range(3)],
    )


def row_times(row, matrix, conj_left=False, conj_right=False):
    a, b = row
    c, d = matrix
    out_re, out_im = [], []
    for j in range(3):
        rr = a[0] * c[0][j]
        ii = b[0] * d[0][j]
        ri = a[0] * d[0][j]
        ir = b[0] * c[0][j]
        for m in (1, 2):
            rr = rr + a[m] * c[m][j]
            ii = ii + b[m] * d[m][j]
            ri = ri + a[m] * d[m][j]
            ir = ir + b[m] * c[m][j]
        out_re.append(rr + ii if conj_left != conj_right else rr - ii)
        if conj_left and conj_right:
            out_im.append(-(ri + ir))
        elif conj_left:
            out_im.append(ri - ir)
        elif conj_right:
            out_im.append(ir - ri)
        else:
            out_im.append(ri + ir)
    return out_re, out_im


def mul(left, right):
    re, im = [], []
    for i in range(3):
        r, m = row_times((left[0][i], left[1][i]), right)
        re.append(r)
        im.append(m)
    return re, im


def transposed(matrix):
    return tuple([[part[j][i] for j in range(3)] for i in range(3)] for part in matrix)


def forward_term(link, temporal, ahead):
    turned = transposed(ahead)
    re, im = [], []
    for i in range(3):
        row = row_times((link[0][i], link[1][i]), temporal)
        r, m = row_times(row, turned, conj_right=True)
        re.append(r)
        im.append(m)
    return re, im


def backward_term(link, temporal, ahead):
    turned = transposed(link)
    re, im = [], []
    for i in range(3):
        row = row_times((turned[0][i], turned[1][i]), temporal, conj_left=True)
        r, m = row_times(row, ahead)
        re.append(r)
        im.append(m)
    return re, im


def plus(left, right):
    return tuple(
        [[left[p][i][j] + right[p][i][j] for j in range(3)] for i in range(3)] for p in range(2)
    )


def mapped(f, matrix):
    return tuple([[f(part[i][j]) for j in range(3)] for i in range(3)] for part in matrix)


def lane():
    return lax.broadcasted_iota(jnp.int32, (ROWS, LANES), 1)


def from_y_above(x):
    r = pltpu.roll(x, LANES - ZDIM, 1)
    return jnp.where(lane() >= LANES - ZDIM, pltpu.roll(r, ROWS - 1, 0), r)


def from_y_below(x):
    r = pltpu.roll(x, ZDIM, 1)
    return jnp.where(lane() < ZDIM, pltpu.roll(r, 1, 0), r)


def from_z_above(x):
    edge = lane() % ZDIM == ZDIM - 1
    return jnp.where(edge, pltpu.roll(x, ZDIM - 1, 1), pltpu.roll(x, LANES - 1, 1))


def from_z_below(x):
    edge = lane() % ZDIM == 0
    return jnp.where(edge, pltpu.roll(x, LANES - ZDIM + 1, 1), pltpu.roll(x, 1, 1))


def squared(d, g01, g02, g12):
    n01 = g01[0] * g01[0] + g01[1] * g01[1]
    n02 = g02[0] * g02[0] + g02[1] * g02[1]
    n12 = g12[0] * g12[0] + g12[1] * g12[1]
    s = (d[0] * d[0] + (n01 + n02), d[1] * d[1] + (n01 + n12), d[2] * d[2] + (n02 + n12))
    k = (g01[0] * g12[0] - g01[1] * g12[1], g01[0] * g12[1] + g01[1] * g12[0])
    s02 = (k[0] - d[1] * g02[0], k[1] - d[1] * g02[1])
    s01 = (
        (g02[0] * g12[0] + g02[1] * g12[1]) - d[2] * g01[0],
        (g02[1] * g12[0] - g02[0] * g12[1]) - d[2] * g01[1],
    )
    s12 = (
        (g01[0] * g02[0] + g01[1] * g02[1]) - d[0] * g12[0],
        (g01[0] * g02[1] - g01[1] * g02[0]) - d[0] * g12[1],
    )
    det = (
        d[0] * (d[1] * d[2] - n12)
        - d[1] * n02
        - d[2] * n01
        + 2.0 * (k[0] * g02[0] + k[1] * g02[1])
    )
    return s, s01, s02, s12, det


def link_of(c):
    d2 = c[7] * (-2.0 * ROOT_THIRD)
    e = c[7] * ROOT_THIRD
    d = (e + c[2], e - c[2], d2)
    g01, g02, g12 = (c[0], -c[1]), (c[3], -c[4]), (c[5], -c[6])
    s, s01, s02, s12, det = squared(d, g01, g02, g12)
    p = (s[0] + s[1] + s[2]) * 0.125
    q = det * 0.125
    qq = q * q
    w = (p * (-1.0 / 5040.0) + 1.0 / 120.0) * p - 1.0 / 6.0
    f0r = qq * (p * (1.0 / 20160.0) - 1.0 / 720.0) + 1.0
    f0i = q * w
    f1r = q * ((p * (0.5 / 13440.0) - 0.5 / 360.0) * p + 0.5 / 24.0)
    f1i = (p * w + qq * (-1.0 / 5040.0)) * 0.5 + 0.5
    f2r = ((p * (0.25 / 40320.0) - 0.25 / 720.0) * p + 0.25 / 24.0) * p + (qq * (0.25 / 40320.0) - 0.125)
    f2i = q * (p * (-0.5 / 5040.0) + 0.25 / 120.0)
    re = [[None] * 3 for _ in range(3)]
    im = [[None] * 3 for _ in range(3)]
    for j in range(3):
        re[j][j] = f0r + (f1r * d[j] + f2r * s[j])
        im[j][j] = f0i + (f1i * d[j] + f2i * s[j])
    for j, k, g, h in ((0, 1, g01, s01), (0, 2, g02, s02), (1, 2, g12, s12)):
        rr = f1r * g[0] + f2r * h[0]
        ii = f1i * g[1] + f2i * h[1]
        ir = f1i * g[0] + f2i * h[0]
        ri = f1r * g[1] + f2r * h[1]
        re[j][k], re[k][j] = rr - ii, rr + ii
        im[j][k], im[k][j] = ir + ri, ir - ri
    return re, im


def smearing(staple, temporal):
    cr, ci = staple
    ur, ui = temporal

    def omega_re(j, k):
        t = cr[j][0] * ur[k][0] + ci[j][0] * ui[k][0]
        for m in (1, 2):
            t = t + (cr[j][m] * ur[k][m] + ci[j][m] * ui[k][m])
        return t

    def omega_im(j, k):
        t = ci[j][0] * ur[k][0] - cr[j][0] * ui[k][0]
        for m in (1, 2):
            t = t + (ci[j][m] * ur[k][m] - cr[j][m] * ui[k][m])
        return t

    half = 0.5 * SMEAR
    diag = [omega_im(j, j) for j in range(3)]
    third = (diag[0] + diag[1] + diag[2]) * (1.0 / 3.0)
    d = [(x - third) * SMEAR for x in diag]
    g = {}
    for j, k in ((0, 1), (0, 2), (1, 2)):
        g[j, k] = (
            (omega_im(j, k) + omega_im(k, j)) * half,
            (omega_re(k, j) - omega_re(j, k)) * half,
        )
    s, s01, s02, s12, q = squared(d, g[0, 1], g[0, 2], g[1, 2])
    p = (s[0] + s[1] + s[2]) * 0.5
    f1 = p * (-1.0 / 6.0) + 1.0
    f0i = q * (-1.0 / 6.0)
    re = [[None] * 3 for _ in range(3)]
    im = [[None] * 3 for _ in range(3)]
    for j in range(3):
        re[j][j] = 1.0 - 0.5 * s[j]
        im[j][j] = f0i + f1 * d[j]
    for j, k, h in ((0, 1, s01), (0, 2, s02), (1, 2, s12)):
        a = f1 * g[j, k][0]
        b = f1 * g[j, k][1]
        c = 0.5 * h[0]
        e = 0.5 * h[1]
        re[j][k], re[k][j] = -b - c, b - c
        im[j][k], im[k][j] = a - e, a + e
    return re, im


def slice_of(rows, direction, t):
    return [rows[direction, a, pl.ds(t, ROWS, stride=NT_LOCAL), :] for a in range(8)]


def fetch(coeffs, rows, sems, directions):
    copies = []
    for n, direction in enumerate(directions):
        for v in range(ROWS):
            copies.append(
                pltpu.make_async_copy(
                    coeffs.at[direction, :, 0, :, pl.ds(v * LANES, LANES)],
                    rows.at[n, :, pl.ds(v * NT_LOCAL, NT_LOCAL), :],
                    sems.at[n, v],
                )
            )
    return copies


def plane_terms(spatial, temporal, ahead, above, below):
    forward = forward_term(spatial, mapped(above, temporal), ahead)
    return plus(forward, mapped(below, backward_term(spatial, temporal, ahead)))


def local_kernel(coeffs, links, staple, rows, sems):
    copies = fetch(coeffs, rows, sems, range(4))
    for copy in copies:
        copy.start()
    for copy in copies:
        copy.wait()
    last = NT_LOCAL - 1
    for direction in range(4):
        write(links, link_of(slice_of(rows, direction, last)), direction, last)

    def step(i, carry):
        t = last - 1 - i
        for direction in range(4):
            write(links, link_of(slice_of(rows, direction, t)), direction, t)
        terms = plane_terms(
            read(links, 1, t), read(links, 3, t), read(links, 1, t + 1), from_y_above, from_y_below
        )
        write(staple, terms, t)
        terms = plane_terms(
            read(links, 2, t), read(links, 3, t), read(links, 2, t + 1), from_z_above, from_z_below
        )
        write(staple, plus(read(staple, t), terms), t)
        return carry

    lax.fori_loop(0, last, step, 0)


def join_kernel(
    links, staple, other, next_rows, other_next, partial, total, rows, ahead, other_ahead, other_links, terms, sems
):
    copies = fetch(other, rows, sems, (0, 3))
    for copy in copies:
        copy.start()
    last = NT_LOCAL - 1
    for direction in range(3):
        write(ahead, link_of([next_rows[direction, a] for a in range(8)]), direction)
    write(other_ahead, link_of([other_next[a] for a in range(8)]))
    write(
        terms,
        plane_terms(
            read(links, 1, last), read(links, 3, last), read(ahead, 1), from_y_above, from_y_below
        ),
    )
    write(
        terms,
        plus(
            read(terms),
            plane_terms(
                read(links, 2, last), read(links, 3, last), read(ahead, 2), from_z_above, from_z_below
            ),
        ),
    )
    one = jnp.ones((ROWS, LANES), jnp.float32)
    zero = jnp.zeros((ROWS, LANES), jnp.float32)
    unit = (
        [[one if i == j else zero for j in range(3)] for i in range(3)],
        [[zero] * 3 for _ in range(3)],
    )
    write(total, unit)
    for copy in copies:
        copy.wait()

    def step(i, carry):
        t = last - i
        write(other_links, link_of(slice_of(rows, 0, t)), 0)
        write(other_links, link_of(slice_of(rows, 1, t)), 1)
        write(
            terms,
            plus(read(terms), forward_term(read(links, 0, t), read(other_links, 1), read(ahead, 0))),
        )
        write(
            terms,
            plus(
                read(terms),
                backward_term(read(other_links, 0), read(other_links, 1), read(other_ahead)),
            ),
        )
        temporal = read(links, 3, t)
        smeared = mul(smearing(read(terms), temporal), temporal)
        running = mul(smeared, read(total))
        write(total, running)
        write(partial, running, t)
        write(ahead, read(links, 0, t), 0)
        write(other_ahead, read(other_links, 0))
        write(terms, read(staple, jnp.maximum(t - 1, 0)))
        return carry

    lax.fori_loop(0, NT_LOCAL, step, 0)


def level_kernel(low, own, by1, by2, by3, tail, new_total, new_tail, held):
    digit = lax.rem(lax.axis_index("tm") // low, 4)
    for k, ref in enumerate((own, by1, by2, by3)):
        for a in range(18):
            held[k, a] = ref[a]
    third = read(held, 3 ^ digit)
    second = mul(read(held, 2 ^ digit), third)
    first = mul(read(held, 1 ^ digit), second)
    write(new_total, mul(read(held, digit), first))
    one = jnp.ones((ROWS, LANES), jnp.float32)
    zero = jnp.zeros((ROWS, LANES), jnp.float32)
    unit = (
        [[one if i == j else zero for j in range(3)] for i in range(3)],
        [[zero] * 3 for _ in range(3)],
    )
    for k, matrix in enumerate((first, second, third, unit)):
        write(held, matrix, k)
    if tail is None:
        write(new_tail, read(held, digit))
    else:
        write(new_tail, mul(read(tail), read(held, digit)))


def first_level_kernel(low, own, by1, by2, by3, new_total, new_tail, held):
    level_kernel(low, own, by1, by2, by3, None, new_total, new_tail, held)


def closing_kernel(partial, tail, out, rows, sems):
    def step(t, carry):
        product = mul(read(partial, t), read(tail))
        for part in range(2):
            for i in range(3):
                for j in range(3):
                    rows[9 * part + 3 * i + j, pl.ds(t, ROWS, stride=NT_LOCAL), :] = product[part][i][j]
        return carry

    lax.fori_loop(0, NT_LOCAL, step, 0)
    copies = []
    for v in range(ROWS):
        copies.append(
            pltpu.make_async_copy(
                rows.at[:, pl.ds(v * NT_LOCAL, NT_LOCAL), :],
                out.at[:, :, pl.ds(v * LANES, LANES)],
                sems.at[v],
            )
        )
    for copy in copies:
        copy.start()
    for copy in copies:
        copy.wait()


def params():
    return pltpu.CompilerParams(vmem_limit_bytes=VMEM_LIMIT)


def field(*lead):
    return jax.ShapeDtypeStruct((*lead, 18, ROWS, LANES), jnp.float32)


def shards(coeffs):
    count = lax.axis_size("tm")
    next_rows = coeffs[0:3, :, 0, 0, :].reshape(3, 8, ROWS, LANES)
    other = lax.ppermute(coeffs, "space", [(0, 1), (1, 0)])
    ahead = lax.ppermute(next_rows, "tm", [((i + 1) % count, i) for i in range(count)])
    other_ahead = lax.ppermute(
        next_rows[0],
        ("tm", "space"),
        [(((i + 1) % count) * 2 + 1 - c, i * 2 + c) for i in range(count) for c in range(2)],
    )
    links, staple = pl.pallas_call(
        local_kernel,
        out_shape=(field(4, NT_LOCAL), field(NT_LOCAL)),
        in_specs=[pl.BlockSpec(memory_space=pl.ANY)],
        out_specs=(WHOLE, WHOLE),
        scratch_shapes=[
            pltpu.VMEM((4, 8, ROWS * NT_LOCAL, LANES), jnp.float32),
            pltpu.SemaphoreType.DMA((4, ROWS)),
        ],
        compiler_params=params(),
        cost_estimate=pl.CostEstimate(flops=20_000_000, bytes_accessed=4_000_000, transcendentals=0),
        name="local_terms",
    )(coeffs)
    partial, total = pl.pallas_call(
        join_kernel,
        out_shape=(field(NT_LOCAL), field()),
        in_specs=[WHOLE, WHOLE, pl.BlockSpec(memory_space=pl.ANY), WHOLE, WHOLE],
        out_specs=(WHOLE, WHOLE),
        scratch_shapes=[
            pltpu.VMEM((2, 8, ROWS * NT_LOCAL, LANES), jnp.float32),
            pltpu.VMEM((3, 18, ROWS, LANES), jnp.float32),
            pltpu.VMEM((18, ROWS, LANES), jnp.float32),
            pltpu.VMEM((2, 18, ROWS, LANES), jnp.float32),
            pltpu.VMEM((18, ROWS, LANES), jnp.float32),
            pltpu.SemaphoreType.DMA((2, ROWS)),
        ],
        compiler_params=params(),
        name="smear_and_join",
    )(links, staple, other, ahead, other_ahead)
    tail = None
    low = 1
    while low < count:
        received = [
            lax.ppermute(total, "tm", [(i, i ^ (low * k)) for i in range(count)]) for k in (1, 2, 3)
        ]
        kernel = first_level_kernel if tail is None else level_kernel
        operands = [total, *received] + ([] if tail is None else [tail])

        def body(*refs, kernel=kernel, low=low):
            kernel(low, *refs)

        total, tail = pl.pallas_call(
            body,
            out_shape=(field(), field()),
            in_specs=[WHOLE] * len(operands),
            out_specs=(WHOLE, WHOLE),
            scratch_shapes=[pltpu.VMEM((4, 18, ROWS, LANES), jnp.float32)],
            compiler_params=params(),
            name=f"level_{low}",
        )(*operands)
        low *= 4
    out = pl.pallas_call(
        closing_kernel,
        out_shape=jax.ShapeDtypeStruct((18, NT_LOCAL, ROWS * LANES), jnp.float32),
        in_specs=[WHOLE, WHOLE],
        out_specs=pl.BlockSpec(memory_space=pl.ANY),
        scratch_shapes=[
            pltpu.VMEM((18, ROWS * NT_LOCAL, LANES), jnp.float32),
            pltpu.SemaphoreType.DMA((ROWS,)),
        ],
        compiler_params=params(),
        name="closing",
    )(partial, tail)
    return out.reshape(2, 3, 3, 1, NT_LOCAL, ROWS * LANES)


def solution(mesh):
    in_specs = (P(None, None, "space", "tm", None),)
    out_specs = P(None, None, None, "space", "tm", None)
    return jax.shard_map(shards, mesh=mesh, in_specs=in_specs, out_specs=out_specs, check_vma=False)
```

profile of v0, /device:TPU:0, one launch (start us, length us, event | category | flops | bytes accessed | tf_op | source)
XLA Modules:
  0.0 45.4 jit_solution(5402130209977037774)
XLA Ops:
  0.0 0.0 collective-permute-start
  0.0 1.2 %slice.8 = f32[3,8,1,1,1024]{4,3,2,1,0:T(1,128)S(1)} slice(f32[4,8,1,8,1024]{4,3,2,1,0:T(8,128)} %coeffs.1), slice={[0:3], [0:8], [0:1], [0:1], [0:1024]} | slice | bytes 196608 | tf_op jit(solution)/shard_map/slice | solution.py:409
  1.2 8.8 %collective-permute-start.1 = (f32[3,8,8,128]{3,2,1,0:T(8,128)S(1)}, f32[3,8,8,128]{3,2,1,0:T(8,128)S(1)}, u32[]{:S(2)}, u32[]{:S(2)}) collective-permute-start(f32[3,8,8,128]{3,2,1,0:T(8,128)S(1)} %bitcast.5), channel_id=1, source_target_pairs={{2,0},{4,2},{6,4},{8,6},{10,8},{12,10},{14,12},{16,14},{18,16},{20... | collective-permute-start | bytes 294920 | tf_op jit(solution)/shard_map/ppermute | solution.py:411
  10.0 1.0 %slice.9 = f32[1,8,1,1,1024]{4,3,2,1,0:T(1,128)S(1)} slice(f32[4,8,1,8,1024]{4,3,2,1,0:T(8,128)} %coeffs.1), slice={[0:1], [0:8], [0:1], [0:1], [0:1024]} | slice | bytes 65536 | tf_op jit(solution)/shard_map/slice | solution.py:413
  11.0 0.7 %collective-permute-start.2 = (f32[8,8,128]{2,1,0:T(8,128)S(1)}, f32[8,8,128]{2,1,0:T(8,128)S(1)}, u32[]{:S(2)}, u32[]{:S(2)}) collective-permute-start(f32[8,8,128]{2,1,0:T(8,128)S(1)} %bitcast.6), channel_id=1, source_target_pairs={{3,0},{2,1},{5,2},{4,3},{7,4},{6,5},{9,6},{8,7},{11,8},{10,9},{13,... | collective-permute-start | bytes 98312 | tf_op jit(solution)/shard_map/ppermute | solution.py:412
  11.7 1.2 %copy-done = f32[4,8,1,8,1024]{4,3,2,1,0:T(8,128)S(1)} copy-done((f32[4,8,1,8,1024]{4,3,2,1,0:T(8,128)S(1)}, f32[4,8,1,8,1024]{4,3,2,1,0:T(8,128)}, u32[]{:S(2)}) %copy-start) | copy-done | bytes 1048600
  13.0 3.3 %local_terms.1 = (f32[4,8,18,8,128]{4,3,2,1,0:T(8,128)S(1)}, f32[8,18,8,128]{3,2,1,0:T(8,128)S(1)}) custom-call(f32[4,8,1,8,1024]{4,3,2,1,0:T(8,128)S(1)} %copy-done), custom_call_target="tpu_custom_call" | custom-call | flops 20000000 | bytes 4000000 | tf_op jit(solution)/shard_map/local_terms/pallas_call | solution.py:417
  16.3 0.0 collective-permute-done.2.other_next
  16.3 0.0 collective-permute-done.1.next_rows
  16.3 0.0 collective-permute-done.other
  16.3 2.8 %smear_and_join.1 = (f32[8,18,8,128]{3,2,1,0:T(8,128)S(1)}, f32[18,8,128]{2,1,0:T(8,128)S(1)}) custom-call(f32[4,8,18,8,128]{4,3,2,1,0:T(8,128)S(1)} %get-tuple-element.14.links, f32[8,18,8,128]{3,2,1,0:T(8,128)S(1)} %get-tuple-element.15.staple, f32[4,8,1,8,1024]{4,3,2,1,0:T(8,128)S(1)} %collective-permute-done.other, ...), custom_call_target="tpu_custom_call" | custom-call | tf_op jit(solution)/shard_map/smear_and_join/pallas_call | solution.py:430
  19.1 0.1 collective-permute-start.5
  19.2 3.3 %collective-permute-start.4 = (f32[18,8,128]{2,1,0:T(8,128)S(1)}, f32[18,8,128]{2,1,0:T(8,128)S(1)}, u32[]{:S(2)}, u32[]{:S(2)}) collective-permute-start(f32[18,8,128]{2,1,0:T(8,128)S(1)} %get-tuple-element.17.refs_0_), channel_id=1, source_target_pairs={{0,4},{2,6},{4,0},{6,2},{8,12},{10,14},{12,8},{14,10},{16,20},{18,... | collective-permute-start | bytes 221192 | tf_op jit(solution)/shard_map/ppermute | solution.py:450
  22.4 0.8 %collective-permute-start.3 = (f32[18,8,128]{2,1,0:T(8,128)S(1)}, f32[18,8,128]{2,1,0:T(8,128)S(1)}, u32[]{:S(2)}, u32[]{:S(2)}) collective-permute-start(f32[18,8,128]{2,1,0:T(8,128)S(1)} %get-tuple-element.17.refs_0_), channel_id=1, source_target_pairs={{0,2},{2,0},{4,6},{6,4},{8,10},{10,8},{12,14},{14,12},{16,18},{18,... | collective-permute-start | bytes 221192 | tf_op jit(solution)/shard_map/ppermute | solution.py:450
  23.3 3.2 %collective-permute-done.5.refs_3_ = f32[18,8,128]{2,1,0:T(8,128)S(1)} collective-permute-done((f32[18,8,128]{2,1,0:T(8,128)S(1)}, f32[18,8,128]{2,1,0:T(8,128)S(1)}, u32[]{:S(2)}, u32[]{:S(2)}) %collective-permute-start.5) | collective-permute-done | bytes 73760 | tf_op jit(solution)/shard_map/ppermute | solution.py:450
  26.4 0.0 collective-permute-done.4.refs_2_
  26.4 0.7 %collective-permute-done.3.refs_1_ = f32[18,8,128]{2,1,0:T(8,128)S(1)} collective-permute-done((f32[18,8,128]{2,1,0:T(8,128)S(1)}, f32[18,8,128]{2,1,0:T(8,128)S(1)}, u32[]{:S(2)}, u32[]{:S(2)}) %collective-permute-start.3) | collective-permute-done | bytes 73760 | tf_op jit(solution)/shard_map/ppermute | solution.py:450
  27.1 0.1 level_1.1
  27.3 0.1 collective-permute-start.8
  27.4 0.1 collective-permute-start.7
  27.5 4.0 %collective-permute-start.6 = (f32[18,8,128]{2,1,0:T(8,128)S(1)}, f32[18,8,128]{2,1,0:T(8,128)S(1)}, u32[]{:S(2)}, u32[]{:S(2)}) collective-permute-start(f32[18,8,128]{2,1,0:T(8,128)S(1)} %get-tuple-element.18.refs_0_), channel_id=1, source_target_pairs={{0,8},{2,10},{4,12},{6,14},{8,0},{10,2},{12,4},{14,6},{16,24},{18,... | collective-permute-start | bytes 221192 | tf_op jit(solution)/shard_map/ppermute | solution.py:450
  31.4 2.3 %collective-permute-done.8.refs_3_ = f32[18,8,128]{2,1,0:T(8,128)S(1)} collective-permute-done((f32[18,8,128]{2,1,0:T(8,128)S(1)}, f32[18,8,128]{2,1,0:T(8,128)S(1)}, u32[]{:S(2)}, u32[]{:S(2)}) %collective-permute-start.8) | collective-permute-done | bytes 73760 | tf_op jit(solution)/shard_map/ppermute | solution.py:450
  33.7 0.0 collective-permute-done.7.refs_2_
  33.7 0.9 %collective-permute-done.6.refs_1_ = f32[18,8,128]{2,1,0:T(8,128)S(1)} collective-permute-done((f32[18,8,128]{2,1,0:T(8,128)S(1)}, f32[18,8,128]{2,1,0:T(8,128)S(1)}, u32[]{:S(2)}, u32[]{:S(2)}) %collective-permute-start.6) | collective-permute-done | bytes 73760 | tf_op jit(solution)/shard_map/ppermute | solution.py:450
  34.6 0.1 level_4.1
  34.7 3.0 %collective-permute-start.11 = (f32[18,8,128]{2,1,0:T(8,128)S(1)}, f32[18,8,128]{2,1,0:T(8,128)S(1)}, u32[]{:S(2)}, u32[]{:S(2)}) collective-permute-start(f32[18,8,128]{2,1,0:T(8,128)S(1)} %get-tuple-element.20.refs_0_), channel_id=1, source_target_pairs={{0,96},{2,98},{4,100},{6,102},{8,104},{10,106},{12,108},{14,110},{... | collective-permute-start | bytes 221192 | tf_op jit(solution)/shard_map/ppermute | solution.py:450
  37.7 0.0 collective-permute-start.10
  37.7 1.2 %collective-permute-start.9 = (f32[18,8,128]{2,1,0:T(8,128)S(1)}, f32[18,8,128]{2,1,0:T(8,128)S(1)}, u32[]{:S(2)}, u32[]{:S(2)}) collective-permute-start(f32[18,8,128]{2,1,0:T(8,128)S(1)} %get-tuple-element.20.refs_0_), channel_id=1, source_target_pairs={{0,32},{2,34},{4,36},{6,38},{8,40},{10,42},{12,44},{14,46},{16,48}... | collective-permute-start | bytes 221192 | tf_op jit(solution)/shard_map/ppermute | solution.py:450
  38.9 1.5 %collective-permute-done.11.refs_3_ = f32[18,8,128]{2,1,0:T(8,128)S(1)} collective-permute-done((f32[18,8,128]{2,1,0:T(8,128)S(1)}, f32[18,8,128]{2,1,0:T(8,128)S(1)}, u32[]{:S(2)}, u32[]{:S(2)}) %collective-permute-start.11) | collective-permute-done | bytes 73760 | tf_op jit(solution)/shard_map/ppermute | solution.py:450
  40.4 3.2 %collective-permute-done.10.refs_2_ = f32[18,8,128]{2,1,0:T(8,128)S(1)} collective-permute-done((f32[18,8,128]{2,1,0:T(8,128)S(1)}, f32[18,8,128]{2,1,0:T(8,128)S(1)}, u32[]{:S(2)}, u32[]{:S(2)}) %collective-permute-start.10) | collective-permute-done | bytes 73760 | tf_op jit(solution)/shard_map/ppermute | solution.py:450
  43.5 0.8 %level_16.1 = (f32[18,8,128]{2,1,0:T(8,128)}, f32[18,8,128]{2,1,0:T(8,128)S(1)}) custom-call(f32[18,8,128]{2,1,0:T(8,128)S(1)} %get-tuple-element.20.refs_0_, f32[18,8,128]{2,1,0:T(8,128)S(1)} %collective-permute-done.9.refs_1_, f32[18,8,128]{2,1,0:T(8,128)S(1)} %collective-permute-done.10.refs_2_, f32[18,8,128]{2,1,0:T(8,128)S(1)} %collective-permute-done.11.refs_3_, ...), custom_call_target="tpu_custom_call" | custom-call | tf_op jit(solution)/shard_map/level_16/pallas_call | solution.py:458
  44.3 1.1 %closing.1 = f32[18,8,1024]{2,1,0:T(8,128)} custom-call(f32[8,18,8,128]{3,2,1,0:T(8,128)S(1)} %get-tuple-element.16.partial, f32[18,8,128]{2,1,0:T(8,128)S(1)} %get-tuple-element.22.tail), custom_call_target="tpu_custom_call" | custom-call | tf_op jit(solution)/shard_map/closing/pallas_call | solution.py:468
  (2 shorter events, 0.0 us)
Async XLA Ops:
  0.0 16.3 %collective-permute-start = (f32[4,8,1,8,1024]{4,3,2,1,0:T(8,128)}, f32[4,8,1,8,1024]{4,3,2,1,0:T(8,128)S(1)}, u32[]{:S(2)}, u32[]{:S(2)}) collective-permute-start(f32[4,8,1,8,1024]{4,3,2,1,0:T(8,128)} %coeffs.1), channel_id=1, source_target_pairs={{0,1},{1,0},{2,3},{3,2},{4,5},{5,4},{6,7},{7,6},{8,9},{9,8},{10,11... | collective-permute-start | bytes 3145736 | tf_op jit(solution)/shard_map/ppermute | solution.py:410
  1.2 15.1 %collective-permute-start.1 = (f32[3,8,8,128]{3,2,1,0:T(8,128)S(1)}, f32[3,8,8,128]{3,2,1,0:T(8,128)S(1)}, u32[]{:S(2)}, u32[]{:S(2)}) collective-permute-start(f32[3,8,8,128]{3,2,1,0:T(8,128)S(1)} %bitcast.5), channel_id=1, source_target_pairs={{2,0},{4,2},{6,4},{8,6},{10,8},{12,10},{14,12},{16,14},{18,16},{20... | collective-permute-start | bytes 294920 | tf_op jit(solution)/shard_map/ppermute | solution.py:411
  11.0 5.3 %collective-permute-start.2 = (f32[8,8,128]{2,1,0:T(8,128)S(1)}, f32[8,8,128]{2,1,0:T(8,128)S(1)}, u32[]{:S(2)}, u32[]{:S(2)}) collective-permute-start(f32[8,8,128]{2,1,0:T(8,128)S(1)} %bitcast.6), channel_id=1, source_target_pairs={{3,0},{2,1},{5,2},{4,3},{7,4},{6,5},{9,6},{8,7},{11,8},{10,9},{13,... | collective-permute-start | bytes 98312 | tf_op jit(solution)/shard_map/ppermute | solution.py:412
  11.7 1.2 %copy-start = (f32[4,8,1,8,1024]{4,3,2,1,0:T(8,128)S(1)}, f32[4,8,1,8,1024]{4,3,2,1,0:T(8,128)}, u32[]{:S(2)}) copy-start(f32[4,8,1,8,1024]{4,3,2,1,0:T(8,128)} %coeffs.1) | copy-start | bytes 3145732
  19.1 7.3 %collective-permute-start.5 = (f32[18,8,128]{2,1,0:T(8,128)S(1)}, f32[18,8,128]{2,1,0:T(8,128)S(1)}, u32[]{:S(2)}, u32[]{:S(2)}) collective-permute-start(f32[18,8,128]{2,1,0:T(8,128)S(1)} %get-tuple-element.17.refs_0_), channel_id=1, source_target_pairs={{0,6},{2,4},{4,2},{6,0},{8,14},{10,12},{12,10},{14,8},{16,22},{18,... | collective-permute-start | bytes 221192 | tf_op jit(solution)/shard_map/ppermute | solution.py:450
  19.2 7.2 %collective-permute-start.4 = (f32[18,8,128]{2,1,0:T(8,128)S(1)}, f32[18,8,128]{2,1,0:T(8,128)S(1)}, u32[]{:S(2)}, u32[]{:S(2)}) collective-permute-start(f32[18,8,128]{2,1,0:T(8,128)S(1)} %get-tuple-element.17.refs_0_), channel_id=1, source_target_pairs={{0,4},{2,6},{4,0},{6,2},{8,12},{10,14},{12,8},{14,10},{16,20},{18,... | collective-permute-start | bytes 221192 | tf_op jit(solution)/shard_map/ppermute | solution.py:450
  22.4 4.7 %collective-permute-start.3 = (f32[18,8,128]{2,1,0:T(8,128)S(1)}, f32[18,8,128]{2,1,0:T(8,128)S(1)}, u32[]{:S(2)}, u32[]{:S(2)}) collective-permute-start(f32[18,8,128]{2,1,0:T(8,128)S(1)} %get-tuple-element.17.refs_0_), channel_id=1, source_target_pairs={{0,2},{2,0},{4,6},{6,4},{8,10},{10,8},{12,14},{14,12},{16,18},{18,... | collective-permute-start | bytes 221192 | tf_op jit(solution)/shard_map/ppermute | solution.py:450
  27.3 6.4 %collective-permute-start.8 = (f32[18,8,128]{2,1,0:T(8,128)S(1)}, f32[18,8,128]{2,1,0:T(8,128)S(1)}, u32[]{:S(2)}, u32[]{:S(2)}) collective-permute-start(f32[18,8,128]{2,1,0:T(8,128)S(1)} %get-tuple-element.18.refs_0_), channel_id=1, source_target_pairs={{0,24},{2,26},{4,28},{6,30},{8,16},{10,18},{12,20},{14,22},{16,8},... | collective-permute-start | bytes 221192 | tf_op jit(solution)/shard_map/ppermute | solution.py:450
  27.4 6.3 %collective-permute-start.7 = (f32[18,8,128]{2,1,0:T(8,128)S(1)}, f32[18,8,128]{2,1,0:T(8,128)S(1)}, u32[]{:S(2)}, u32[]{:S(2)}) collective-permute-start(f32[18,8,128]{2,1,0:T(8,128)S(1)} %get-tuple-element.18.refs_0_), channel_id=1, source_target_pairs={{0,16},{2,18},{4,20},{6,22},{8,24},{10,26},{12,28},{14,30},{16,0},... | collective-permute-start | bytes 221192 | tf_op jit(solution)/shard_map/ppermute | solution.py:450
  27.5 7.1 %collective-permute-start.6 = (f32[18,8,128]{2,1,0:T(8,128)S(1)}, f32[18,8,128]{2,1,0:T(8,128)S(1)}, u32[]{:S(2)}, u32[]{:S(2)}) collective-permute-start(f32[18,8,128]{2,1,0:T(8,128)S(1)} %get-tuple-element.18.refs_0_), channel_id=1, source_target_pairs={{0,8},{2,10},{4,12},{6,14},{8,0},{10,2},{12,4},{14,6},{16,24},{18,... | collective-permute-start | bytes 221192 | tf_op jit(solution)/shard_map/ppermute | solution.py:450
  34.7 5.6 %collective-permute-start.11 = (f32[18,8,128]{2,1,0:T(8,128)S(1)}, f32[18,8,128]{2,1,0:T(8,128)S(1)}, u32[]{:S(2)}, u32[]{:S(2)}) collective-permute-start(f32[18,8,128]{2,1,0:T(8,128)S(1)} %get-tuple-element.20.refs_0_), channel_id=1, source_target_pairs={{0,96},{2,98},{4,100},{6,102},{8,104},{10,106},{12,108},{14,110},{... | collective-permute-start | bytes 221192 | tf_op jit(solution)/shard_map/ppermute | solution.py:450
  37.7 5.9 %collective-permute-start.10 = (f32[18,8,128]{2,1,0:T(8,128)S(1)}, f32[18,8,128]{2,1,0:T(8,128)S(1)}, u32[]{:S(2)}, u32[]{:S(2)}) collective-permute-start(f32[18,8,128]{2,1,0:T(8,128)S(1)} %get-tuple-element.20.refs_0_), channel_id=1, source_target_pairs={{0,64},{2,66},{4,68},{6,70},{8,72},{10,74},{12,76},{14,78},{16,80}... | collective-permute-start | bytes 221192 | tf_op jit(solution)/shard_map/ppermute | solution.py:450
  37.7 5.9 %collective-permute-start.9 = (f32[18,8,128]{2,1,0:T(8,128)S(1)}, f32[18,8,128]{2,1,0:T(8,128)S(1)}, u32[]{:S(2)}, u32[]{:S(2)}) collective-permute-start(f32[18,8,128]{2,1,0:T(8,128)S(1)} %get-tuple-element.20.refs_0_), channel_id=1, source_target_pairs={{0,32},{2,34},{4,36},{6,38},{8,40},{10,42},{12,44},{14,46},{16,48}... | collective-permute-start | bytes 221192 | tf_op jit(solution)/shard_map/ppermute | solution.py:450
where the time goes:
time: 45.6 us; the launch traced here: 45.4 us
  starting transfers between devices  22.1 us (48%)
  waiting for transfers between devices  11.6 us (25%)
  Pallas kernels  8.27 us (18%)
  local copies, waits for them, and re-layouts  3.38 us (7%)
    ppermute x9, starting transfers between devices, shards(): lax.ppermute(total, 'tm', [(i, i ^ low * k) for i in range(count)])  12.5 us
    ppermute x9, waiting for transfers between devices, shards(): lax.ppermute(total, 'tm', [(i, i ^ low * k) for i in range(count)])  11.6 us
    ppermute x1, starting transfers between devices, shards(): lax.ppermute(next_rows, 'tm', [((i + 1) % count, i) for i in range(count)])  8.83 us
    pallas_call x1, Pallas kernels, shards(): pl.pallas_call(local_kernel, out_shape=(field(4, NT_LOCAL), field(NT_LOCA...  3.33 us
    pallas_call x1, Pallas kernels, shards(): pl.pallas_call(join_kernel, out_shape=(field(NT_LOCAL), field()), in_spec...  2.78 us
    unnamed x2, local copies, waits for them, and re-layouts  1.22 us
    slice x1, local copies, waits for them, and re-layouts, shards(): next_rows = coeffs[0:3, :, 0, 0, :].reshape(3, 8, ROWS, LANES)  1.18 us
    pallas_call x1, Pallas kernels, shards(): pl.pallas_call(closing_kernel, out_shape=jax.ShapeDtypeStruct((18, NT_LOC...  1.14 us
  transfers between devices with their start and end apart: 12, of which 6 were waited for; matrix products, arithmetic and copies ran while one was open for 5% of the time, Pallas kernels for 7%

commit v1 on v0

v1 whole, which is shorter than its diff:
```python
import jax
import jax.numpy as jnp
from jax import lax
from jax.experimental import pallas as pl
from jax.experimental.pallas import tpu as pltpu
from jax.sharding import PartitionSpec as P

ZDIM = 32
LANES = 128
ROWS = 8
NT_LOCAL = 8
SMEAR = 0.1
SPLIT = 2
PEERS = (1, 3, 2)
LAST_PEERS = (1, 3, 2)
ROOT_THIRD = 1.0 / 3.0**0.5
VMEM_LIMIT = 48 * 1024 * 1024
WHOLE = pl.BlockSpec(memory_space=pltpu.VMEM)


def read(ref, *index):
    re = [[ref[(*index, 3 * i + j)] for j in range(3)] for i in range(3)]
    im = [[ref[(*index, 9 + 3 * i + j)] for j in range(3)] for i in range(3)]
    return re, im


def write(ref, matrix, *index):
    for part in range(2):
        for i in range(3):
            for j in range(3):
                ref[(*index, 9 * part + 3 * i + j)] = matrix[part][i][j]


def row_times(row, matrix, conj_left=False, conj_right=False):
    a, b = row
    c, d = matrix
    out_re, out_im = [], []
    for j in range(3):
        rr = a[0] * c[0][j]
        ii = b[0] * d[0][j]
        ri = a[0] * d[0][j]
        ir = b[0] * c[0][j]
        for m in (1, 2):
            rr = rr + a[m] * c[m][j]
            ii = ii + b[m] * d[m][j]
            ri = ri + a[m] * d[m][j]
            ir = ir + b[m] * c[m][j]
        out_re.append(rr + ii if conj_left != conj_right else rr - ii)
        if conj_left and conj_right:
            out_im.append(-(ri + ir))
        elif conj_left:
            out_im.append(ri - ir)
        elif conj_right:
            out_im.append(ir - ri)
        else:
            out_im.append(ri + ir)
    return out_re, out_im


def mul(left, right):
    re, im = [], []
    for i in range(3):
        r, m = row_times((left[0][i], left[1][i]), right)
        re.append(r)
        im.append(m)
    return re, im


def transposed(matrix):
    return tuple([[part[j][i] for j in range(3)] for i in range(3)] for part in matrix)


def forward_term(link, temporal, ahead):
    turned = transposed(ahead)
    re, im = [], []
    for i in range(3):
        row = row_times((link[0][i], link[1][i]), temporal)
        r, m = row_times(row, turned, conj_right=True)
        re.append(r)
        im.append(m)
    return re, im


def backward_term(link, temporal, ahead):
    turned = transposed(link)
    re, im = [], []
    for i in range(3):
        row = row_times((turned[0][i], turned[1][i]), temporal, conj_left=True)
        r, m = row_times(row, ahead)
        re.append(r)
        im.append(m)
    return re, im


def plus(left, right):
    return tuple(
        [[left[p][i][j] + right[p][i][j] for j in range(3)] for i in range(3)] for p in range(2)
    )


def mapped(f, matrix):
    return tuple([[f(part[i][j]) for j in range(3)] for i in range(3)] for part in matrix)


def lane():
    return lax.broadcasted_iota(jnp.int32, (ROWS, LANES), 1)


def from_y_above(x):
    r = pltpu.roll(x, LANES - ZDIM, 1)
    return jnp.where(lane() >= LANES - ZDIM, pltpu.roll(r, ROWS - 1, 0), r)


def from_y_below(x):
    r = pltpu.roll(x, ZDIM, 1)
    return jnp.where(lane() < ZDIM, pltpu.roll(r, 1, 0), r)


def from_z_above(x):
    edge = lane() % ZDIM == ZDIM - 1
    return jnp.where(edge, pltpu.roll(x, ZDIM - 1, 1), pltpu.roll(x, LANES - 1, 1))


def from_z_below(x):
    edge = lane() % ZDIM == 0
    return jnp.where(edge, pltpu.roll(x, LANES - ZDIM + 1, 1), pltpu.roll(x, 1, 1))


def squared(d, g01, g02, g12):
    n01 = g01[0] * g01[0] + g01[1] * g01[1]
    n02 = g02[0] * g02[0] + g02[1] * g02[1]
    n12 = g12[0] * g12[0] + g12[1] * g12[1]
    s = (d[0] * d[0] + (n01 + n02), d[1] * d[1] + (n01 + n12), d[2] * d[2] + (n02 + n12))
    k = (g01[0] * g12[0] - g01[1] * g12[1], g01[0] * g12[1] + g01[1] * g12[0])
    s02 = (k[0] - d[1] * g02[0], k[1] - d[1] * g02[1])
    s01 = (
        (g02[0] * g12[0] + g02[1] * g12[1]) - d[2] * g01[0],
        (g02[1] * g12[0] - g02[0] * g12[1]) - d[2] * g01[1],
    )
    s12 = (
        (g01[0] * g02[0] + g01[1] * g02[1]) - d[0] * g12[0],
        (g01[0] * g02[1] - g01[1] * g02[0]) - d[0] * g12[1],
    )
    det = (
        d[0] * (d[1] * d[2] - n12)
        - d[1] * n02
        - d[2] * n01
        + 2.0 * (k[0] * g02[0] + k[1] * g02[1])
    )
    return s, s01, s02, s12, det


def link_of(c):
    d2 = c[7] * (-2.0 * ROOT_THIRD)
    e = c[7] * ROOT_THIRD
    d = (e + c[2], e - c[2], d2)
    g01, g02, g12 = (c[0], -c[1]), (c[3], -c[4]), (c[5], -c[6])
    s, s01, s02, s12, det = squared(d, g01, g02, g12)
    p = (s[0] + s[1] + s[2]) * 0.125
    q = det * 0.125
    qq = q * q
    w = (p * (-1.0 / 5040.0) + 1.0 / 120.0) * p - 1.0 / 6.0
    f0r = qq * (p * (1.0 / 20160.0) - 1.0 / 720.0) + 1.0
    f0i = q * w
    f1r = q * ((p * (0.5 / 13440.0) - 0.5 / 360.0) * p + 0.5 / 24.0)
    f1i = (p * w + qq * (-1.0 / 5040.0)) * 0.5 + 0.5
    f2r = ((p * (0.25 / 40320.0) - 0.25 / 720.0) * p + 0.25 / 24.0) * p + (qq * (0.25 / 40320.0) - 0.125)
    f2i = q * (p * (-0.5 / 5040.0) + 0.25 / 120.0)
    re = [[None] * 3 for _ in range(3)]
    im = [[None] * 3 for _ in range(3)]
    for j in range(3):
        re[j][j] = f0r + (f1r * d[j] + f2r * s[j])
        im[j][j] = f0i + (f1i * d[j] + f2i * s[j])
    for j, k, g, h in ((0, 1, g01, s01), (0, 2, g02, s02), (1, 2, g12, s12)):
        rr = f1r * g[0] + f2r * h[0]
        ii = f1i * g[1] + f2i * h[1]
        ir = f1i * g[0] + f2i * h[0]
        ri = f1r * g[1] + f2r * h[1]
        re[j][k], re[k][j] = rr - ii, rr + ii
        im[j][k], im[k][j] = ir + ri, ir - ri
    return re, im


def smearing(staple, temporal):
    cr, ci = staple
    ur, ui = temporal

    def omega_re(j, k):
        t = cr[j][0] * ur[k][0] + ci[j][0] * ui[k][0]
        for m in (1, 2):
            t = t + (cr[j][m] * ur[k][m] + ci[j][m] * ui[k][m])
        return t

    def omega_im(j, k):
        t = ci[j][0] * ur[k][0] - cr[j][0] * ui[k][0]
        for m in (1, 2):
            t = t + (ci[j][m] * ur[k][m] - cr[j][m] * ui[k][m])
        return t

    half = 0.5 * SMEAR
    diag = [omega_im(j, j) for j in range(3)]
    third = (diag[0] + diag[1] + diag[2]) * (1.0 / 3.0)
    d = [(x - third) * SMEAR for x in diag]
    g = {}
    for j, k in ((0, 1), (0, 2), (1, 2)):
        g[j, k] = (
            (omega_im(j, k) + omega_im(k, j)) * half,
            (omega_re(k, j) - omega_re(j, k)) * half,
        )
    s, s01, s02, s12, q = squared(d, g[0, 1], g[0, 2], g[1, 2])
    p = (s[0] + s[1] + s[2]) * 0.5
    f1 = p * (-1.0 / 6.0) + 1.0
    f0i = q * (-1.0 / 6.0)
    re = [[None] * 3 for _ in range(3)]
    im = [[None] * 3 for _ in range(3)]
    for j in range(3):
        re[j][j] = 1.0 - 0.5 * s[j]
        im[j][j] = f0i + f1 * d[j]
    for j, k, h in ((0, 1, s01), (0, 2, s02), (1, 2, s12)):
        a = f1 * g[j, k][0]
        b = f1 * g[j, k][1]
        c = 0.5 * h[0]
        e = 0.5 * h[1]
        re[j][k], re[k][j] = -b - c, b - c
        im[j][k], im[k][j] = a - e, a + e
    return re, im


def slice_of(rows, n, t):
    return [rows[n, a, pl.ds(t, ROWS, stride=NT_LOCAL), :] for a in range(8)]


def unit():
    one = jnp.ones((ROWS, LANES), jnp.float32)
    zero = jnp.zeros((ROWS, LANES), jnp.float32)
    return (
        [[one if i == j else zero for j in range(3)] for i in range(3)],
        [[zero] * 3 for _ in range(3)],
    )


def plane_terms(spatial, temporal, ahead, above, below):
    forward = forward_term(spatial, mapped(above, temporal), ahead)
    return plus(forward, mapped(below, backward_term(spatial, temporal, ahead)))


def by_row(coeffs, rows, sems, directions):
    return [
        pltpu.make_async_copy(
            coeffs.at[direction, :, 0, :, pl.ds(v * LANES, LANES)],
            rows.at[n, :, pl.ds(v * NT_LOCAL, NT_LOCAL), :],
            sems.at[n, v],
        )
        for n, direction in enumerate(directions)
        for v in range(ROWS)
    ]


def prepare_kernel(coeffs, rows, first, sems):
    copies = by_row(coeffs, rows, sems, (0, 1, 2, 3))
    for copy in copies:
        copy.start()
    for direction in range(4):
        for copy in copies[direction * ROWS : (direction + 1) * ROWS]:
            copy.wait()
        if direction < 3:
            for a, value in enumerate(slice_of(rows, direction, 0)):
                first[direction, a] = value


def local_kernel(rows, other, links, staple, other_rows, sems):
    last = NT_LOCAL - 1
    copies = by_row(other, other_rows, sems, (0, 3))
    for copy in copies:
        copy.start()

    def make(t):
        for direction in range(4):
            write(links, link_of(slice_of(rows, direction, t)), direction, t)

    make(last)

    def step(i, carry):
        t = last - 1 - i
        make(t)
        terms = plane_terms(
            read(links, 1, t), read(links, 3, t), read(links, 1, t + 1), from_y_above, from_y_below
        )
        write(staple, terms, t)
        terms = plane_terms(
            read(links, 2, t), read(links, 3, t), read(links, 2, t + 1), from_z_above, from_z_below
        )
        write(staple, plus(read(staple, t), terms), t)
        return carry

    lax.fori_loop(0, last, step, 0)
    for copy in copies:
        copy.wait()


def chain_steps(high, low, links, staple, rows, other_links, terms, later, put):
    def step(i, carry):
        t = high - 1 - i
        write(other_links, link_of(slice_of(rows, 1, t)), 1)
        write(other_links, link_of(slice_of(rows, 0, t)), 2)
        write(
            terms,
            plus(
                read(staple, t),
                forward_term(read(links, 0, t), read(other_links, 1), read(links, 0, t + 1)),
            ),
        )
        write(
            terms,
            plus(
                read(terms),
                backward_term(read(other_links, 2), read(other_links, 1), read(other_links, 0)),
            ),
        )
        temporal = read(links, 3, t)
        smeared = mul(smearing(read(terms), temporal), temporal)
        running = mul(smeared, read(later))
        write(later, running)
        put(t, running)
        write(other_links, read(other_links, 2), 0)
        return carry

    lax.fori_loop(0, high - low, step, 0)


def late_chain_kernel(links, staple, rows, partial, other_last, other_links, terms, later):
    last = NT_LOCAL - 1
    for n in range(2):
        write(other_last, link_of(slice_of(rows, n, last)), n)
    write(other_links, read(other_last, 0), 0)
    write(later, unit())

    def put(t, product):
        write(partial, product, t - SPLIT)

    chain_steps(last, SPLIT, links, staple, rows, other_links, terms, later, put)


def early_chain_kernel(links, staple, rows, late, after, partial, other_links, terms, later):
    del after
    write(other_links, link_of(slice_of(rows, 0, SPLIT)), 0)
    write(later, read(late, 0))

    def put(t, product):
        write(partial, product, t)

    chain_steps(SPLIT, 0, links, staple, rows, other_links, terms, later, put)


def pick_kernel(ahead, after, out):
    del after
    out[...] = ahead[0]


def last_slice_kernel(links, other_last, next_rows, other_next, partial, smeared_last, total, ahead, terms):
    last = NT_LOCAL - 1
    for direction in range(3):
        write(ahead, link_of([next_rows[direction, a] for a in range(8)]), direction)
    write(ahead, link_of([other_next[a] for a in range(8)]), 3)
    temporal = read(links, 3, last)
    write(
        terms,
        plane_terms(read(links, 1, last), temporal, read(ahead, 1), from_y_above, from_y_below),
    )
    for term in (
        lambda: plane_terms(read(links, 2, last), temporal, read(ahead, 2), from_z_above, from_z_below),
        lambda: forward_term(read(links, 0, last), read(other_last, 1), read(ahead, 0)),
        lambda: backward_term(read(other_last, 0), read(other_last, 1), read(ahead, 3)),
    ):
        write(terms, plus(read(terms), term()))
    smeared = mul(smearing(read(terms), temporal), temporal)
    write(smeared_last, smeared)
    write(total, mul(read(partial, 0), read(smeared_last)))


def suffixes(low, peers, own, by1, by2, by3, held):
    digit = lax.rem(lax.axis_index("tm") // low, 4)
    for k, ref in zip((0, *peers), (own, by1, by2, by3)):
        for a in range(18):
            held[k, a] = ref[a]
    third = read(held, 3 ^ digit)
    second = mul(read(held, 2 ^ digit), third)
    first = mul(read(held, 1 ^ digit), second)
    zeroth = read(held, digit)
    for k, matrix in enumerate((first, second, third, unit())):
        write(held, matrix, 4 + k)
    return zeroth, 4 + digit


def level_kernel(low, own, by1, by2, by3, tail, new_total, new_tail, held):
    zeroth, at = suffixes(low, PEERS, own, by1, by2, by3, held)
    write(new_total, mul(zeroth, read(held, 4)))
    write(new_tail, mul(read(tail), read(held, at)))


def closing_kernel(low, own, by1, by2, by3, tail, early, late, out, held, rows, sems):
    _, at = suffixes(low, LAST_PEERS, own, by1, by2, by3, held)
    write(held, mul(read(tail), read(held, at)), 0)
    last = NT_LOCAL - 1
    copies = []
    for i in range(3):

        def put(t, row, i=i):
            for part in range(2):
                for j in range(3):
                    rows[9 * part + 3 * i + j, pl.ds(t, ROWS, stride=NT_LOCAL), :] = row[part][j]

        for partial, low, high in ((early, 0, SPLIT), (late, SPLIT, last)):

            def step(t, carry, partial=partial, low=low, i=i, put=put):
                left = [[partial[t - low, 9 * part + 3 * i + j] for j in range(3)] for part in range(2)]
                put(t, row_times(left, read(held, 0)))
                return carry

            lax.fori_loop(low, high, step, 0)
        put(last, [[held[0, 9 * part + 3 * i + j] for j in range(3)] for part in range(2)])
        for part in range(2):
            for v in range(ROWS):
                copies.append(
                    pltpu.make_async_copy(
                        rows.at[pl.ds(9 * part + 3 * i, 3), pl.ds(v * NT_LOCAL, NT_LOCAL), :],
                        out.at[pl.ds(9 * part + 3 * i, 3), :, pl.ds(v * LANES, LANES)],
                        sems.at[i, part, v],
                    )
                )
                copies[-1].start()
    for copy in copies:
        copy.wait()


def params():
    return pltpu.CompilerParams(vmem_limit_bytes=VMEM_LIMIT)


def field(*lead):
    return jax.ShapeDtypeStruct((*lead, 18, ROWS, LANES), jnp.float32)


def cost(flops):
    return pl.CostEstimate(flops=flops, bytes_accessed=1_000_000, transcendentals=0)


def block(*shape):
    return jax.ShapeDtypeStruct(shape, jnp.float32)


def shards(coeffs):
    count = lax.axis_size("tm")
    other = lax.ppermute(coeffs, "space", [(0, 1), (1, 0)])
    rows, first = pl.pallas_call(
        prepare_kernel,
        out_shape=(block(4, 8, ROWS * NT_LOCAL, LANES), block(3, 8, ROWS, LANES)),
        in_specs=[pl.BlockSpec(memory_space=pltpu.HBM)],
        out_specs=(WHOLE, WHOLE),
        scratch_shapes=[pltpu.SemaphoreType.DMA((4, ROWS))],
        compiler_params=params(),
        name="prepare",
    )(pltpu.with_memory_space_constraint(coeffs, pltpu.HBM))
    ahead = lax.ppermute(first, "tm", [((i + 1) % count, i) for i in range(count)])
    links, staple, other_rows = pl.pallas_call(
        local_kernel,
        out_shape=(field(4, NT_LOCAL), field(NT_LOCAL), block(2, 8, ROWS * NT_LOCAL, LANES)),
        in_specs=[WHOLE, WHOLE],
        out_specs=(WHOLE, WHOLE, WHOLE),
        scratch_shapes=[pltpu.SemaphoreType.DMA((2, ROWS))],
        compiler_params=params(),
        cost_estimate=cost(20_000_000),
        name="local_terms",
    )(rows, other)
    chain_scratch = [
        pltpu.VMEM((3, 18, ROWS, LANES), jnp.float32),
        pltpu.VMEM((18, ROWS, LANES), jnp.float32),
        pltpu.VMEM((18, ROWS, LANES), jnp.float32),
    ]
    late, other_last = pl.pallas_call(
        late_chain_kernel,
        out_shape=(field(NT_LOCAL - 1 - SPLIT), field(2)),
        in_specs=[WHOLE] * 3,
        out_specs=(WHOLE, WHOLE),
        scratch_shapes=chain_scratch,
        compiler_params=params(),
        cost_estimate=cost(8_000_000),
        name="late_chain",
    )(links, staple, other_rows)
    ahead_x = pl.pallas_call(
        pick_kernel,
        out_shape=block(8, ROWS, LANES),
        in_specs=[WHOLE, WHOLE],
        out_specs=WHOLE,
        compiler_params=params(),
        name="pick",
    )(ahead, late)
    other_ahead = lax.ppermute(ahead_x, "space", [(0, 1), (1, 0)])
    early = pl.pallas_call(
        early_chain_kernel,
        out_shape=field(SPLIT),
        in_specs=[WHOLE] * 5,
        out_specs=WHOLE,
        scratch_shapes=chain_scratch,
        compiler_params=params(),
        cost_estimate=cost(8_000_000),
        name="early_chain",
    )(links, staple, other_rows, late, ahead_x)
    tail, total = pl.pallas_call(
        last_slice_kernel,
        out_shape=(field(), field()),
        in_specs=[WHOLE] * 5,
        out_specs=(WHOLE, WHOLE),
        scratch_shapes=[
            pltpu.VMEM((4, 18, ROWS, LANES), jnp.float32),
            pltpu.VMEM((18, ROWS, LANES), jnp.float32),
        ],
        compiler_params=params(),
        cost_estimate=cost(5_000_000),
        name="last_slice",
    )(links, other_last, ahead, other_ahead, early)
    low = 1
    while True:
        peers = LAST_PEERS if low * 4 >= count else PEERS
        received = [
            lax.ppermute(total, "tm", [(i, i ^ (low * k)) for i in range(count)]) for k in peers
        ]
        held = pltpu.VMEM((8, 18, ROWS, LANES), jnp.float32)
        if low * 4 >= count:
            break

        def level(*refs, low=low):
            level_kernel(low, *refs)

        total, tail = pl.pallas_call(
            level,
            out_shape=(field(), field()),
            in_specs=[WHOLE] * 5,
            out_specs=(WHOLE, WHOLE),
            scratch_shapes=[held],
            compiler_params=params(),
            name=f"level_{low}",
        )(total, *received, tail)
        low *= 4

    def closing(*refs, low=low):
        closing_kernel(low, *refs)

    out = pl.pallas_call(
        closing,
        out_shape=jax.ShapeDtypeStruct((18, NT_LOCAL, ROWS * LANES), jnp.float32),
        in_specs=[WHOLE] * 7,
        out_specs=pl.BlockSpec(memory_space=pltpu.HBM),
        scratch_shapes=[
            held,
            pltpu.VMEM((18, ROWS * NT_LOCAL, LANES), jnp.float32),
            pltpu.SemaphoreType.DMA((3, 2, ROWS)),
        ],
        compiler_params=params(),
        name="closing",
    )(total, *received, tail, early, late)
    return out.reshape(2, 3, 3, 1, NT_LOCAL, ROWS * LANES)


def solution(mesh):
    in_specs = (P(None, None, "space", "tm", None),)
    out_specs = P(None, None, None, "space", "tm", None)
    return jax.shard_map(shards, mesh=mesh, in_specs=in_specs, out_specs=out_specs, check_vma=False)
```

time: 45.6 us -> 40.1 us (0.88)
  local copies, waits for them, and re-layouts: 3.38 us -> 0 us
  starting transfers between devices: 22.1 us -> 19.8 us
  Pallas kernels: 8.27 us -> 8.96 us
  waiting for transfers between devices: 11.6 us -> 11 us
    slice x2 -> x0, local copies, waits for them, and re-layouts: 2.15 us -> none  [the longest x1 1.18 us: shards(): next_rows = coeffs[0:3, :, 0, 0, :].reshape(3, 8, ROWS, LANES)]
    ppermute x9, starting transfers between devices: 12.5 us -> 10.7 us  [shards(): lax.ppermute(total, 'tm', [(i, i ^ low * k) for i in range(count)])]
    unnamed x2 -> x0, local copies, waits for them, and re-layouts: 1.22 us -> none
    ppermute x9, waiting for transfers between devices: 11.6 us -> 10.6 us  [shards(): lax.ppermute(total, 'tm', [(i, i ^ low * k) for i in range(count)])]
    pallas_call x5 -> x8, Pallas kernels: 4.95 us -> 5.9 us  [the longest x1 1.57 us: shards(): pl.pallas_call(closing, out_shape=jax.ShapeDtypeStruct((18, NT_LOCAL, ROW...]
  transfers between devices with their start and end apart: 12 -> 12, of which waited for: 6 -> 7; matrix products, arithmetic and copies ran while one was open for 5% -> 0% of each run, Pallas kernels for 7% -> 16%
where the time goes in v1:
time: 40.1 us; the launch traced here: 39.8 us
  starting transfers between devices  19.8 us (49%)
  waiting for transfers between devices  11 us (27%)
  Pallas kernels  8.96 us (22%)
    ppermute x9, starting transfers between devices, shards(): lax.ppermute(total, 'tm', [(i, i ^ low * k) for i in range(count)])  10.7 us
    ppermute x9, waiting for transfers between devices, shards(): lax.ppermute(total, 'tm', [(i, i ^ low * k) for i in range(count)])  10.6 us
    ppermute x1, starting transfers between devices, shards(): lax.ppermute(first, 'tm', [((i + 1) % count, i) for i in range(count)])  8.84 us
    pallas_call x1, Pallas kernels, shards(): pl.pallas_call(local_kernel, out_shape=(field(4, NT_LOCAL), field(NT_LOCA...  3.06 us
    pallas_call x1, Pallas kernels, shards(): pl.pallas_call(closing, out_shape=jax.ShapeDtypeStruct((18, NT_LOCAL, ROW...  1.57 us
    pallas_call x1, Pallas kernels, shards(): pl.pallas_call(prepare_kernel, out_shape=(block(4, 8, ROWS * NT_LOCAL, LA...  1.45 us
    pallas_call x1, Pallas kernels, shards(): pl.pallas_call(late_chain_kernel, out_shape=(field(NT_LOCAL - 1 - SPLIT),...  1.44 us
  transfers between devices with their start and end apart: 12, of which 7 were waited for; matrix products, arithmetic and copies ran while one was open for 0% of the time, Pallas kernels for 16%

profile of v1, /device:TPU:0, one launch (start us, length us, event | category | flops | bytes accessed | tf_op | source)
XLA Modules:
  0.0 39.8 jit_solution(9752487513100078465)
XLA Ops:
  0.0 0.0 collective-permute-start
  0.0 1.5 %prepare.1 = (f32[4,8,64,128]{3,2,1,0:T(8,128)S(1)}, f32[3,8,8,128]{3,2,1,0:T(8,128)S(1)}) custom-call(f32[4,8,1,8,1024]{4,3,2,1,0:T(8,128)} %coeffs.1), custom_call_target="tpu_custom_call" | custom-call | tf_op jit(solution)/shard_map/prepare/pallas_call | solution.py:455
  1.5 8.8 %collective-permute-start.1 = (f32[3,8,8,128]{3,2,1,0:T(8,128)S(1)}, f32[3,8,8,128]{3,2,1,0:T(8,128)S(1)}, u32[]{:S(2)}, u32[]{:S(2)}) collective-permute-start(f32[3,8,8,128]{3,2,1,0:T(8,128)S(1)} %get-tuple-element.23), channel_id=1, source_target_pairs={{2,0},{4,2},{6,4},{8,6},{10,8},{12,10},{14,12},{16,14},{18,16},{20... | collective-permute-start | bytes 294920 | tf_op jit(solution)/shard_map/ppermute | solution.py:464
  10.3 0.0 collective-permute-done.other
  10.3 3.1 %local_terms.1 = (f32[4,8,18,8,128]{4,3,2,1,0:T(8,128)S(1)}, f32[8,18,8,128]{3,2,1,0:T(8,128)S(1)}, f32[2,8,64,128]{3,2,1,0:T(8,128)S(1)}) custom-call(f32[4,8,64,128]{3,2,1,0:T(8,128)S(1)} %get-tuple-element.18.rows, f32[4,8,1,8,1024]{4,3,2,1,0:T(8,128)S(1)} %collective-permute-done.other), custom_call_target="tpu_custom_call" | custom-call | flops 20000000 | bytes 1000000 | tf_op jit(solution)/shard_map/local_terms/pallas_call | solution.py:465
  13.4 1.4 %late_chain.1 = (f32[5,18,8,128]{3,2,1,0:T(8,128)S(1)}, f32[2,18,8,128]{3,2,1,0:T(8,128)S(1)}) custom-call(f32[4,8,18,8,128]{4,3,2,1,0:T(8,128)S(1)} %get-tuple-element.19.links, f32[8,18,8,128]{3,2,1,0:T(8,128)S(1)} %get-tuple-element.20.staple, f32[2,8,64,128]{3,2,1,0:T(8,128)S(1)} %get-tuple-element.21.rows), custom_call_target="tpu_custom_call" | custom-call | flops 8000000 | bytes 1000000 | tf_op jit(solution)/shard_map/late_chain/pallas_call | solution.py:480
  14.8 0.0 collective-permute-done.1.ahead.next_rows
  14.8 0.3 collective-permute-start.2
  15.1 0.6 %early_chain.1.partial.refs_5_ = f32[2,18,8,128]{3,2,1,0:T(8,128)S(1)} custom-call(f32[4,8,18,8,128]{4,3,2,1,0:T(8,128)S(1)} %get-tuple-element.19.links, f32[8,18,8,128]{3,2,1,0:T(8,128)S(1)} %get-tuple-element.20.staple, f32[2,8,64,128]{3,2,1,0:T(8,128)S(1)} %get-tuple-element.21.rows, f32[5,18,8,128]{3,2,1,0:T(8,128)S(1)} %get-tuple-element.24.after.late.refs_6_, ...), custom_call_target="tpu_custom_call" | custom-call | flops 8000000 | bytes 1000000 | tf_op jit(solution)/shard_map/early_chain/pallas_call | solution.py:499
  15.7 0.4 collective-permute-done.2.other_next
  16.1 0.6 %last_slice.1 = (f32[18,8,128]{2,1,0:T(8,128)S(1)}, f32[18,8,128]{2,1,0:T(8,128)S(1)}) custom-call(f32[4,8,18,8,128]{4,3,2,1,0:T(8,128)S(1)} %get-tuple-element.19.links, f32[2,18,8,128]{3,2,1,0:T(8,128)S(1)} %get-tuple-element.22.other_last, f32[3,8,8,128]{3,2,1,0:T(8,128)S(1)} %collective-permute-done.1.ahead.next_rows, ...), custom_call_target="tpu_custom_call" | custom-call | flops 5000000 | bytes 1000000 | tf_op jit(solution)/shard_map/last_slice/pallas_call | solution.py:509
  16.7 0.1 collective-permute-start.5
  16.8 0.1 collective-permute-start.4
  16.9 3.4 %collective-permute-start.3 = (f32[18,8,128]{2,1,0:T(8,128)S(1)}, f32[18,8,128]{2,1,0:T(8,128)S(1)}, u32[]{:S(2)}, u32[]{:S(2)}) collective-permute-start(f32[18,8,128]{2,1,0:T(8,128)S(1)} %get-tuple-element.25.refs_0_), channel_id=1, source_target_pairs={{0,2},{2,0},{4,6},{6,4},{8,10},{10,8},{12,14},{14,12},{16,18},{18,... | collective-permute-start | bytes 221192 | tf_op jit(solution)/shard_map/ppermute | solution.py:526
  20.3 3.1 %collective-permute-done.5.refs_3_ = f32[18,8,128]{2,1,0:T(8,128)S(1)} collective-permute-done((f32[18,8,128]{2,1,0:T(8,128)S(1)}, f32[18,8,128]{2,1,0:T(8,128)S(1)}, u32[]{:S(2)}, u32[]{:S(2)}) %collective-permute-start.5) | collective-permute-done | bytes 73760 | tf_op jit(solution)/shard_map/ppermute | solution.py:526
  23.3 0.7 %collective-permute-done.4.refs_2_ = f32[18,8,128]{2,1,0:T(8,128)S(1)} collective-permute-done((f32[18,8,128]{2,1,0:T(8,128)S(1)}, f32[18,8,128]{2,1,0:T(8,128)S(1)}, u32[]{:S(2)}, u32[]{:S(2)}) %collective-permute-start.4) | collective-permute-done | bytes 73760 | tf_op jit(solution)/shard_map/ppermute | solution.py:526
  24.1 0.0 collective-permute-done.3.refs_1_
  24.1 0.1 level_1.1
  24.2 0.1 collective-permute-start.8
  24.3 0.1 collective-permute-start.7
  24.4 3.4 %collective-permute-start.6 = (f32[18,8,128]{2,1,0:T(8,128)S(1)}, f32[18,8,128]{2,1,0:T(8,128)S(1)}, u32[]{:S(2)}, u32[]{:S(2)}) collective-permute-start(f32[18,8,128]{2,1,0:T(8,128)S(1)} %get-tuple-element.27.refs_0_), channel_id=1, source_target_pairs={{0,8},{2,10},{4,12},{6,14},{8,0},{10,2},{12,4},{14,6},{16,24},{18,... | collective-permute-start | bytes 221192 | tf_op jit(solution)/shard_map/ppermute | solution.py:526
  27.8 3.0 %collective-permute-done.8.refs_3_ = f32[18,8,128]{2,1,0:T(8,128)S(1)} collective-permute-done((f32[18,8,128]{2,1,0:T(8,128)S(1)}, f32[18,8,128]{2,1,0:T(8,128)S(1)}, u32[]{:S(2)}, u32[]{:S(2)}) %collective-permute-start.8) | collective-permute-done | bytes 73760 | tf_op jit(solution)/shard_map/ppermute | solution.py:526
  30.8 0.4 collective-permute-done.7.refs_2_
  31.2 0.0 collective-permute-done.6.refs_1_
  31.2 0.1 level_4.1
  31.3 0.9 %collective-permute-start.11 = (f32[18,8,128]{2,1,0:T(8,128)S(1)}, f32[18,8,128]{2,1,0:T(8,128)S(1)}, u32[]{:S(2)}, u32[]{:S(2)}) collective-permute-start(f32[18,8,128]{2,1,0:T(8,128)S(1)} %get-tuple-element.29.refs_0_), channel_id=1, source_target_pairs={{0,64},{2,66},{4,68},{6,70},{8,72},{10,74},{12,76},{14,78},{16,80}... | collective-permute-start | bytes 221192 | tf_op jit(solution)/shard_map/ppermute | solution.py:526
  32.2 1.5 %collective-permute-start.10 = (f32[18,8,128]{2,1,0:T(8,128)S(1)}, f32[18,8,128]{2,1,0:T(8,128)S(1)}, u32[]{:S(2)}, u32[]{:S(2)}) collective-permute-start(f32[18,8,128]{2,1,0:T(8,128)S(1)} %get-tuple-element.29.refs_0_), channel_id=1, source_target_pairs={{0,96},{2,98},{4,100},{6,102},{8,104},{10,106},{12,108},{14,110},{... | collective-permute-start | bytes 221192 | tf_op jit(solution)/shard_map/ppermute | solution.py:526
  33.7 1.2 %collective-permute-start.9 = (f32[18,8,128]{2,1,0:T(8,128)S(1)}, f32[18,8,128]{2,1,0:T(8,128)S(1)}, u32[]{:S(2)}, u32[]{:S(2)}) collective-permute-start(f32[18,8,128]{2,1,0:T(8,128)S(1)} %get-tuple-element.29.refs_0_), channel_id=1, source_target_pairs={{0,32},{2,34},{4,36},{6,38},{8,40},{10,42},{12,44},{14,46},{16,48}... | collective-permute-start | bytes 221192 | tf_op jit(solution)/shard_map/ppermute | solution.py:526
  34.9 2.8 %collective-permute-done.11.refs_3_ = f32[18,8,128]{2,1,0:T(8,128)S(1)} collective-permute-done((f32[18,8,128]{2,1,0:T(8,128)S(1)}, f32[18,8,128]{2,1,0:T(8,128)S(1)}, u32[]{:S(2)}, u32[]{:S(2)}) %collective-permute-start.11) | collective-permute-done | bytes 73760 | tf_op jit(solution)/shard_map/ppermute | solution.py:526
  37.7 0.6 %collective-permute-done.10.refs_2_ = f32[18,8,128]{2,1,0:T(8,128)S(1)} collective-permute-done((f32[18,8,128]{2,1,0:T(8,128)S(1)}, f32[18,8,128]{2,1,0:T(8,128)S(1)}, u32[]{:S(2)}, u32[]{:S(2)}) %collective-permute-start.10) | collective-permute-done | bytes 73760 | tf_op jit(solution)/shard_map/ppermute | solution.py:526
  38.3 0.0 collective-permute-done.9.refs_1_
  38.3 1.6 %closing.1 = f32[18,8,1024]{2,1,0:T(8,128)} custom-call(f32[18,8,128]{2,1,0:T(8,128)S(1)} %get-tuple-element.29.refs_0_, f32[18,8,128]{2,1,0:T(8,128)S(1)} %collective-permute-done.9.refs_1_, f32[18,8,128]{2,1,0:T(8,128)S(1)} %collective-permute-done.10.refs_2_, f32[18,8,128]{2,1,0:T(8,128)S(1)} %collective-permute-done.11.refs_3_, ...), custom_call_target="tpu_custom_call" | custom-call | tf_op jit(solution)/shard_map/closing/pallas_call | solution.py:549
  (1 shorter events, 0.0 us)
Async XLA Ops:
  0.0 10.3 %collective-permute-start = (f32[4,8,1,8,1024]{4,3,2,1,0:T(8,128)}, f32[4,8,1,8,1024]{4,3,2,1,0:T(8,128)S(1)}, u32[]{:S(2)}, u32[]{:S(2)}) collective-permute-start(f32[4,8,1,8,1024]{4,3,2,1,0:T(8,128)} %coeffs.1), channel_id=1, source_target_pairs={{0,1},{1,0},{2,3},{3,2},{4,5},{5,4},{6,7},{7,6},{8,9},{9,8},{10,11... | collective-permute-start | bytes 3145736 | tf_op jit(solution)/shard_map/ppermute | solution.py:454
  1.5 13.4 %collective-permute-start.1 = (f32[3,8,8,128]{3,2,1,0:T(8,128)S(1)}, f32[3,8,8,128]{3,2,1,0:T(8,128)S(1)}, u32[]{:S(2)}, u32[]{:S(2)}) collective-permute-start(f32[3,8,8,128]{3,2,1,0:T(8,128)S(1)} %get-tuple-element.23), channel_id=1, source_target_pairs={{2,0},{4,2},{6,4},{8,6},{10,8},{12,10},{14,12},{16,14},{18,16},{20... | collective-permute-start | bytes 294920 | tf_op jit(solution)/shard_map/ppermute | solution.py:464
  14.8 1.3 %collective-permute-start.2 = (f32[8,8,128]{2,1,0:T(8,128)S(1)}, f32[8,8,128]{2,1,0:T(8,128)S(1)}, u32[]{:S(2)}, u32[]{:S(2)}) collective-permute-start(f32[8,8,128]{2,1,0:T(8,128)S(1)} %pick.1.after), channel_id=1, source_target_pairs={{0,1},{1,0},{2,3},{3,2},{4,5},{5,4},{6,7},{7,6},{8,9},{9,8},{10,11... | collective-permute-start | bytes 98312 | tf_op jit(solution)/shard_map/ppermute | solution.py:498
  16.7 6.6 %collective-permute-start.5 = (f32[18,8,128]{2,1,0:T(8,128)S(1)}, f32[18,8,128]{2,1,0:T(8,128)S(1)}, u32[]{:S(2)}, u32[]{:S(2)}) collective-permute-start(f32[18,8,128]{2,1,0:T(8,128)S(1)} %get-tuple-element.25.refs_0_), channel_id=1, source_target_pairs={{0,4},{2,6},{4,0},{6,2},{8,12},{10,14},{12,8},{14,10},{16,20},{18,... | collective-permute-start | bytes 221192 | tf_op jit(solution)/shard_map/ppermute | solution.py:526
  16.8 7.3 %collective-permute-start.4 = (f32[18,8,128]{2,1,0:T(8,128)S(1)}, f32[18,8,128]{2,1,0:T(8,128)S(1)}, u32[]{:S(2)}, u32[]{:S(2)}) collective-permute-start(f32[18,8,128]{2,1,0:T(8,128)S(1)} %get-tuple-element.25.refs_0_), channel_id=1, source_target_pairs={{0,6},{2,4},{4,2},{6,0},{8,14},{10,12},{12,10},{14,8},{16,22},{18,... | collective-permute-start | bytes 221192 | tf_op jit(solution)/shard_map/ppermute | solution.py:526
  16.9 7.2 %collective-permute-start.3 = (f32[18,8,128]{2,1,0:T(8,128)S(1)}, f32[18,8,128]{2,1,0:T(8,128)S(1)}, u32[]{:S(2)}, u32[]{:S(2)}) collective-permute-start(f32[18,8,128]{2,1,0:T(8,128)S(1)} %get-tuple-element.25.refs_0_), channel_id=1, source_target_pairs={{0,2},{2,0},{4,6},{6,4},{8,10},{10,8},{12,14},{14,12},{16,18},{18,... | collective-permute-start | bytes 221192 | tf_op jit(solution)/shard_map/ppermute | solution.py:526
  24.2 6.6 %collective-permute-start.8 = (f32[18,8,128]{2,1,0:T(8,128)S(1)}, f32[18,8,128]{2,1,0:T(8,128)S(1)}, u32[]{:S(2)}, u32[]{:S(2)}) collective-permute-start(f32[18,8,128]{2,1,0:T(8,128)S(1)} %get-tuple-element.27.refs_0_), channel_id=1, source_target_pairs={{0,16},{2,18},{4,20},{6,22},{8,24},{10,26},{12,28},{14,30},{16,0},... | collective-permute-start | bytes 221192 | tf_op jit(solution)/shard_map/ppermute | solution.py:526
  24.3 6.9 %collective-permute-start.7 = (f32[18,8,128]{2,1,0:T(8,128)S(1)}, f32[18,8,128]{2,1,0:T(8,128)S(1)}, u32[]{:S(2)}, u32[]{:S(2)}) collective-permute-start(f32[18,8,128]{2,1,0:T(8,128)S(1)} %get-tuple-element.27.refs_0_), channel_id=1, source_target_pairs={{0,24},{2,26},{4,28},{6,30},{8,16},{10,18},{12,20},{14,22},{16,8},... | collective-permute-start | bytes 221192 | tf_op jit(solution)/shard_map/ppermute | solution.py:526
  24.4 6.8 %collective-permute-start.6 = (f32[18,8,128]{2,1,0:T(8,128)S(1)}, f32[18,8,128]{2,1,0:T(8,128)S(1)}, u32[]{:S(2)}, u32[]{:S(2)}) collective-permute-start(f32[18,8,128]{2,1,0:T(8,128)S(1)} %get-tuple-element.27.refs_0_), channel_id=1, source_target_pairs={{0,8},{2,10},{4,12},{6,14},{8,0},{10,2},{12,4},{14,6},{16,24},{18,... | collective-permute-start | bytes 221192 | tf_op jit(solution)/shard_map/ppermute | solution.py:526
  31.3 6.4 %collective-permute-start.11 = (f32[18,8,128]{2,1,0:T(8,128)S(1)}, f32[18,8,128]{2,1,0:T(8,128)S(1)}, u32[]{:S(2)}, u32[]{:S(2)}) collective-permute-start(f32[18,8,128]{2,1,0:T(8,128)S(1)} %get-tuple-element.29.refs_0_), channel_id=1, source_target_pairs={{0,64},{2,66},{4,68},{6,70},{8,72},{10,74},{12,76},{14,78},{16,80}... | collective-permute-start | bytes 221192 | tf_op jit(solution)/shard_map/ppermute | solution.py:526
  32.2 6.0 %collective-permute-start.10 = (f32[18,8,128]{2,1,0:T(8,128)S(1)}, f32[18,8,128]{2,1,0:T(8,128)S(1)}, u32[]{:S(2)}, u32[]{:S(2)}) collective-permute-start(f32[18,8,128]{2,1,0:T(8,128)S(1)} %get-tuple-element.29.refs_0_), channel_id=1, source_target_pairs={{0,96},{2,98},{4,100},{6,102},{8,104},{10,106},{12,108},{14,110},{... | collective-permute-start | bytes 221192 | tf_op jit(solution)/shard_map/ppermute | solution.py:526
  33.7 4.6 %collective-permute-start.9 = (f32[18,8,128]{2,1,0:T(8,128)S(1)}, f32[18,8,128]{2,1,0:T(8,128)S(1)}, u32[]{:S(2)}, u32[]{:S(2)}) collective-permute-start(f32[18,8,128]{2,1,0:T(8,128)S(1)} %get-tuple-element.29.refs_0_), channel_id=1, source_target_pairs={{0,32},{2,34},{4,36},{6,38},{8,40},{10,42},{12,44},{14,46},{16,48}... | collective-permute-start | bytes 221192 | tf_op jit(solution)/shard_map/ppermute | solution.py:526

commit v2 on v1

--- a/solution.py
+++ b/solution.py
@@ -11,8 +11,8 @@
 NT_LOCAL = 8
 SMEAR = 0.1
 SPLIT = 2
-PEERS = (1, 3, 2)
-LAST_PEERS = (1, 3, 2)
+PEERS = (2, 3, 1)
+LAST_PEERS = (1, 2, 3)
 ROOT_THIRD = 1.0 / 3.0**0.5
 VMEM_LIMIT = 48 * 1024 * 1024
 WHOLE = pl.BlockSpec(memory_space=pltpu.VMEM)
@@ -244,35 +244,19 @@
     return plus(forward, mapped(below, backward_term(spatial, temporal, ahead)))
 
 
-def by_row(coeffs, rows, sems, directions):
-    return [
-        pltpu.make_async_copy(
-            coeffs.at[direction, :, 0, :, pl.ds(v * LANES, LANES)],
-            rows.at[n, :, pl.ds(v * NT_LOCAL, NT_LOCAL), :],
-            sems.at[n, v],
-        )
-        for n, direction in enumerate(directions)
-        for v in range(ROWS)
-    ]
-
-
 def prepare_kernel(coeffs, rows, first, sems):
-    copies = by_row(coeffs, rows, sems, (0, 1, 2, 3))
+    copies = [pltpu.make_async_copy(coeffs.at[n], rows.at[n], sems.at[n]) for n in range(4)]
     for copy in copies:
         copy.start()
     for direction in range(4):
-        for copy in copies[direction * ROWS : (direction + 1) * ROWS]:
-            copy.wait()
+        copies[direction].wait()
         if direction < 3:
             for a, value in enumerate(slice_of(rows, direction, 0)):
                 first[direction, a] = value
 
 
-def local_kernel(rows, other, links, staple, other_rows, sems):
+def local_kernel(rows, links, staple):
     last = NT_LOCAL - 1
-    copies = by_row(other, other_rows, sems, (0, 3))
-    for copy in copies:
-        copy.start()
 
     def make(t):
         for direction in range(4):
@@ -294,14 +278,12 @@
         return carry
 
     lax.fori_loop(0, last, step, 0)
-    for copy in copies:
-        copy.wait()
 
 
 def chain_steps(high, low, links, staple, rows, other_links, terms, later, put):
     def step(i, carry):
         t = high - 1 - i
-        write(other_links, link_of(slice_of(rows, 1, t)), 1)
+        write(other_links, link_of(slice_of(rows, 3, t)), 1)
         write(other_links, link_of(slice_of(rows, 0, t)), 2)
         write(
             terms,
@@ -330,8 +312,8 @@
 
 def late_chain_kernel(links, staple, rows, partial, other_last, other_links, terms, later):
     last = NT_LOCAL - 1
-    for n in range(2):
-        write(other_last, link_of(slice_of(rows, n, last)), n)
+    for n, direction in enumerate((0, 3)):
+        write(other_last, link_of(slice_of(rows, direction, last)), n)
     write(other_links, read(other_last, 0), 0)
     write(later, unit())
 
@@ -341,8 +323,9 @@
     chain_steps(last, SPLIT, links, staple, rows, other_links, terms, later, put)
 
 
-def early_chain_kernel(links, staple, rows, late, after, partial, other_links, terms, later):
-    del after
+def early_chain_kernel(
+    links, staple, rows, late, other_last, next_rows, partial, last_terms, other_links, terms, later, ahead
+):
     write(other_links, link_of(slice_of(rows, 0, SPLIT)), 0)
     write(later, read(late, 0))
 
@@ -350,6 +333,19 @@
         write(partial, product, t)
 
     chain_steps(SPLIT, 0, links, staple, rows, other_links, terms, later, put)
+    last = NT_LOCAL - 1
+    for direction in range(3):
+        write(ahead, link_of([next_rows[direction, a] for a in range(8)]), direction)
+    temporal = read(links, 3, last)
+    write(
+        last_terms,
+        plane_terms(read(links, 1, last), temporal, read(ahead, 1), from_y_above, from_y_below),
+    )
+    for term in (
+        lambda: plane_terms(read(links, 2, last), temporal, read(ahead, 2), from_z_above, from_z_below),
+        lambda: forward_term(read(links, 0, last), read(other_last, 1), read(ahead, 0)),
+    ):
+        write(last_terms, plus(read(last_terms), term()))
 
 
 def pick_kernel(ahead, after, out):
@@ -357,23 +353,14 @@
     out[...] = ahead[0]
 
 
-def last_slice_kernel(links, other_last, next_rows, other_next, partial, smeared_last, total, ahead, terms):
-    last = NT_LOCAL - 1
-    for direction in range(3):
-        write(ahead, link_of([next_rows[direction, a] for a in range(8)]), direction)
-    write(ahead, link_of([other_next[a] for a in range(8)]), 3)
-    temporal = read(links, 3, last)
-    write(
-        terms,
-        plane_terms(read(links, 1, last), temporal, read(ahead, 1), from_y_above, from_y_below),
-    )
-    for term in (
-        lambda: plane_terms(read(links, 2, last), temporal, read(ahead, 2), from_z_above, from_z_below),
-        lambda: forward_term(read(links, 0, last), read(other_last, 1), read(ahead, 0)),
-        lambda: backward_term(read(other_last, 0), read(other_last, 1), read(ahead, 3)),
-    ):
-        write(terms, plus(read(terms), term()))
-    smeared = mul(smearing(read(terms), temporal), temporal)
+def last_slice_kernel(links, other_last, last_terms, other_next, partial, smeared_last, total, ahead):
+    write(ahead, link_of([other_next[a] for a in range(8)]))
+    temporal = read(links, 3, NT_LOCAL - 1)
+    terms = plus(
+        read(last_terms), backward_term(read(other_last, 0), read(other_last, 1), read(ahead))
+    )
+    write(ahead, terms)
+    smeared = mul(smearing(read(ahead), temporal), temporal)
     write(smeared_last, smeared)
     write(total, mul(read(partial, 0), read(smeared_last)))
 
@@ -420,15 +407,9 @@
             lax.fori_loop(low, high, step, 0)
         put(last, [[held[0, 9 * part + 3 * i + j] for j in range(3)] for part in range(2)])
         for part in range(2):
-            for v in range(ROWS):
-                copies.append(
-                    pltpu.make_async_copy(
-                        rows.at[pl.ds(9 * part + 3 * i, 3), pl.ds(v * NT_LOCAL, NT_LOCAL), :],
-                        out.at[pl.ds(9 * part + 3 * i, 3), :, pl.ds(v * LANES, LANES)],
-                        sems.at[i, part, v],
-                    )
-                )
-                copies[-1].start()
+            planes = pl.ds(9 * part + 3 * i, 3)
+            copies.append(pltpu.make_async_copy(rows.at[planes], out.at[planes], sems.at[i, part]))
+            copies[-1].start()
     for copy in copies:
         copy.wait()
 
@@ -451,27 +432,28 @@
 
 def shards(coeffs):
     count = lax.axis_size("tm")
-    other = lax.ppermute(coeffs, "space", [(0, 1), (1, 0)])
+    coeffs = coeffs.reshape(4, 8, NT_LOCAL, ROWS, LANES).swapaxes(2, 3)
+    coeffs = coeffs.reshape(4, 8, ROWS * NT_LOCAL, LANES)
+    other_rows = lax.ppermute(coeffs, "space", [(0, 1), (1, 0)])
     rows, first = pl.pallas_call(
         prepare_kernel,
         out_shape=(block(4, 8, ROWS * NT_LOCAL, LANES), block(3, 8, ROWS, LANES)),
         in_specs=[pl.BlockSpec(memory_space=pltpu.HBM)],
         out_specs=(WHOLE, WHOLE),
-        scratch_shapes=[pltpu.SemaphoreType.DMA((4, ROWS))],
+        scratch_shapes=[pltpu.SemaphoreType.DMA((4,))],
         compiler_params=params(),
         name="prepare",
     )(pltpu.with_memory_space_constraint(coeffs, pltpu.HBM))
     ahead = lax.ppermute(first, "tm", [((i + 1) % count, i) for i in range(count)])
-    links, staple, other_rows = pl.pallas_call(
+    links, staple = pl.pallas_call(
         local_kernel,
-        out_shape=(field(4, NT_LOCAL), field(NT_LOCAL), block(2, 8, ROWS * NT_LOCAL, LANES)),
-        in_specs=[WHOLE, WHOLE],
-        out_specs=(WHOLE, WHOLE, WHOLE),
-        scratch_shapes=[pltpu.SemaphoreType.DMA((2, ROWS))],
+        out_shape=(field(4, NT_LOCAL), field(NT_LOCAL)),
+        in_specs=[WHOLE],
+        out_specs=(WHOLE, WHOLE),
         compiler_params=params(),
         cost_estimate=cost(20_000_000),
         name="local_terms",
-    )(rows, other)
+    )(rows)
     chain_scratch = [
         pltpu.VMEM((3, 18, ROWS, LANES), jnp.float32),
         pltpu.VMEM((18, ROWS, LANES), jnp.float32),
@@ -496,29 +478,26 @@
         name="pick",
     )(ahead, late)
     other_ahead = lax.ppermute(ahead_x, "space", [(0, 1), (1, 0)])
-    early = pl.pallas_call(
+    early, last_terms = pl.pallas_call(
         early_chain_kernel,
-        out_shape=field(SPLIT),
-        in_specs=[WHOLE] * 5,
-        out_specs=WHOLE,
-        scratch_shapes=chain_scratch,
+        out_shape=(field(SPLIT), field()),
+        in_specs=[WHOLE] * 6,
+        out_specs=(WHOLE, WHOLE),
+        scratch_shapes=chain_scratch + [pltpu.VMEM((3, 18, ROWS, LANES), jnp.float32)],
         compiler_params=params(),
         cost_estimate=cost(8_000_000),
         name="early_chain",
-    )(links, staple, other_rows, late, ahead_x)
+    )(links, staple, other_rows, late, other_last, ahead)
     tail, total = pl.pallas_call(
         last_slice_kernel,
         out_shape=(field(), field()),
         in_specs=[WHOLE] * 5,
         out_specs=(WHOLE, WHOLE),
-        scratch_shapes=[
-            pltpu.VMEM((4, 18, ROWS, LANES), jnp.float32),
-            pltpu.VMEM((18, ROWS, LANES), jnp.float32),
-        ],
-        compiler_params=params(),
-        cost_estimate=cost(5_000_000),
+        scratch_shapes=[pltpu.VMEM((18, ROWS, LANES), jnp.float32)],
+        compiler_params=params(),
+        cost_estimate=cost(3_000_000),
         name="last_slice",
-    )(links, other_last, ahead, other_ahead, early)
+    )(links, other_last, last_terms, other_ahead, early)
     low = 1
     while True:
         peers = LAST_PEERS if low * 4 >= count else PEERS
@@ -548,17 +527,18 @@
 
     out = pl.pallas_call(
         closing,
-        out_shape=jax.ShapeDtypeStruct((18, NT_LOCAL, ROWS * LANES), jnp.float32),
+        out_shape=block(18, ROWS * NT_LOCAL, LANES),
         in_specs=[WHOLE] * 7,
         out_specs=pl.BlockSpec(memory_space=pltpu.HBM),
         scratch_shapes=[
             held,
             pltpu.VMEM((18, ROWS * NT_LOCAL, LANES), jnp.float32),
-            pltpu.SemaphoreType.DMA((3, 2, ROWS)),
+            pltpu.SemaphoreType.DMA((3, 2)),
         ],
         compiler_params=params(),
         name="closing",
     )(total, *received, tail, early, late)
+    out = out.reshape(18, ROWS, NT_LOCAL, LANES).swapaxes(1, 2)
     return out.reshape(2, 3, 3, 1, NT_LOCAL, ROWS * LANES)
 
 

time: 40.1 us -> 38.9 us (0.970)
  Pallas kernels: 8.96 us -> 8.03 us
  transfers between devices with their start and end apart: 12 -> 12, of which waited for: 7 -> 6; matrix products, arithmetic and copies ran while one was open for 0% -> 0% of each run, Pallas kernels for 16% -> 16%
where the time goes in v2:
time: 38.9 us; the launch traced here: 38.8 us
  starting transfers between devices  19.8 us (51%)
  waiting for transfers between devices  10.8 us (28%)
  Pallas kernels  8.03 us (21%)
    ppermute x9, waiting for transfers between devices, shards(): lax.ppermute(total, 'tm', [(i, i ^ low * k) for i in range(count)])  10.8 us
    ppermute x9, starting transfers between devices, shards(): lax.ppermute(total, 'tm', [(i, i ^ low * k) for i in range(count)])  10.7 us
    ppermute x1, starting transfers between devices, shards(): lax.ppermute(first, 'tm', [((i + 1) % count, i) for i in range(count)])  8.83 us
    pallas_call x1, Pallas kernels, shards(): pl.pallas_call(local_kernel, out_shape=(field(4, NT_LOCAL), field(NT_LOCA...  2.77 us
    pallas_call x1, Pallas kernels, shards(): pl.pallas_call(late_chain_kernel, out_shape=(field(NT_LOCAL - 1 - SPLIT),...  1.43 us
    pallas_call x1, Pallas kernels, shards(): pl.pallas_call(prepare_kernel, out_shape=(block(4, 8, ROWS * NT_LOCAL, LA...  1.22 us
    pallas_call x1, Pallas kernels, shards(): pl.pallas_call(closing, out_shape=block(18, ROWS * NT_LOCAL, LANES), in_s...  1.18 us
    pallas_call x1, Pallas kernels, shards(): pl.pallas_call(early_chain_kernel, out_shape=(field(SPLIT), field()), in_...  0.96 us
  transfers between devices with their start and end apart: 12, of which 6 were waited for; matrix products, arithmetic and copies ran while one was open for 0% of the time, Pallas kernels for 16%

profile of v2, /device:TPU:0, one launch (start us, length us, event | category | flops | bytes accessed | tf_op | source)
XLA Modules:
  0.0 38.8 jit_solution(17558162078811552538)
XLA Ops:
  0.0 0.0 collective-permute-start
  0.0 1.2 %prepare.1 = (f32[4,8,64,128]{3,2,1,0:T(8,128)S(1)}, f32[3,8,8,128]{3,2,1,0:T(8,128)S(1)}) custom-call(f32[4,8,64,128]{3,2,1,0:T(8,128)} %bitcast.11), custom_call_target="tpu_custom_call" | custom-call | tf_op jit(solution)/shard_map/prepare/pallas_call | solution.py:438
  1.2 8.8 %collective-permute-start.1 = (f32[3,8,8,128]{3,2,1,0:T(8,128)S(1)}, f32[3,8,8,128]{3,2,1,0:T(8,128)S(1)}, u32[]{:S(2)}, u32[]{:S(2)}) collective-permute-start(f32[3,8,8,128]{3,2,1,0:T(8,128)S(1)} %get-tuple-element.24), channel_id=1, source_target_pairs={{2,0},{4,2},{6,4},{8,6},{10,8},{12,10},{14,12},{16,14},{18,16},{20... | collective-permute-start | bytes 294920 | tf_op jit(solution)/shard_map/ppermute | solution.py:447
  10.1 2.8 %local_terms.1 = (f32[4,8,18,8,128]{4,3,2,1,0:T(8,128)S(1)}, f32[8,18,8,128]{3,2,1,0:T(8,128)S(1)}) custom-call(f32[4,8,64,128]{3,2,1,0:T(8,128)S(1)} %get-tuple-element.19.rows), custom_call_target="tpu_custom_call" | custom-call | flops 20000000 | bytes 1000000 | tf_op jit(solution)/shard_map/local_terms/pallas_call | solution.py:448
  12.8 0.0 collective-permute-done.rows
  12.9 1.4 %late_chain.1 = (f32[5,18,8,128]{3,2,1,0:T(8,128)S(1)}, f32[2,18,8,128]{3,2,1,0:T(8,128)S(1)}) custom-call(f32[4,8,18,8,128]{4,3,2,1,0:T(8,128)S(1)} %get-tuple-element.20.links, f32[8,18,8,128]{3,2,1,0:T(8,128)S(1)} %get-tuple-element.21.staple, f32[4,8,64,128]{3,2,1,0:T(8,128)S(1)} %collective-permute-done.rows), custom_call_target="tpu_custom_call" | custom-call | flops 8000000 | bytes 1000000 | tf_op jit(solution)/shard_map/late_chain/pallas_call | solution.py:462
  14.3 0.0 collective-permute-done.1.next_rows.ahead
  14.3 0.3 collective-permute-start.2
  14.6 1.0 %early_chain.1 = (f32[2,18,8,128]{3,2,1,0:T(8,128)S(1)}, f32[18,8,128]{2,1,0:T(8,128)S(1)}) custom-call(f32[4,8,18,8,128]{4,3,2,1,0:T(8,128)S(1)} %get-tuple-element.20.links, f32[8,18,8,128]{3,2,1,0:T(8,128)S(1)} %get-tuple-element.21.staple, f32[4,8,64,128]{3,2,1,0:T(8,128)S(1)} %collective-permute-done.rows, ...), custom_call_target="tpu_custom_call" | custom-call | flops 8000000 | bytes 1000000 | tf_op jit(solution)/shard_map/early_chain/pallas_call | solution.py:481
  15.6 0.0 collective-permute-done.2.other_next
  15.6 0.2 last_slice.1
  15.8 0.1 collective-permute-start.3
  15.9 0.1 collective-permute-start.4
  16.0 3.4 %collective-permute-start.5 = (f32[18,8,128]{2,1,0:T(8,128)S(1)}, f32[18,8,128]{2,1,0:T(8,128)S(1)}, u32[]{:S(2)}, u32[]{:S(2)}) collective-permute-start(f32[18,8,128]{2,1,0:T(8,128)S(1)} %get-tuple-element.27.refs_0_), channel_id=1, source_target_pairs={{0,2},{2,0},{4,6},{6,4},{8,10},{10,8},{12,14},{14,12},{16,18},{18,... | collective-permute-start | bytes 221192 | tf_op jit(solution)/shard_map/ppermute | solution.py:505
  19.3 3.1 %collective-permute-done.3.refs_1_ = f32[18,8,128]{2,1,0:T(8,128)S(1)} collective-permute-done((f32[18,8,128]{2,1,0:T(8,128)S(1)}, f32[18,8,128]{2,1,0:T(8,128)S(1)}, u32[]{:S(2)}, u32[]{:S(2)}) %collective-permute-start.3) | collective-permute-done | bytes 73760 | tf_op jit(solution)/shard_map/ppermute | solution.py:505
  22.5 0.7 %collective-permute-done.4.refs_2_ = f32[18,8,128]{2,1,0:T(8,128)S(1)} collective-permute-done((f32[18,8,128]{2,1,0:T(8,128)S(1)}, f32[18,8,128]{2,1,0:T(8,128)S(1)}, u32[]{:S(2)}, u32[]{:S(2)}) %collective-permute-start.4) | collective-permute-done | bytes 73760 | tf_op jit(solution)/shard_map/ppermute | solution.py:505
  23.2 0.0 collective-permute-done.5.refs_3_
  23.2 0.1 level_1.1
  23.3 0.1 collective-permute-start.6
  23.4 0.1 collective-permute-start.7
  23.5 3.4 %collective-permute-start.8 = (f32[18,8,128]{2,1,0:T(8,128)S(1)}, f32[18,8,128]{2,1,0:T(8,128)S(1)}, u32[]{:S(2)}, u32[]{:S(2)}) collective-permute-start(f32[18,8,128]{2,1,0:T(8,128)S(1)} %get-tuple-element.29.refs_0_), channel_id=1, source_target_pairs={{0,8},{2,10},{4,12},{6,14},{8,0},{10,2},{12,4},{14,6},{16,24},{18,... | collective-permute-start | bytes 221192 | tf_op jit(solution)/shard_map/ppermute | solution.py:505
  26.9 3.0 %collective-permute-done.6.refs_1_ = f32[18,8,128]{2,1,0:T(8,128)S(1)} collective-permute-done((f32[18,8,128]{2,1,0:T(8,128)S(1)}, f32[18,8,128]{2,1,0:T(8,128)S(1)}, u32[]{:S(2)}, u32[]{:S(2)}) %collective-permute-start.6) | collective-permute-done | bytes 73760 | tf_op jit(solution)/shard_map/ppermute | solution.py:505
  29.9 0.4 collective-permute-done.7.refs_2_
  30.3 0.0 collective-permute-done.8.refs_3_
  30.3 0.1 level_4.1
  30.4 1.3 %collective-permute-start.10 = (f32[18,8,128]{2,1,0:T(8,128)S(1)}, f32[18,8,128]{2,1,0:T(8,128)S(1)}, u32[]{:S(2)}, u32[]{:S(2)}) collective-permute-start(f32[18,8,128]{2,1,0:T(8,128)S(1)} %get-tuple-element.31.refs_0_), channel_id=1, source_target_pairs={{0,64},{2,66},{4,68},{6,70},{8,72},{10,74},{12,76},{14,78},{16,80}... | collective-permute-start | bytes 221192 | tf_op jit(solution)/shard_map/ppermute | solution.py:505
  31.7 1.5 %collective-permute-start.11 = (f32[18,8,128]{2,1,0:T(8,128)S(1)}, f32[18,8,128]{2,1,0:T(8,128)S(1)}, u32[]{:S(2)}, u32[]{:S(2)}) collective-permute-start(f32[18,8,128]{2,1,0:T(8,128)S(1)} %get-tuple-element.31.refs_0_), channel_id=1, source_target_pairs={{0,96},{2,98},{4,100},{6,102},{8,104},{10,106},{12,108},{14,110},{... | collective-permute-start | bytes 221192 | tf_op jit(solution)/shard_map/ppermute | solution.py:505
  33.2 0.8 %collective-permute-start.9 = (f32[18,8,128]{2,1,0:T(8,128)S(1)}, f32[18,8,128]{2,1,0:T(8,128)S(1)}, u32[]{:S(2)}, u32[]{:S(2)}) collective-permute-start(f32[18,8,128]{2,1,0:T(8,128)S(1)} %get-tuple-element.31.refs_0_), channel_id=1, source_target_pairs={{0,32},{2,34},{4,36},{6,38},{8,40},{10,42},{12,44},{14,46},{16,48}... | collective-permute-start | bytes 221192 | tf_op jit(solution)/shard_map/ppermute | solution.py:505
  34.0 2.8 %collective-permute-done.10.refs_2_ = f32[18,8,128]{2,1,0:T(8,128)S(1)} collective-permute-done((f32[18,8,128]{2,1,0:T(8,128)S(1)}, f32[18,8,128]{2,1,0:T(8,128)S(1)}, u32[]{:S(2)}, u32[]{:S(2)}) %collective-permute-start.10) | collective-permute-done | bytes 73760 | tf_op jit(solution)/shard_map/ppermute | solution.py:505
  36.8 0.8 %collective-permute-done.11.refs_3_ = f32[18,8,128]{2,1,0:T(8,128)S(1)} collective-permute-done((f32[18,8,128]{2,1,0:T(8,128)S(1)}, f32[18,8,128]{2,1,0:T(8,128)S(1)}, u32[]{:S(2)}, u32[]{:S(2)}) %collective-permute-start.11) | collective-permute-done | bytes 73760 | tf_op jit(solution)/shard_map/ppermute | solution.py:505
  37.6 0.0 collective-permute-done.9.refs_1_
  37.6 1.2 %closing.1 = f32[18,64,128]{2,1,0:T(8,128)} custom-call(f32[18,8,128]{2,1,0:T(8,128)S(1)} %get-tuple-element.31.refs_0_, f32[18,8,128]{2,1,0:T(8,128)S(1)} %collective-permute-done.9.refs_1_, f32[18,8,128]{2,1,0:T(8,128)S(1)} %collective-permute-done.10.refs_2_, f32[18,8,128]{2,1,0:T(8,128)S(1)} %collective-permute-done.11.refs_3_, ...), custom_call_target="tpu_custom_call" | custom-call | tf_op jit(solution)/shard_map/closing/pallas_call | solution.py:528
  (1 shorter events, 0.0 us)
Async XLA Ops:
  0.0 12.8 %collective-permute-start = (f32[4,8,64,128]{3,2,1,0:T(8,128)}, f32[4,8,64,128]{3,2,1,0:T(8,128)S(1)}, u32[]{:S(2)}, u32[]{:S(2)}) collective-permute-start(f32[4,8,64,128]{3,2,1,0:T(8,128)} %bitcast.10), channel_id=1, source_target_pairs={{0,1},{1,0},{2,3},{3,2},{4,5},{5,4},{6,7},{7,6},{8,9},{9,8},{10,11... | collective-permute-start | bytes 3145736 | tf_op jit(solution)/shard_map/ppermute | solution.py:437
  1.2 13.1 %collective-permute-start.1 = (f32[3,8,8,128]{3,2,1,0:T(8,128)S(1)}, f32[3,8,8,128]{3,2,1,0:T(8,128)S(1)}, u32[]{:S(2)}, u32[]{:S(2)}) collective-permute-start(f32[3,8,8,128]{3,2,1,0:T(8,128)S(1)} %get-tuple-element.24), channel_id=1, source_target_pairs={{2,0},{4,2},{6,4},{8,6},{10,8},{12,10},{14,12},{16,14},{18,16},{20... | collective-permute-start | bytes 294920 | tf_op jit(solution)/shard_map/ppermute | solution.py:447
  14.3 1.3 %collective-permute-start.2 = (f32[8,8,128]{2,1,0:T(8,128)S(1)}, f32[8,8,128]{2,1,0:T(8,128)S(1)}, u32[]{:S(2)}, u32[]{:S(2)}) collective-permute-start(f32[8,8,128]{2,1,0:T(8,128)S(1)} %pick.1), channel_id=1, source_target_pairs={{0,1},{1,0},{2,3},{3,2},{4,5},{5,4},{6,7},{7,6},{8,9},{9,8},{10,11... | collective-permute-start | bytes 98312 | tf_op jit(solution)/shard_map/ppermute | solution.py:480
  15.8 6.7 %collective-permute-start.3 = (f32[18,8,128]{2,1,0:T(8,128)S(1)}, f32[18,8,128]{2,1,0:T(8,128)S(1)}, u32[]{:S(2)}, u32[]{:S(2)}) collective-permute-start(f32[18,8,128]{2,1,0:T(8,128)S(1)} %get-tuple-element.27.refs_0_), channel_id=1, source_target_pairs={{0,4},{2,6},{4,0},{6,2},{8,12},{10,14},{12,8},{14,10},{16,20},{18,... | collective-permute-start | bytes 221192 | tf_op jit(solution)/shard_map/ppermute | solution.py:505
  15.9 7.3 %collective-permute-start.4 = (f32[18,8,128]{2,1,0:T(8,128)S(1)}, f32[18,8,128]{2,1,0:T(8,128)S(1)}, u32[]{:S(2)}, u32[]{:S(2)}) collective-permute-start(f32[18,8,128]{2,1,0:T(8,128)S(1)} %get-tuple-element.27.refs_0_), channel_id=1, source_target_pairs={{0,6},{2,4},{4,2},{6,0},{8,14},{10,12},{12,10},{14,8},{16,22},{18,... | collective-permute-start | bytes 221192 | tf_op jit(solution)/shard_map/ppermute | solution.py:505
  16.0 7.2 %collective-permute-start.5 = (f32[18,8,128]{2,1,0:T(8,128)S(1)}, f32[18,8,128]{2,1,0:T(8,128)S(1)}, u32[]{:S(2)}, u32[]{:S(2)}) collective-permute-start(f32[18,8,128]{2,1,0:T(8,128)S(1)} %get-tuple-element.27.refs_0_), channel_id=1, source_target_pairs={{0,2},{2,0},{4,6},{6,4},{8,10},{10,8},{12,14},{14,12},{16,18},{18,... | collective-permute-start | bytes 221192 | tf_op jit(solution)/shard_map/ppermute | solution.py:505
  23.3 6.6 %collective-permute-start.6 = (f32[18,8,128]{2,1,0:T(8,128)S(1)}, f32[18,8,128]{2,1,0:T(8,128)S(1)}, u32[]{:S(2)}, u32[]{:S(2)}) collective-permute-start(f32[18,8,128]{2,1,0:T(8,128)S(1)} %get-tuple-element.29.refs_0_), channel_id=1, source_target_pairs={{0,16},{2,18},{4,20},{6,22},{8,24},{10,26},{12,28},{14,30},{16,0},... | collective-permute-start | bytes 221192 | tf_op jit(solution)/shard_map/ppermute | solution.py:505
  23.4 6.9 %collective-permute-start.7 = (f32[18,8,128]{2,1,0:T(8,128)S(1)}, f32[18,8,128]{2,1,0:T(8,128)S(1)}, u32[]{:S(2)}, u32[]{:S(2)}) collective-permute-start(f32[18,8,128]{2,1,0:T(8,128)S(1)} %get-tuple-element.29.refs_0_), channel_id=1, source_target_pairs={{0,24},{2,26},{4,28},{6,30},{8,16},{10,18},{12,20},{14,22},{16,8},... | collective-permute-start | bytes 221192 | tf_op jit(solution)/shard_map/ppermute | solution.py:505
  23.5 6.8 %collective-permute-start.8 = (f32[18,8,128]{2,1,0:T(8,128)S(1)}, f32[18,8,128]{2,1,0:T(8,128)S(1)}, u32[]{:S(2)}, u32[]{:S(2)}) collective-permute-start(f32[18,8,128]{2,1,0:T(8,128)S(1)} %get-tuple-element.29.refs_0_), channel_id=1, source_target_pairs={{0,8},{2,10},{4,12},{6,14},{8,0},{10,2},{12,4},{14,6},{16,24},{18,... | collective-permute-start | bytes 221192 | tf_op jit(solution)/shard_map/ppermute | solution.py:505
  30.4 6.4 %collective-permute-start.10 = (f32[18,8,128]{2,1,0:T(8,128)S(1)}, f32[18,8,128]{2,1,0:T(8,128)S(1)}, u32[]{:S(2)}, u32[]{:S(2)}) collective-permute-start(f32[18,8,128]{2,1,0:T(8,128)S(1)} %get-tuple-element.31.refs_0_), channel_id=1, source_target_pairs={{0,64},{2,66},{4,68},{6,70},{8,72},{10,74},{12,76},{14,78},{16,80}... | collective-permute-start | bytes 221192 | tf_op jit(solution)/shard_map/ppermute | solution.py:505
  31.7 5.8 %collective-permute-start.11 = (f32[18,8,128]{2,1,0:T(8,128)S(1)}, f32[18,8,128]{2,1,0:T(8,128)S(1)}, u32[]{:S(2)}, u32[]{:S(2)}) collective-permute-start(f32[18,8,128]{2,1,0:T(8,128)S(1)} %get-tuple-element.31.refs_0_), channel_id=1, source_target_pairs={{0,96},{2,98},{4,100},{6,102},{8,104},{10,106},{12,108},{14,110},{... | collective-permute-start | bytes 221192 | tf_op jit(solution)/shard_map/ppermute | solution.py:505
  33.2 4.4 %collective-permute-start.9 = (f32[18,8,128]{2,1,0:T(8,128)S(1)}, f32[18,8,128]{2,1,0:T(8,128)S(1)}, u32[]{:S(2)}, u32[]{:S(2)}) collective-permute-start(f32[18,8,128]{2,1,0:T(8,128)S(1)} %get-tuple-element.31.refs_0_), channel_id=1, source_target_pairs={{0,32},{2,34},{4,36},{6,38},{8,40},{10,42},{12,44},{14,46},{16,48}... | collective-permute-start | bytes 221192 | tf_op jit(solution)/shard_map/ppermute | solution.py:505

commit v3 on v2

--- a/solution.py
+++ b/solution.py
@@ -244,18 +244,7 @@
     return plus(forward, mapped(below, backward_term(spatial, temporal, ahead)))
 
 
-def prepare_kernel(coeffs, rows, first, sems):
-    copies = [pltpu.make_async_copy(coeffs.at[n], rows.at[n], sems.at[n]) for n in range(4)]
-    for copy in copies:
-        copy.start()
-    for direction in range(4):
-        copies[direction].wait()
-        if direction < 3:
-            for a, value in enumerate(slice_of(rows, direction, 0)):
-                first[direction, a] = value
-
-
-def local_kernel(rows, links, staple):
+def local_terms(rows, links, staple):
     last = NT_LOCAL - 1
 
     def make(t):
@@ -278,6 +267,27 @@
         return carry
 
     lax.fori_loop(0, last, step, 0)
+
+
+def first_kernel(coeffs, coeffs_by_row, first, links, staple, rows, sem):
+    copy = pltpu.make_async_copy(coeffs.at[pl.ds(0, 3), :, :, 0, :], first, sem)
+    copy.start()
+    copy.wait()
+
+    @pl.when(lax.axis_index("tm") == 0)
+    def _():
+        fetch = pltpu.make_async_copy(coeffs_by_row, rows, sem)
+        fetch.start()
+        fetch.wait()
+        local_terms(rows, links, staple)
+
+
+def local_kernel(rows, links_before, staple_before, links, staple):
+    del links_before, staple_before
+
+    @pl.when(lax.axis_index("tm") != 0)
+    def _():
+        local_terms(rows, links, staple)
 
 
 def chain_steps(high, low, links, staple, rows, other_links, terms, later, put):
@@ -399,12 +409,9 @@
 
         for partial, low, high in ((early, 0, SPLIT), (late, SPLIT, last)):
 
-            def step(t, carry, partial=partial, low=low, i=i, put=put):
+            for t in range(low, high):
                 left = [[partial[t - low, 9 * part + 3 * i + j] for j in range(3)] for part in range(2)]
                 put(t, row_times(left, read(held, 0)))
-                return carry
-
-            lax.fori_loop(low, high, step, 0)
         put(last, [[held[0, 9 * part + 3 * i + j] for j in range(3)] for part in range(2)])
         for part in range(2):
             planes = pl.ds(9 * part + 3 * i, 3)
@@ -433,27 +440,35 @@
 def shards(coeffs):
     count = lax.axis_size("tm")
     coeffs = coeffs.reshape(4, 8, NT_LOCAL, ROWS, LANES).swapaxes(2, 3)
-    coeffs = coeffs.reshape(4, 8, ROWS * NT_LOCAL, LANES)
-    other_rows = lax.ppermute(coeffs, "space", [(0, 1), (1, 0)])
-    rows, first = pl.pallas_call(
-        prepare_kernel,
-        out_shape=(block(4, 8, ROWS * NT_LOCAL, LANES), block(3, 8, ROWS, LANES)),
-        in_specs=[pl.BlockSpec(memory_space=pltpu.HBM)],
-        out_specs=(WHOLE, WHOLE),
-        scratch_shapes=[pltpu.SemaphoreType.DMA((4,))],
-        compiler_params=params(),
-        name="prepare",
-    )(pltpu.with_memory_space_constraint(coeffs, pltpu.HBM))
+    rows = coeffs.reshape(4, 8, ROWS * NT_LOCAL, LANES)
+    other_rows = lax.ppermute(rows, "space", [(0, 1), (1, 0)])
+    first, links, staple = pl.pallas_call(
+        first_kernel,
+        out_shape=(block(3, 8, ROWS, LANES), field(4, NT_LOCAL), field(NT_LOCAL)),
+        in_specs=[pl.BlockSpec(memory_space=pltpu.HBM)] * 2,
+        out_specs=(WHOLE, WHOLE, WHOLE),
+        scratch_shapes=[
+            pltpu.VMEM((4, 8, ROWS * NT_LOCAL, LANES), jnp.float32),
+            pltpu.SemaphoreType.DMA,
+        ],
+        compiler_params=params(),
+        cost_estimate=cost(1_000_000_000),
+        name="first_slice",
+    )(
+        pltpu.with_memory_space_constraint(coeffs, pltpu.HBM),
+        pltpu.with_memory_space_constraint(rows, pltpu.HBM),
+    )
     ahead = lax.ppermute(first, "tm", [((i + 1) % count, i) for i in range(count)])
     links, staple = pl.pallas_call(
         local_kernel,
         out_shape=(field(4, NT_LOCAL), field(NT_LOCAL)),
-        in_specs=[WHOLE],
+        in_specs=[WHOLE] * 3,
         out_specs=(WHOLE, WHOLE),
+        input_output_aliases={1: 0, 2: 1},
         compiler_params=params(),
         cost_estimate=cost(20_000_000),
         name="local_terms",
-    )(rows)
+    )(rows, links, staple)
     chain_scratch = [
         pltpu.VMEM((3, 18, ROWS, LANES), jnp.float32),
         pltpu.VMEM((18, ROWS, LANES), jnp.float32),

time: 38.9 us -> 38.4 us (0.987)
  starting transfers between devices: 19.8 us -> 17.1 us
  waiting for transfers between devices: 10.8 us -> 12.3 us
  Pallas kernels: 8.03 us -> 8.91 us
    ppermute x1, starting transfers between devices: 8.83 us -> 4.82 us  [shards(): lax.ppermute(first, 'tm', [((i + 1) % count, i) for i in range(count)])]
    pallas_call x1, Pallas kernels: 1.22 us -> 5.01 us  [shards(): pl.pallas_call(first_kernel, out_shape=(block(3, 8, ROWS, LANES), field(4...]
    pallas_call x1, Pallas kernels: 2.77 us -> 0.01 us  [shards(): pl.pallas_call(local_kernel, out_shape=(field(4, NT_LOCAL), field(NT_LOCA...]
    ppermute x9, starting transfers between devices: 10.7 us -> 12.2 us  [shards(): lax.ppermute(total, 'tm', [(i, i ^ low * k) for i in range(count)])]
    ppermute x1, waiting for transfers between devices: 0.01 us -> 1.21 us  [shards(): lax.ppermute(first, 'tm', [((i + 1) % count, i) for i in range(count)])]
  transfers between devices with their start and end apart: 12 -> 12, of which waited for: 6 -> 9; matrix products, arithmetic and copies ran while one was open for 0% -> 0% of each run, Pallas kernels for 16% -> 19%
where the time goes in v3:
time: 38.4 us; the launch traced here: 38.3 us
  starting transfers between devices  17.1 us (45%)
  waiting for transfers between devices  12.3 us (32%)
  Pallas kernels  8.91 us (23%)
    ppermute x9, starting transfers between devices, shards(): lax.ppermute(total, 'tm', [(i, i ^ low * k) for i in range(count)])  12.2 us
    ppermute x9, waiting for transfers between devices, shards(): lax.ppermute(total, 'tm', [(i, i ^ low * k) for i in range(count)])  10.8 us
    pallas_call x1, Pallas kernels, shards(): pl.pallas_call(first_kernel, out_shape=(block(3, 8, ROWS, LANES), field(4...  5.01 us
    ppermute x1, starting transfers between devices, shards(): lax.ppermute(first, 'tm', [((i + 1) % count, i) for i in range(count)])  4.82 us
    pallas_call x1, Pallas kernels, shards(): pl.pallas_call(late_chain_kernel, out_shape=(field(NT_LOCAL - 1 - SPLIT),...  1.43 us
    ppermute x1, waiting for transfers between devices, shards(): lax.ppermute(first, 'tm', [((i + 1) % count, i) for i in range(count)])  1.21 us
    pallas_call x1, Pallas kernels, shards(): pl.pallas_call(closing, out_shape=block(18, ROWS * NT_LOCAL, LANES), in_s...  1.06 us
    pallas_call x1, Pallas kernels, shards(): pl.pallas_call(early_chain_kernel, out_shape=(field(SPLIT), field()), in_...  0.96 us
  transfers between devices with their start and end apart: 12, of which 9 were waited for; matrix products, arithmetic and copies ran while one was open for 0% of the time, Pallas kernels for 19%

profile of v3, /device:TPU:0, one launch (start us, length us, event | category | flops | bytes accessed | tf_op | source)
XLA Modules:
  0.0 38.3 jit_solution(361500598768643624)
XLA Ops:
  0.0 0.0 collective-permute-start
  0.0 5.0 %first_slice.1 = (f32[3,8,8,128]{3,2,1,0:T(8,128)S(1)}, f32[4,8,18,8,128]{4,3,2,1,0:T(8,128)S(1)}, f32[8,18,8,128]{3,2,1,0:T(8,128)S(1)}) custom-call(f32[4,8,8,8,128]{4,3,2,1,0:T(8,128)} %bitcast.12, f32[4,8,64,128]{3,2,1,0:T(8,128)} %bitcast.11), custom_call_target="tpu_custom_call" | custom-call | flops 1000000000 | bytes 1000000 | tf_op jit(solution)/shard_map/first_slice/pallas_call | solution.py:445
  5.0 4.8 %collective-permute-start.1 = (f32[3,8,8,128]{3,2,1,0:T(8,128)S(1)}, f32[3,8,8,128]{3,2,1,0:T(8,128)S(1)}, u32[]{:S(2)}, u32[]{:S(2)}) collective-permute-start(f32[3,8,8,128]{3,2,1,0:T(8,128)S(1)} %get-tuple-element.26), channel_id=1, source_target_pairs={{2,0},{4,2},{6,4},{8,6},{10,8},{12,10},{14,12},{16,14},{18,16},{20... | collective-permute-start | bytes 294920 | tf_op jit(solution)/shard_map/ppermute | solution.py:461
  9.8 0.0 copy-done
  9.8 0.0 collective-permute-done.rows
  9.8 1.4 %late_chain.1 = (f32[5,18,8,128]{3,2,1,0:T(8,128)S(1)}, f32[2,18,8,128]{3,2,1,0:T(8,128)S(1)}) custom-call(f32[4,8,18,8,128]{4,3,2,1,0:T(8,128)S(1)} %get-tuple-element.22.links, f32[8,18,8,128]{3,2,1,0:T(8,128)S(1)} %get-tuple-element.23.staple, f32[4,8,64,128]{3,2,1,0:T(8,128)S(1)} %collective-permute-done.rows), custom_call_target="tpu_custom_call" | custom-call | flops 8000000 | bytes 1000000 | tf_op jit(solution)/shard_map/late_chain/pallas_call | solution.py:477
  11.3 1.2 %collective-permute-done.1.next_rows.ahead = f32[3,8,8,128]{3,2,1,0:T(8,128)S(1)} collective-permute-done((f32[3,8,8,128]{3,2,1,0:T(8,128)S(1)}, f32[3,8,8,128]{3,2,1,0:T(8,128)S(1)}, u32[]{:S(2)}, u32[]{:S(2)}) %collective-permute-start.1) | collective-permute-done | bytes 98336 | tf_op jit(solution)/shard_map/ppermute | solution.py:461
  12.5 0.0 collective-permute-start.2
  12.5 1.0 %early_chain.1 = (f32[2,18,8,128]{3,2,1,0:T(8,128)S(1)}, f32[18,8,128]{2,1,0:T(8,128)S(1)}) custom-call(f32[4,8,18,8,128]{4,3,2,1,0:T(8,128)S(1)} %get-tuple-element.22.links, f32[8,18,8,128]{3,2,1,0:T(8,128)S(1)} %get-tuple-element.23.staple, f32[4,8,64,128]{3,2,1,0:T(8,128)S(1)} %collective-permute-done.rows, ...), custom_call_target="tpu_custom_call" | custom-call | flops 8000000 | bytes 1000000 | tf_op jit(solution)/shard_map/early_chain/pallas_call | solution.py:496
  13.5 0.2 collective-permute-done.2.other_next
  13.7 0.2 last_slice.1
  13.9 0.1 collective-permute-start.3
  14.0 1.6 %collective-permute-start.4 = (f32[18,8,128]{2,1,0:T(8,128)S(1)}, f32[18,8,128]{2,1,0:T(8,128)S(1)}, u32[]{:S(2)}, u32[]{:S(2)}) collective-permute-start(f32[18,8,128]{2,1,0:T(8,128)S(1)} %get-tuple-element.29.refs_0_), channel_id=1, source_target_pairs={{0,6},{2,4},{4,2},{6,0},{8,14},{10,12},{12,10},{14,8},{16,22},{18,... | collective-permute-start | bytes 221192 | tf_op jit(solution)/shard_map/ppermute | solution.py:520
  15.6 1.9 %collective-permute-start.5 = (f32[18,8,128]{2,1,0:T(8,128)S(1)}, f32[18,8,128]{2,1,0:T(8,128)S(1)}, u32[]{:S(2)}, u32[]{:S(2)}) collective-permute-start(f32[18,8,128]{2,1,0:T(8,128)S(1)} %get-tuple-element.29.refs_0_), channel_id=1, source_target_pairs={{0,2},{2,0},{4,6},{6,4},{8,10},{10,8},{12,14},{14,12},{16,18},{18,... | collective-permute-start | bytes 221192 | tf_op jit(solution)/shard_map/ppermute | solution.py:520
  17.4 3.1 %collective-permute-done.3.refs_1_ = f32[18,8,128]{2,1,0:T(8,128)S(1)} collective-permute-done((f32[18,8,128]{2,1,0:T(8,128)S(1)}, f32[18,8,128]{2,1,0:T(8,128)S(1)}, u32[]{:S(2)}, u32[]{:S(2)}) %collective-permute-start.3) | collective-permute-done | bytes 73760 | tf_op jit(solution)/shard_map/ppermute | solution.py:520
  20.6 0.7 %collective-permute-done.4.refs_2_ = f32[18,8,128]{2,1,0:T(8,128)S(1)} collective-permute-done((f32[18,8,128]{2,1,0:T(8,128)S(1)}, f32[18,8,128]{2,1,0:T(8,128)S(1)}, u32[]{:S(2)}, u32[]{:S(2)}) %collective-permute-start.4) | collective-permute-done | bytes 73760 | tf_op jit(solution)/shard_map/ppermute | solution.py:520
  21.3 0.0 collective-permute-done.5.refs_3_
  21.3 0.1 level_1.1
  21.4 0.1 collective-permute-start.6
  21.5 1.4 %collective-permute-start.7 = (f32[18,8,128]{2,1,0:T(8,128)S(1)}, f32[18,8,128]{2,1,0:T(8,128)S(1)}, u32[]{:S(2)}, u32[]{:S(2)}) collective-permute-start(f32[18,8,128]{2,1,0:T(8,128)S(1)} %get-tuple-element.31.refs_0_), channel_id=1, source_target_pairs={{0,24},{2,26},{4,28},{6,30},{8,16},{10,18},{12,20},{14,22},{16,8},... | collective-permute-start | bytes 221192 | tf_op jit(solution)/shard_map/ppermute | solution.py:520
  23.0 2.0 %collective-permute-start.8 = (f32[18,8,128]{2,1,0:T(8,128)S(1)}, f32[18,8,128]{2,1,0:T(8,128)S(1)}, u32[]{:S(2)}, u32[]{:S(2)}) collective-permute-start(f32[18,8,128]{2,1,0:T(8,128)S(1)} %get-tuple-element.31.refs_0_), channel_id=1, source_target_pairs={{0,8},{2,10},{4,12},{6,14},{8,0},{10,2},{12,4},{14,6},{16,24},{18,... | collective-permute-start | bytes 221192 | tf_op jit(solution)/shard_map/ppermute | solution.py:520
  25.0 3.0 %collective-permute-done.6.refs_1_ = f32[18,8,128]{2,1,0:T(8,128)S(1)} collective-permute-done((f32[18,8,128]{2,1,0:T(8,128)S(1)}, f32[18,8,128]{2,1,0:T(8,128)S(1)}, u32[]{:S(2)}, u32[]{:S(2)}) %collective-permute-start.6) | collective-permute-done | bytes 73760 | tf_op jit(solution)/shard_map/ppermute | solution.py:520
  28.0 0.4 collective-permute-done.7.refs_2_
  28.4 0.0 collective-permute-done.8.refs_3_
  28.4 0.1 level_4.1
  28.5 2.9 %collective-permute-start.10 = (f32[18,8,128]{2,1,0:T(8,128)S(1)}, f32[18,8,128]{2,1,0:T(8,128)S(1)}, u32[]{:S(2)}, u32[]{:S(2)}) collective-permute-start(f32[18,8,128]{2,1,0:T(8,128)S(1)} %get-tuple-element.33.refs_0_), channel_id=1, source_target_pairs={{0,64},{2,66},{4,68},{6,70},{8,72},{10,74},{12,76},{14,78},{16,80}... | collective-permute-start | bytes 221192 | tf_op jit(solution)/shard_map/ppermute | solution.py:520
  31.4 1.5 %collective-permute-start.11 = (f32[18,8,128]{2,1,0:T(8,128)S(1)}, f32[18,8,128]{2,1,0:T(8,128)S(1)}, u32[]{:S(2)}, u32[]{:S(2)}) collective-permute-start(f32[18,8,128]{2,1,0:T(8,128)S(1)} %get-tuple-element.33.refs_0_), channel_id=1, source_target_pairs={{0,96},{2,98},{4,100},{6,102},{8,104},{10,106},{12,108},{14,110},{... | collective-permute-start | bytes 221192 | tf_op jit(solution)/shard_map/ppermute | solution.py:520
  32.9 0.8 %collective-permute-start.9 = (f32[18,8,128]{2,1,0:T(8,128)S(1)}, f32[18,8,128]{2,1,0:T(8,128)S(1)}, u32[]{:S(2)}, u32[]{:S(2)}) collective-permute-start(f32[18,8,128]{2,1,0:T(8,128)S(1)} %get-tuple-element.33.refs_0_), channel_id=1, source_target_pairs={{0,32},{2,34},{4,36},{6,38},{8,40},{10,42},{12,44},{14,46},{16,48}... | collective-permute-start | bytes 221192 | tf_op jit(solution)/shard_map/ppermute | solution.py:520
  33.7 0.9 %collective-permute-done.10.refs_2_ = f32[18,8,128]{2,1,0:T(8,128)S(1)} collective-permute-done((f32[18,8,128]{2,1,0:T(8,128)S(1)}, f32[18,8,128]{2,1,0:T(8,128)S(1)}, u32[]{:S(2)}, u32[]{:S(2)}) %collective-permute-start.10) | collective-permute-done | bytes 73760 | tf_op jit(solution)/shard_map/ppermute | solution.py:520
  34.6 2.4 %collective-permute-done.11.refs_3_ = f32[18,8,128]{2,1,0:T(8,128)S(1)} collective-permute-done((f32[18,8,128]{2,1,0:T(8,128)S(1)}, f32[18,8,128]{2,1,0:T(8,128)S(1)}, u32[]{:S(2)}, u32[]{:S(2)}) %collective-permute-start.11) | collective-permute-done | bytes 73760 | tf_op jit(solution)/shard_map/ppermute | solution.py:520
  37.0 0.3 collective-permute-done.9.refs_1_
  37.2 1.1 %closing.1 = f32[18,64,128]{2,1,0:T(8,128)} custom-call(f32[18,8,128]{2,1,0:T(8,128)S(1)} %get-tuple-element.33.refs_0_, f32[18,8,128]{2,1,0:T(8,128)S(1)} %collective-permute-done.9.refs_1_, f32[18,8,128]{2,1,0:T(8,128)S(1)} %collective-permute-done.10.refs_2_, f32[18,8,128]{2,1,0:T(8,128)S(1)} %collective-permute-done.11.refs_3_, ...), custom_call_target="tpu_custom_call" | custom-call | tf_op jit(solution)/shard_map/closing/pallas_call | solution.py:543
  (3 shorter events, 0.0 us)
Async XLA Ops:
  0.0 9.8 %copy-start = (f32[4,8,1,8,1024]{4,3,2,1,0:T(8,128)S(1)}, f32[4,8,1,8,1024]{4,3,2,1,0:T(8,128)}, u32[]{:S(2)}) copy-start(f32[4,8,1,8,1024]{4,3,2,1,0:T(8,128)} %param.1) | copy-start | bytes 3145732
  0.0 9.8 %collective-permute-start = (f32[4,8,64,128]{3,2,1,0:T(8,128)}, f32[4,8,64,128]{3,2,1,0:T(8,128)S(1)}, u32[]{:S(2)}, u32[]{:S(2)}) collective-permute-start(f32[4,8,64,128]{3,2,1,0:T(8,128)} %bitcast.10), channel_id=1, source_target_pairs={{0,1},{1,0},{2,3},{3,2},{4,5},{5,4},{6,7},{7,6},{8,9},{9,8},{10,11... | collective-permute-start | bytes 3145736 | tf_op jit(solution)/shard_map/ppermute | solution.py:444
  5.0 7.5 %collective-permute-start.1 = (f32[3,8,8,128]{3,2,1,0:T(8,128)S(1)}, f32[3,8,8,128]{3,2,1,0:T(8,128)S(1)}, u32[]{:S(2)}, u32[]{:S(2)}) collective-permute-start(f32[3,8,8,128]{3,2,1,0:T(8,128)S(1)} %get-tuple-element.26), channel_id=1, source_target_pairs={{2,0},{4,2},{6,4},{8,6},{10,8},{12,10},{14,12},{16,14},{18,16},{20... | collective-permute-start | bytes 294920 | tf_op jit(solution)/shard_map/ppermute | solution.py:461
  12.5 1.2 %collective-permute-start.2 = (f32[8,8,128]{2,1,0:T(8,128)S(1)}, f32[8,8,128]{2,1,0:T(8,128)S(1)}, u32[]{:S(2)}, u32[]{:S(2)}) collective-permute-start(f32[8,8,128]{2,1,0:T(8,128)S(1)} %pick.1), channel_id=1, source_target_pairs={{0,1},{1,0},{2,3},{3,2},{4,5},{5,4},{6,7},{7,6},{8,9},{9,8},{10,11... | collective-permute-start | bytes 98312 | tf_op jit(solution)/shard_map/ppermute | solution.py:495
  13.9 6.7 %collective-permute-start.3 = (f32[18,8,128]{2,1,0:T(8,128)S(1)}, f32[18,8,128]{2,1,0:T(8,128)S(1)}, u32[]{:S(2)}, u32[]{:S(2)}) collective-permute-start(f32[18,8,128]{2,1,0:T(8,128)S(1)} %get-tuple-element.29.refs_0_), channel_id=1, source_target_pairs={{0,4},{2,6},{4,0},{6,2},{8,12},{10,14},{12,8},{14,10},{16,20},{18,... | collective-permute-start | bytes 221192 | tf_op jit(solution)/shard_map/ppermute | solution.py:520
  14.0 7.3 %collective-permute-start.4 = (f32[18,8,128]{2,1,0:T(8,128)S(1)}, f32[18,8,128]{2,1,0:T(8,128)S(1)}, u32[]{:S(2)}, u32[]{:S(2)}) collective-permute-start(f32[18,8,128]{2,1,0:T(8,128)S(1)} %get-tuple-element.29.refs_0_), channel_id=1, source_target_pairs={{0,6},{2,4},{4,2},{6,0},{8,14},{10,12},{12,10},{14,8},{16,22},{18,... | collective-permute-start | bytes 221192 | tf_op jit(solution)/shard_map/ppermute | solution.py:520
  15.6 5.7 %collective-permute-start.5 = (f32[18,8,128]{2,1,0:T(8,128)S(1)}, f32[18,8,128]{2,1,0:T(8,128)S(1)}, u32[]{:S(2)}, u32[]{:S(2)}) collective-permute-start(f32[18,8,128]{2,1,0:T(8,128)S(1)} %get-tuple-element.29.refs_0_), channel_id=1, source_target_pairs={{0,2},{2,0},{4,6},{6,4},{8,10},{10,8},{12,14},{14,12},{16,18},{18,... | collective-permute-start | bytes 221192 | tf_op jit(solution)/shard_map/ppermute | solution.py:520
  21.4 6.6 %collective-permute-start.6 = (f32[18,8,128]{2,1,0:T(8,128)S(1)}, f32[18,8,128]{2,1,0:T(8,128)S(1)}, u32[]{:S(2)}, u32[]{:S(2)}) collective-permute-start(f32[18,8,128]{2,1,0:T(8,128)S(1)} %get-tuple-element.31.refs_0_), channel_id=1, source_target_pairs={{0,16},{2,18},{4,20},{6,22},{8,24},{10,26},{12,28},{14,30},{16,0},... | collective-permute-start | bytes 221192 | tf_op jit(solution)/shard_map/ppermute | solution.py:520
  21.5 6.9 %collective-permute-start.7 = (f32[18,8,128]{2,1,0:T(8,128)S(1)}, f32[18,8,128]{2,1,0:T(8,128)S(1)}, u32[]{:S(2)}, u32[]{:S(2)}) collective-permute-start(f32[18,8,128]{2,1,0:T(8,128)S(1)} %get-tuple-element.31.refs_0_), channel_id=1, source_target_pairs={{0,24},{2,26},{4,28},{6,30},{8,16},{10,18},{12,20},{14,22},{16,8},... | collective-permute-start | bytes 221192 | tf_op jit(solution)/shard_map/ppermute | solution.py:520
  23.0 5.4 %collective-permute-start.8 = (f32[18,8,128]{2,1,0:T(8,128)S(1)}, f32[18,8,128]{2,1,0:T(8,128)S(1)}, u32[]{:S(2)}, u32[]{:S(2)}) collective-permute-start(f32[18,8,128]{2,1,0:T(8,128)S(1)} %get-tuple-element.31.refs_0_), channel_id=1, source_target_pairs={{0,8},{2,10},{4,12},{6,14},{8,0},{10,2},{12,4},{14,6},{16,24},{18,... | collective-permute-start | bytes 221192 | tf_op jit(solution)/shard_map/ppermute | solution.py:520
  28.5 6.0 %collective-permute-start.10 = (f32[18,8,128]{2,1,0:T(8,128)S(1)}, f32[18,8,128]{2,1,0:T(8,128)S(1)}, u32[]{:S(2)}, u32[]{:S(2)}) collective-permute-start(f32[18,8,128]{2,1,0:T(8,128)S(1)} %get-tuple-element.33.refs_0_), channel_id=1, source_target_pairs={{0,64},{2,66},{4,68},{6,70},{8,72},{10,74},{12,76},{14,78},{16,80}... | collective-permute-start | bytes 221192 | tf_op jit(solution)/shard_map/ppermute | solution.py:520
  31.4 5.6 %collective-permute-start.11 = (f32[18,8,128]{2,1,0:T(8,128)S(1)}, f32[18,8,128]{2,1,0:T(8,128)S(1)}, u32[]{:S(2)}, u32[]{:S(2)}) collective-permute-start(f32[18,8,128]{2,1,0:T(8,128)S(1)} %get-tuple-element.33.refs_0_), channel_id=1, source_target_pairs={{0,96},{2,98},{4,100},{6,102},{8,104},{10,106},{12,108},{14,110},{... | collective-permute-start | bytes 221192 | tf_op jit(solution)/shard_map/ppermute | solution.py:520
  32.9 4.4 %collective-permute-start.9 = (f32[18,8,128]{2,1,0:T(8,128)S(1)}, f32[18,8,128]{2,1,0:T(8,128)S(1)}, u32[]{:S(2)}, u32[]{:S(2)}) collective-permute-start(f32[18,8,128]{2,1,0:T(8,128)S(1)} %get-tuple-element.33.refs_0_), channel_id=1, source_target_pairs={{0,32},{2,34},{4,36},{6,38},{8,40},{10,42},{12,44},{14,46},{16,48}... | collective-permute-start | bytes 221192 | tf_op jit(solution)/shard_map/ppermute | solution.py:520

commit v4 on v3

--- a/solution.py
+++ b/solution.py
@@ -11,8 +11,8 @@
 NT_LOCAL = 8
 SMEAR = 0.1
 SPLIT = 2
-PEERS = (2, 3, 1)
-LAST_PEERS = (1, 2, 3)
+PEERS = (1, 3, 2)
+LAST_PEERS = (1, 3, 2)
 ROOT_THIRD = 1.0 / 3.0**0.5
 VMEM_LIMIT = 48 * 1024 * 1024
 WHOLE = pl.BlockSpec(memory_space=pltpu.VMEM)
@@ -244,18 +244,17 @@
     return plus(forward, mapped(below, backward_term(spatial, temporal, ahead)))
 
 
-def local_terms(rows, links, staple):
-    last = NT_LOCAL - 1
-
-    def make(t):
+def make_links(rows, links):
+    def step(t, carry):
         for direction in range(4):
             write(links, link_of(slice_of(rows, direction, t)), direction, t)
-
-    make(last)
-
-    def step(i, carry):
-        t = last - 1 - i
-        make(t)
+        return carry
+
+    lax.fori_loop(0, NT_LOCAL, step, 0)
+
+
+def make_staple(links, staple):
+    def step(t, carry):
         terms = plane_terms(
             read(links, 1, t), read(links, 3, t), read(links, 1, t + 1), from_y_above, from_y_below
         )
@@ -266,7 +265,7 @@
         write(staple, plus(read(staple, t), terms), t)
         return carry
 
-    lax.fori_loop(0, last, step, 0)
+    lax.fori_loop(0, NT_LOCAL - 1, step, 0)
 
 
 def first_kernel(coeffs, coeffs_by_row, first, links, staple, rows, sem):
@@ -279,21 +278,33 @@
         fetch = pltpu.make_async_copy(coeffs_by_row, rows, sem)
         fetch.start()
         fetch.wait()
-        local_terms(rows, links, staple)
-
-
-def local_kernel(rows, links_before, staple_before, links, staple):
-    del links_before, staple_before
+        make_links(rows, links)
+        make_staple(links, staple)
+
+
+def links_kernel(rows, links_before, links, sent):
+    del links_before
+    for n, direction in enumerate((0, 3)):
+        for a in range(8):
+            sent[n, a] = rows[direction, a]
 
     @pl.when(lax.axis_index("tm") != 0)
     def _():
-        local_terms(rows, links, staple)
+        make_links(rows, links)
+
+
+def staple_kernel(links, staple_before, staple):
+    del staple_before
+
+    @pl.when(lax.axis_index("tm") != 0)
+    def _():
+        make_staple(links, staple)
 
 
 def chain_steps(high, low, links, staple, rows, other_links, terms, later, put):
     def step(i, carry):
         t = high - 1 - i
-        write(other_links, link_of(slice_of(rows, 3, t)), 1)
+        write(other_links, link_of(slice_of(rows, 1, t)), 1)
         write(other_links, link_of(slice_of(rows, 0, t)), 2)
         write(
             terms,
@@ -322,8 +333,8 @@
 
 def late_chain_kernel(links, staple, rows, partial, other_last, other_links, terms, later):
     last = NT_LOCAL - 1
-    for n, direction in enumerate((0, 3)):
-        write(other_last, link_of(slice_of(rows, direction, last)), n)
+    for n in range(2):
+        write(other_last, link_of(slice_of(rows, n, last)), n)
     write(other_links, read(other_last, 0), 0)
     write(later, unit())
 
@@ -441,7 +452,6 @@
     count = lax.axis_size("tm")
     coeffs = coeffs.reshape(4, 8, NT_LOCAL, ROWS, LANES).swapaxes(2, 3)
     rows = coeffs.reshape(4, 8, ROWS * NT_LOCAL, LANES)
-    other_rows = lax.ppermute(rows, "space", [(0, 1), (1, 0)])
     first, links, staple = pl.pallas_call(
         first_kernel,
         out_shape=(block(3, 8, ROWS, LANES), field(4, NT_LOCAL), field(NT_LOCAL)),
@@ -459,16 +469,27 @@
         pltpu.with_memory_space_constraint(rows, pltpu.HBM),
     )
     ahead = lax.ppermute(first, "tm", [((i + 1) % count, i) for i in range(count)])
-    links, staple = pl.pallas_call(
-        local_kernel,
-        out_shape=(field(4, NT_LOCAL), field(NT_LOCAL)),
-        in_specs=[WHOLE] * 3,
+    links, sent = pl.pallas_call(
+        links_kernel,
+        out_shape=(field(4, NT_LOCAL), block(2, 8, ROWS * NT_LOCAL, LANES)),
+        in_specs=[WHOLE] * 2,
         out_specs=(WHOLE, WHOLE),
-        input_output_aliases={1: 0, 2: 1},
-        compiler_params=params(),
-        cost_estimate=cost(20_000_000),
-        name="local_terms",
-    )(rows, links, staple)
+        input_output_aliases={1: 0},
+        compiler_params=params(),
+        cost_estimate=cost(10_000_000),
+        name="links",
+    )(rows, links)
+    other_rows = lax.ppermute(sent, "space", [(0, 1), (1, 0)])
+    staple = pl.pallas_call(
+        staple_kernel,
+        out_shape=field(NT_LOCAL),
+        in_specs=[WHOLE] * 2,
+        out_specs=WHOLE,
+        input_output_aliases={1: 0},
+        compiler_params=params(),
+        cost_estimate=cost(20_000_000_000),
+        name="staple",
+    )(links, staple)
     chain_scratch = [
         pltpu.VMEM((3, 18, ROWS, LANES), jnp.float32),
         pltpu.VMEM((18, ROWS, LANES), jnp.float32),

time: 38.4 us -> 37.9 us (0.987)
  starting transfers between devices: 17.1 us -> 16 us
  waiting for transfers between devices: 12.3 us -> 12.8 us
    ppermute x1, waiting for transfers between devices: 0.01 us -> 1.87 us  [shards(): other_rows = lax.ppermute(sent, 'space', [(0, 1), (1, 0)])]
    ppermute x9, starting transfers between devices: 12.2 us -> 10.8 us  [shards(): lax.ppermute(total, 'tm', [(i, i ^ low * k) for i in range(count)])]
    ppermute x1, waiting for transfers between devices: 1.21 us -> 0.01 us  [shards(): lax.ppermute(first, 'tm', [((i + 1) % count, i) for i in range(count)])]
  transfers between devices with their start and end apart: 12 -> 12, of which waited for: 9 -> 9; matrix products, arithmetic and copies ran while one was open for 0% -> 0% of each run, Pallas kernels for 19% -> 6%
where the time goes in v4:
time: 37.9 us; the launch traced here: 37.8 us
  starting transfers between devices  16 us (42%)
  waiting for transfers between devices  12.8 us (34%)
  Pallas kernels  8.86 us (23%)
    ppermute x9, waiting for transfers between devices, shards(): lax.ppermute(total, 'tm', [(i, i ^ low * k) for i in range(count)])  10.8 us
    ppermute x9, starting transfers between devices, shards(): lax.ppermute(total, 'tm', [(i, i ^ low * k) for i in range(count)])  10.8 us
    ppermute x1, starting transfers between devices, shards(): lax.ppermute(first, 'tm', [((i + 1) % count, i) for i in range(count)])  4.92 us
    pallas_call x1, Pallas kernels, shards(): pl.pallas_call(first_kernel, out_shape=(block(3, 8, ROWS, LANES), field(4...  4.9 us
    ppermute x1, waiting for transfers between devices, shards(): other_rows = lax.ppermute(sent, 'space', [(0, 1), (1, 0)])  1.87 us
    pallas_call x1, Pallas kernels, shards(): pl.pallas_call(late_chain_kernel, out_shape=(field(NT_LOCAL - 1 - SPLIT),...  1.43 us
    pallas_call x1, Pallas kernels, shards(): pl.pallas_call(closing, out_shape=block(18, ROWS * NT_LOCAL, LANES), in_s...  1.05 us
    pallas_call x1, Pallas kernels, shards(): pl.pallas_call(early_chain_kernel, out_shape=(field(SPLIT), field()), in_...  0.96 us
  transfers between devices with their start and end apart: 12, of which 9 were waited for; matrix products, arithmetic and copies ran while one was open for 0% of the time, Pallas kernels for 6%

profile of v4, /device:TPU:0, one launch (start us, length us, event | category | flops | bytes accessed | tf_op | source)
XLA Modules:
  0.0 37.8 jit_solution(18440805319204444974)
XLA Ops:
  0.0 4.9 %first_slice.1 = (f32[3,8,8,128]{3,2,1,0:T(8,128)S(1)}, f32[4,8,18,8,128]{4,3,2,1,0:T(8,128)S(1)}, f32[8,18,8,128]{3,2,1,0:T(8,128)S(1)}) custom-call(f32[4,8,8,8,128]{4,3,2,1,0:T(8,128)} %bitcast.11, f32[4,8,64,128]{3,2,1,0:T(8,128)} %bitcast.10), custom_call_target="tpu_custom_call" | custom-call | flops 1000000000 | bytes 1000000 | tf_op jit(solution)/shard_map/first_slice/pallas_call | solution.py:455
  4.9 4.9 %collective-permute-start.1 = (f32[3,8,8,128]{3,2,1,0:T(8,128)S(1)}, f32[3,8,8,128]{3,2,1,0:T(8,128)S(1)}, u32[]{:S(2)}, u32[]{:S(2)}) collective-permute-start(f32[3,8,8,128]{3,2,1,0:T(8,128)S(1)} %get-tuple-element.26), channel_id=1, source_target_pairs={{2,0},{4,2},{6,4},{8,6},{10,8},{12,10},{14,12},{16,14},{18,16},{20... | collective-permute-start | bytes 294920 | tf_op jit(solution)/shard_map/ppermute | solution.py:471
  9.8 0.0 copy-done
  9.9 0.1 collective-permute-start
  10.0 1.9 %collective-permute-done.rows = f32[2,8,64,128]{3,2,1,0:T(8,128)S(1)} collective-permute-done((f32[2,8,64,128]{3,2,1,0:T(8,128)S(1)}, f32[2,8,64,128]{3,2,1,0:T(8,128)S(1)}, u32[]{:S(2)}, u32[]{:S(2)}) %collective-permute-start) | collective-permute-done | bytes 524320 | tf_op jit(solution)/shard_map/ppermute | solution.py:482
  11.9 1.4 %late_chain.1 = (f32[5,18,8,128]{3,2,1,0:T(8,128)S(1)}, f32[2,18,8,128]{3,2,1,0:T(8,128)S(1)}) custom-call(f32[4,8,18,8,128]{4,3,2,1,0:T(8,128)S(1)} %get-tuple-element.21.links, f32[8,18,8,128]{3,2,1,0:T(8,128)S(1)} %staple.1, f32[2,8,64,128]{3,2,1,0:T(8,128)S(1)} %collective-permute-done.rows), custom_call_target="tpu_custom_call" | custom-call | flops 8000000 | bytes 1000000 | tf_op jit(solution)/shard_map/late_chain/pallas_call | solution.py:498
  13.3 0.0 collective-permute-done.1.next_rows.ahead
  13.3 0.2 collective-permute-start.2
  13.5 1.0 %early_chain.1 = (f32[2,18,8,128]{3,2,1,0:T(8,128)S(1)}, f32[18,8,128]{2,1,0:T(8,128)S(1)}) custom-call(f32[4,8,18,8,128]{4,3,2,1,0:T(8,128)S(1)} %get-tuple-element.21.links, f32[8,18,8,128]{3,2,1,0:T(8,128)S(1)} %staple.1, f32[2,8,64,128]{3,2,1,0:T(8,128)S(1)} %collective-permute-done.rows, f32[5,18,8,128]{3,2,1,0:T(8,128)S(1)} %get-tuple-element.25.late.after.refs_6_, ...), custom_call_target="tpu_custom_call" | custom-call | flops 8000000 | bytes 1000000 | tf_op jit(solution)/shard_map/early_chain/pallas_call | solution.py:517
  14.5 0.1 collective-permute-done.2.other_next
  14.6 0.2 last_slice.1
  14.8 0.1 collective-permute-start.5
  14.9 0.9 %collective-permute-start.4 = (f32[18,8,128]{2,1,0:T(8,128)S(1)}, f32[18,8,128]{2,1,0:T(8,128)S(1)}, u32[]{:S(2)}, u32[]{:S(2)}) collective-permute-start(f32[18,8,128]{2,1,0:T(8,128)S(1)} %get-tuple-element.29.refs_0_), channel_id=1, source_target_pairs={{0,6},{2,4},{4,2},{6,0},{8,14},{10,12},{12,10},{14,8},{16,22},{18,... | collective-permute-start | bytes 221192 | tf_op jit(solution)/shard_map/ppermute | solution.py:541
  15.8 2.6 %collective-permute-start.3 = (f32[18,8,128]{2,1,0:T(8,128)S(1)}, f32[18,8,128]{2,1,0:T(8,128)S(1)}, u32[]{:S(2)}, u32[]{:S(2)}) collective-permute-start(f32[18,8,128]{2,1,0:T(8,128)S(1)} %get-tuple-element.29.refs_0_), channel_id=1, source_target_pairs={{0,2},{2,0},{4,6},{6,4},{8,10},{10,8},{12,14},{14,12},{16,18},{18,... | collective-permute-start | bytes 221192 | tf_op jit(solution)/shard_map/ppermute | solution.py:541
  18.4 3.1 %collective-permute-done.5.refs_3_ = f32[18,8,128]{2,1,0:T(8,128)S(1)} collective-permute-done((f32[18,8,128]{2,1,0:T(8,128)S(1)}, f32[18,8,128]{2,1,0:T(8,128)S(1)}, u32[]{:S(2)}, u32[]{:S(2)}) %collective-permute-start.5) | collective-permute-done | bytes 73760 | tf_op jit(solution)/shard_map/ppermute | solution.py:541
  21.5 0.7 %collective-permute-done.4.refs_2_ = f32[18,8,128]{2,1,0:T(8,128)S(1)} collective-permute-done((f32[18,8,128]{2,1,0:T(8,128)S(1)}, f32[18,8,128]{2,1,0:T(8,128)S(1)}, u32[]{:S(2)}, u32[]{:S(2)}) %collective-permute-start.4) | collective-permute-done | bytes 73760 | tf_op jit(solution)/shard_map/ppermute | solution.py:541
  22.2 0.0 collective-permute-done.3.refs_1_
  22.2 0.1 level_1.1
  22.4 0.1 collective-permute-start.8
  22.4 0.1 collective-permute-start.7
  22.5 3.4 %collective-permute-start.6 = (f32[18,8,128]{2,1,0:T(8,128)S(1)}, f32[18,8,128]{2,1,0:T(8,128)S(1)}, u32[]{:S(2)}, u32[]{:S(2)}) collective-permute-start(f32[18,8,128]{2,1,0:T(8,128)S(1)} %get-tuple-element.31.refs_0_), channel_id=1, source_target_pairs={{0,8},{2,10},{4,12},{6,14},{8,0},{10,2},{12,4},{14,6},{16,24},{18,... | collective-permute-start | bytes 221192 | tf_op jit(solution)/shard_map/ppermute | solution.py:541
  25.9 3.0 %collective-permute-done.8.refs_3_ = f32[18,8,128]{2,1,0:T(8,128)S(1)} collective-permute-done((f32[18,8,128]{2,1,0:T(8,128)S(1)}, f32[18,8,128]{2,1,0:T(8,128)S(1)}, u32[]{:S(2)}, u32[]{:S(2)}) %collective-permute-start.8) | collective-permute-done | bytes 73760 | tf_op jit(solution)/shard_map/ppermute | solution.py:541
  28.9 0.4 %collective-permute-done.7.refs_2_ = f32[18,8,128]{2,1,0:T(8,128)S(1)} collective-permute-done((f32[18,8,128]{2,1,0:T(8,128)S(1)}, f32[18,8,128]{2,1,0:T(8,128)S(1)}, u32[]{:S(2)}, u32[]{:S(2)}) %collective-permute-start.7) | collective-permute-done | bytes 73760 | tf_op jit(solution)/shard_map/ppermute | solution.py:541
  29.3 0.0 collective-permute-done.6.refs_1_
  29.3 0.1 level_4.1
  29.5 1.5 %collective-permute-start.11 = (f32[18,8,128]{2,1,0:T(8,128)S(1)}, f32[18,8,128]{2,1,0:T(8,128)S(1)}, u32[]{:S(2)}, u32[]{:S(2)}) collective-permute-start(f32[18,8,128]{2,1,0:T(8,128)S(1)} %get-tuple-element.33.refs_0_), channel_id=1, source_target_pairs={{0,64},{2,66},{4,68},{6,70},{8,72},{10,74},{12,76},{14,78},{16,80}... | collective-permute-start | bytes 221192 | tf_op jit(solution)/shard_map/ppermute | solution.py:541
  30.9 1.5 %collective-permute-start.10 = (f32[18,8,128]{2,1,0:T(8,128)S(1)}, f32[18,8,128]{2,1,0:T(8,128)S(1)}, u32[]{:S(2)}, u32[]{:S(2)}) collective-permute-start(f32[18,8,128]{2,1,0:T(8,128)S(1)} %get-tuple-element.33.refs_0_), channel_id=1, source_target_pairs={{0,96},{2,98},{4,100},{6,102},{8,104},{10,106},{12,108},{14,110},{... | collective-permute-start | bytes 221192 | tf_op jit(solution)/shard_map/ppermute | solution.py:541
  32.4 0.8 %collective-permute-start.9 = (f32[18,8,128]{2,1,0:T(8,128)S(1)}, f32[18,8,128]{2,1,0:T(8,128)S(1)}, u32[]{:S(2)}, u32[]{:S(2)}) collective-permute-start(f32[18,8,128]{2,1,0:T(8,128)S(1)} %get-tuple-element.33.refs_0_), channel_id=1, source_target_pairs={{0,32},{2,34},{4,36},{6,38},{8,40},{10,42},{12,44},{14,46},{16,48}... | collective-permute-start | bytes 221192 | tf_op jit(solution)/shard_map/ppermute | solution.py:541
  33.1 2.5 %collective-permute-done.11.refs_3_ = f32[18,8,128]{2,1,0:T(8,128)S(1)} collective-permute-done((f32[18,8,128]{2,1,0:T(8,128)S(1)}, f32[18,8,128]{2,1,0:T(8,128)S(1)}, u32[]{:S(2)}, u32[]{:S(2)}) %collective-permute-start.11) | collective-permute-done | bytes 73760 | tf_op jit(solution)/shard_map/ppermute | solution.py:541
  35.7 0.8 %collective-permute-done.10.refs_2_ = f32[18,8,128]{2,1,0:T(8,128)S(1)} collective-permute-done((f32[18,8,128]{2,1,0:T(8,128)S(1)}, f32[18,8,128]{2,1,0:T(8,128)S(1)}, u32[]{:S(2)}, u32[]{:S(2)}) %collective-permute-start.10) | collective-permute-done | bytes 73760 | tf_op jit(solution)/shard_map/ppermute | solution.py:541
  36.5 0.3 collective-permute-done.9.refs_1_
  36.7 1.1 %closing.1 = f32[18,64,128]{2,1,0:T(8,128)} custom-call(f32[18,8,128]{2,1,0:T(8,128)S(1)} %get-tuple-element.33.refs_0_, f32[18,8,128]{2,1,0:T(8,128)S(1)} %collective-permute-done.9.refs_1_, f32[18,8,128]{2,1,0:T(8,128)S(1)} %collective-permute-done.10.refs_2_, f32[18,8,128]{2,1,0:T(8,128)S(1)} %collective-permute-done.11.refs_3_, ...), custom_call_target="tpu_custom_call" | custom-call | tf_op jit(solution)/shard_map/closing/pallas_call | solution.py:564
  (4 shorter events, 0.1 us)
Async XLA Ops:
  0.0 9.8 %copy-start = (f32[4,8,1,8,1024]{4,3,2,1,0:T(8,128)S(1)}, f32[4,8,1,8,1024]{4,3,2,1,0:T(8,128)}, u32[]{:S(2)}) copy-start(f32[4,8,1,8,1024]{4,3,2,1,0:T(8,128)} %param.1) | copy-start | bytes 3145732
  4.9 8.4 %collective-permute-start.1 = (f32[3,8,8,128]{3,2,1,0:T(8,128)S(1)}, f32[3,8,8,128]{3,2,1,0:T(8,128)S(1)}, u32[]{:S(2)}, u32[]{:S(2)}) collective-permute-start(f32[3,8,8,128]{3,2,1,0:T(8,128)S(1)} %get-tuple-element.26), channel_id=1, source_target_pairs={{2,0},{4,2},{6,4},{8,6},{10,8},{12,10},{14,12},{16,14},{18,16},{20... | collective-permute-start | bytes 294920 | tf_op jit(solution)/shard_map/ppermute | solution.py:471
  9.9 2.0 %collective-permute-start = (f32[2,8,64,128]{3,2,1,0:T(8,128)S(1)}, f32[2,8,64,128]{3,2,1,0:T(8,128)S(1)}, u32[]{:S(2)}, u32[]{:S(2)}) collective-permute-start(f32[2,8,64,128]{3,2,1,0:T(8,128)S(1)} %get-tuple-element.23), channel_id=1, source_target_pairs={{0,1},{1,0},{2,3},{3,2},{4,5},{5,4},{6,7},{7,6},{8,9},{9,8},{10,11... | collective-permute-start | bytes 1572872 | tf_op jit(solution)/shard_map/ppermute | solution.py:482
  13.3 1.3 %collective-permute-start.2 = (f32[8,8,128]{2,1,0:T(8,128)S(1)}, f32[8,8,128]{2,1,0:T(8,128)S(1)}, u32[]{:S(2)}, u32[]{:S(2)}) collective-permute-start(f32[8,8,128]{2,1,0:T(8,128)S(1)} %pick.1), channel_id=1, source_target_pairs={{0,1},{1,0},{2,3},{3,2},{4,5},{5,4},{6,7},{7,6},{8,9},{9,8},{10,11... | collective-permute-start | bytes 98312 | tf_op jit(solution)/shard_map/ppermute | solution.py:516
  14.8 6.7 %collective-permute-start.5 = (f32[18,8,128]{2,1,0:T(8,128)S(1)}, f32[18,8,128]{2,1,0:T(8,128)S(1)}, u32[]{:S(2)}, u32[]{:S(2)}) collective-permute-start(f32[18,8,128]{2,1,0:T(8,128)S(1)} %get-tuple-element.29.refs_0_), channel_id=1, source_target_pairs={{0,4},{2,6},{4,0},{6,2},{8,12},{10,14},{12,8},{14,10},{16,20},{18,... | collective-permute-start | bytes 221192 | tf_op jit(solution)/shard_map/ppermute | solution.py:541
  14.9 7.3 %collective-permute-start.4 = (f32[18,8,128]{2,1,0:T(8,128)S(1)}, f32[18,8,128]{2,1,0:T(8,128)S(1)}, u32[]{:S(2)}, u32[]{:S(2)}) collective-permute-start(f32[18,8,128]{2,1,0:T(8,128)S(1)} %get-tuple-element.29.refs_0_), channel_id=1, source_target_pairs={{0,6},{2,4},{4,2},{6,0},{8,14},{10,12},{12,10},{14,8},{16,22},{18,... | collective-permute-start | bytes 221192 | tf_op jit(solution)/shard_map/ppermute | solution.py:541
  15.8 6.4 %collective-permute-start.3 = (f32[18,8,128]{2,1,0:T(8,128)S(1)}, f32[18,8,128]{2,1,0:T(8,128)S(1)}, u32[]{:S(2)}, u32[]{:S(2)}) collective-permute-start(f32[18,8,128]{2,1,0:T(8,128)S(1)} %get-tuple-element.29.refs_0_), channel_id=1, source_target_pairs={{0,2},{2,0},{4,6},{6,4},{8,10},{10,8},{12,14},{14,12},{16,18},{18,... | collective-permute-start | bytes 221192 | tf_op jit(solution)/shard_map/ppermute | solution.py:541
  22.4 6.6 %collective-permute-start.8 = (f32[18,8,128]{2,1,0:T(8,128)S(1)}, f32[18,8,128]{2,1,0:T(8,128)S(1)}, u32[]{:S(2)}, u32[]{:S(2)}) collective-permute-start(f32[18,8,128]{2,1,0:T(8,128)S(1)} %get-tuple-element.31.refs_0_), channel_id=1, source_target_pairs={{0,16},{2,18},{4,20},{6,22},{8,24},{10,26},{12,28},{14,30},{16,0},... | collective-permute-start | bytes 221192 | tf_op jit(solution)/shard_map/ppermute | solution.py:541
  22.4 6.9 %collective-permute-start.7 = (f32[18,8,128]{2,1,0:T(8,128)S(1)}, f32[18,8,128]{2,1,0:T(8,128)S(1)}, u32[]{:S(2)}, u32[]{:S(2)}) collective-permute-start(f32[18,8,128]{2,1,0:T(8,128)S(1)} %get-tuple-element.31.refs_0_), channel_id=1, source_target_pairs={{0,24},{2,26},{4,28},{6,30},{8,16},{10,18},{12,20},{14,22},{16,8},... | collective-permute-start | bytes 221192 | tf_op jit(solution)/shard_map/ppermute | solution.py:541
  22.5 6.8 %collective-permute-start.6 = (f32[18,8,128]{2,1,0:T(8,128)S(1)}, f32[18,8,128]{2,1,0:T(8,128)S(1)}, u32[]{:S(2)}, u32[]{:S(2)}) collective-permute-start(f32[18,8,128]{2,1,0:T(8,128)S(1)} %get-tuple-element.31.refs_0_), channel_id=1, source_target_pairs={{0,8},{2,10},{4,12},{6,14},{8,0},{10,2},{12,4},{14,6},{16,24},{18,... | collective-permute-start | bytes 221192 | tf_op jit(solution)/shard_map/ppermute | solution.py:541
  29.5 6.2 %collective-permute-start.11 = (f32[18,8,128]{2,1,0:T(8,128)S(1)}, f32[18,8,128]{2,1,0:T(8,128)S(1)}, u32[]{:S(2)}, u32[]{:S(2)}) collective-permute-start(f32[18,8,128]{2,1,0:T(8,128)S(1)} %get-tuple-element.33.refs_0_), channel_id=1, source_target_pairs={{0,64},{2,66},{4,68},{6,70},{8,72},{10,74},{12,76},{14,78},{16,80}... | collective-permute-start | bytes 221192 | tf_op jit(solution)/shard_map/ppermute | solution.py:541
  30.9 5.6 %collective-permute-start.10 = (f32[18,8,128]{2,1,0:T(8,128)S(1)}, f32[18,8,128]{2,1,0:T(8,128)S(1)}, u32[]{:S(2)}, u32[]{:S(2)}) collective-permute-start(f32[18,8,128]{2,1,0:T(8,128)S(1)} %get-tuple-element.33.refs_0_), channel_id=1, source_target_pairs={{0,96},{2,98},{4,100},{6,102},{8,104},{10,106},{12,108},{14,110},{... | collective-permute-start | bytes 221192 | tf_op jit(solution)/shard_map/ppermute | solution.py:541
  32.4 4.4 %collective-permute-start.9 = (f32[18,8,128]{2,1,0:T(8,128)S(1)}, f32[18,8,128]{2,1,0:T(8,128)S(1)}, u32[]{:S(2)}, u32[]{:S(2)}) collective-permute-start(f32[18,8,128]{2,1,0:T(8,128)S(1)} %get-tuple-element.33.refs_0_), channel_id=1, source_target_pairs={{0,32},{2,34},{4,36},{6,38},{8,40},{10,42},{12,44},{14,46},{16,48}... | collective-permute-start | bytes 221192 | tf_op jit(solution)/shard_map/ppermute | solution.py:541

commit v5 on v4

--- a/solution.py
+++ b/solution.py
@@ -273,12 +273,15 @@
     copy.start()
     copy.wait()
 
-    @pl.when(lax.axis_index("tm") == 0)
+    @pl.when(lax.rem(lax.axis_index("tm"), 16) == 0)
     def _():
         fetch = pltpu.make_async_copy(coeffs_by_row, rows, sem)
         fetch.start()
         fetch.wait()
         make_links(rows, links)
+
+    @pl.when(lax.axis_index("tm") == 0)
+    def _():
         make_staple(links, staple)
 
 
@@ -288,7 +291,7 @@
         for a in range(8):
             sent[n, a] = rows[direction, a]
 
-    @pl.when(lax.axis_index("tm") != 0)
+    @pl.when(lax.rem(lax.axis_index("tm"), 16) != 0)
     def _():
         make_links(rows, links)
 
@@ -400,10 +403,14 @@
     return zeroth, 4 + digit
 
 
-def level_kernel(low, own, by1, by2, by3, tail, new_total, new_tail, held):
+def level_kernel(low, own, by1, by2, by3, new_total, suffix, held):
     zeroth, at = suffixes(low, PEERS, own, by1, by2, by3, held)
     write(new_total, mul(zeroth, read(held, 4)))
-    write(new_tail, mul(read(tail), read(held, at)))
+    write(suffix, read(held, at))
+
+
+def tail_kernel(tail, suffix, new_tail):
+    write(new_tail, mul(read(tail), read(suffix)))
 
 
 def closing_kernel(low, own, by1, by2, by3, tail, early, late, out, held, rows, sems):
@@ -547,15 +554,23 @@
         def level(*refs, low=low):
             level_kernel(low, *refs)
 
-        total, tail = pl.pallas_call(
+        total, suffix = pl.pallas_call(
             level,
             out_shape=(field(), field()),
-            in_specs=[WHOLE] * 5,
+            in_specs=[WHOLE] * 4,
             out_specs=(WHOLE, WHOLE),
             scratch_shapes=[held],
             compiler_params=params(),
             name=f"level_{low}",
-        )(total, *received, tail)
+        )(total, *received)
+        tail = pl.pallas_call(
+            tail_kernel,
+            out_shape=field(),
+            in_specs=[WHOLE] * 2,
+            out_specs=WHOLE,
+            compiler_params=params(),
+            name=f"tail_{low}",
+        )(tail, suffix)
         low *= 4
 
     def closing(*refs, low=low):

time: 37.9 us -> 37.9 us (level)
  transfers between devices with their start and end apart: 12 -> 12, of which waited for: 9 -> 9; matrix products, arithmetic and copies ran while one was open for 0% -> 0% of each run, Pallas kernels for 6% -> 7%
where the time goes in v5:
time: 37.9 us; the launch traced here: 37.7 us
  starting transfers between devices  16 us (42%)
  waiting for transfers between devices  12.7 us (34%)
  Pallas kernels  8.88 us (23%)
    ppermute x9, starting transfers between devices, shards(): lax.ppermute(total, 'tm', [(i, i ^ low * k) for i in range(count)])  10.8 us
    ppermute x9, waiting for transfers between devices, shards(): lax.ppermute(total, 'tm', [(i, i ^ low * k) for i in range(count)])  10.7 us
    ppermute x1, starting transfers between devices, shards(): lax.ppermute(first, 'tm', [((i + 1) % count, i) for i in range(count)])  4.93 us
    pallas_call x1, Pallas kernels, shards(): pl.pallas_call(first_kernel, out_shape=(block(3, 8, ROWS, LANES), field(4...  4.9 us
    ppermute x1, waiting for transfers between devices, shards(): other_rows = lax.ppermute(sent, 'space', [(0, 1), (1, 0)])  1.87 us
    pallas_call x1, Pallas kernels, shards(): pl.pallas_call(late_chain_kernel, out_shape=(field(NT_LOCAL - 1 - SPLIT),...  1.43 us
    pallas_call x1, Pallas kernels, shards(): pl.pallas_call(closing, out_shape=block(18, ROWS * NT_LOCAL, LANES), in_s...  1.05 us
    pallas_call x1, Pallas kernels, shards(): pl.pallas_call(early_chain_kernel, out_shape=(field(SPLIT), field()), in_...  0.96 us
  transfers between devices with their start and end apart: 12, of which 9 were waited for; matrix products, arithmetic and copies ran while one was open for 0% of the time, Pallas kernels for 7%

profile of v5, /device:TPU:0, one launch (start us, length us, event | category | flops | bytes accessed | tf_op | source)
XLA Modules:
  0.0 37.7 jit_solution(645355086154954980)
XLA Ops:
  0.0 4.9 %first_slice.1 = (f32[3,8,8,128]{3,2,1,0:T(8,128)S(1)}, f32[4,8,18,8,128]{4,3,2,1,0:T(8,128)S(1)}, f32[8,18,8,128]{3,2,1,0:T(8,128)S(1)}) custom-call(f32[4,8,8,8,128]{4,3,2,1,0:T(8,128)} %bitcast.11, f32[4,8,64,128]{3,2,1,0:T(8,128)} %bitcast.10), custom_call_target="tpu_custom_call" | custom-call | flops 1000000000 | bytes 1000000 | tf_op jit(solution)/shard_map/first_slice/pallas_call | solution.py:462
  4.9 4.9 %collective-permute-start.1 = (f32[3,8,8,128]{3,2,1,0:T(8,128)S(1)}, f32[3,8,8,128]{3,2,1,0:T(8,128)S(1)}, u32[]{:S(2)}, u32[]{:S(2)}) collective-permute-start(f32[3,8,8,128]{3,2,1,0:T(8,128)S(1)} %get-tuple-element.26), channel_id=1, source_target_pairs={{2,0},{4,2},{6,4},{8,6},{10,8},{12,10},{14,12},{16,14},{18,16},{20... | collective-permute-start | bytes 294920 | tf_op jit(solution)/shard_map/ppermute | solution.py:478
  9.8 0.0 copy-done
  9.9 0.1 collective-permute-start
  10.0 1.9 %collective-permute-done.rows = f32[2,8,64,128]{3,2,1,0:T(8,128)S(1)} collective-permute-done((f32[2,8,64,128]{3,2,1,0:T(8,128)S(1)}, f32[2,8,64,128]{3,2,1,0:T(8,128)S(1)}, u32[]{:S(2)}, u32[]{:S(2)}) %collective-permute-start) | collective-permute-done | bytes 524320 | tf_op jit(solution)/shard_map/ppermute | solution.py:489
  11.9 1.4 %late_chain.1 = (f32[5,18,8,128]{3,2,1,0:T(8,128)S(1)}, f32[2,18,8,128]{3,2,1,0:T(8,128)S(1)}) custom-call(f32[4,8,18,8,128]{4,3,2,1,0:T(8,128)S(1)} %get-tuple-element.21.links, f32[8,18,8,128]{3,2,1,0:T(8,128)S(1)} %staple.1, f32[2,8,64,128]{3,2,1,0:T(8,128)S(1)} %collective-permute-done.rows), custom_call_target="tpu_custom_call" | custom-call | flops 8000000 | bytes 1000000 | tf_op jit(solution)/shard_map/late_chain/pallas_call | solution.py:505
  13.3 0.0 collective-permute-done.1.next_rows.ahead
  13.3 0.2 collective-permute-start.2
  13.5 1.0 %early_chain.1 = (f32[2,18,8,128]{3,2,1,0:T(8,128)S(1)}, f32[18,8,128]{2,1,0:T(8,128)S(1)}) custom-call(f32[4,8,18,8,128]{4,3,2,1,0:T(8,128)S(1)} %get-tuple-element.21.links, f32[8,18,8,128]{3,2,1,0:T(8,128)S(1)} %staple.1, f32[2,8,64,128]{3,2,1,0:T(8,128)S(1)} %collective-permute-done.rows, f32[5,18,8,128]{3,2,1,0:T(8,128)S(1)} %get-tuple-element.25.late.after.refs_6_, ...), custom_call_target="tpu_custom_call" | custom-call | flops 8000000 | bytes 1000000 | tf_op jit(solution)/shard_map/early_chain/pallas_call | solution.py:524
  14.5 0.1 collective-permute-done.2.other_next
  14.6 0.2 last_slice.1
  14.8 0.1 collective-permute-start.5
  14.9 0.9 %collective-permute-start.4 = (f32[18,8,128]{2,1,0:T(8,128)S(1)}, f32[18,8,128]{2,1,0:T(8,128)S(1)}, u32[]{:S(2)}, u32[]{:S(2)}) collective-permute-start(f32[18,8,128]{2,1,0:T(8,128)S(1)} %get-tuple-element.29.refs_0_), channel_id=1, source_target_pairs={{0,6},{2,4},{4,2},{6,0},{8,14},{10,12},{12,10},{14,8},{16,22},{18,... | collective-permute-start | bytes 221192 | tf_op jit(solution)/shard_map/ppermute | solution.py:548
  15.8 2.6 %collective-permute-start.3 = (f32[18,8,128]{2,1,0:T(8,128)S(1)}, f32[18,8,128]{2,1,0:T(8,128)S(1)}, u32[]{:S(2)}, u32[]{:S(2)}) collective-permute-start(f32[18,8,128]{2,1,0:T(8,128)S(1)} %get-tuple-element.29.refs_0_), channel_id=1, source_target_pairs={{0,2},{2,0},{4,6},{6,4},{8,10},{10,8},{12,14},{14,12},{16,18},{18,... | collective-permute-start | bytes 221192 | tf_op jit(solution)/shard_map/ppermute | solution.py:548
  18.4 3.1 %collective-permute-done.5.refs_3_ = f32[18,8,128]{2,1,0:T(8,128)S(1)} collective-permute-done((f32[18,8,128]{2,1,0:T(8,128)S(1)}, f32[18,8,128]{2,1,0:T(8,128)S(1)}, u32[]{:S(2)}, u32[]{:S(2)}) %collective-permute-start.5) | collective-permute-done | bytes 73760 | tf_op jit(solution)/shard_map/ppermute | solution.py:548
  21.5 0.7 %collective-permute-done.4.refs_2_ = f32[18,8,128]{2,1,0:T(8,128)S(1)} collective-permute-done((f32[18,8,128]{2,1,0:T(8,128)S(1)}, f32[18,8,128]{2,1,0:T(8,128)S(1)}, u32[]{:S(2)}, u32[]{:S(2)}) %collective-permute-start.4) | collective-permute-done | bytes 73760 | tf_op jit(solution)/shard_map/ppermute | solution.py:548
  22.2 0.0 collective-permute-done.3.refs_1_
  22.2 0.1 level_1.1
  22.3 0.1 collective-permute-start.8
  22.4 0.1 collective-permute-start.7
  22.5 3.4 %collective-permute-start.6 = (f32[18,8,128]{2,1,0:T(8,128)S(1)}, f32[18,8,128]{2,1,0:T(8,128)S(1)}, u32[]{:S(2)}, u32[]{:S(2)}) collective-permute-start(f32[18,8,128]{2,1,0:T(8,128)S(1)} %get-tuple-element.30.refs_0_), channel_id=1, source_target_pairs={{0,8},{2,10},{4,12},{6,14},{8,0},{10,2},{12,4},{14,6},{16,24},{18,... | collective-permute-start | bytes 221192 | tf_op jit(solution)/shard_map/ppermute | solution.py:548
  25.9 3.0 %collective-permute-done.8.refs_3_ = f32[18,8,128]{2,1,0:T(8,128)S(1)} collective-permute-done((f32[18,8,128]{2,1,0:T(8,128)S(1)}, f32[18,8,128]{2,1,0:T(8,128)S(1)}, u32[]{:S(2)}, u32[]{:S(2)}) %collective-permute-start.8) | collective-permute-done | bytes 73760 | tf_op jit(solution)/shard_map/ppermute | solution.py:548
  28.9 0.4 %collective-permute-done.7.refs_2_ = f32[18,8,128]{2,1,0:T(8,128)S(1)} collective-permute-done((f32[18,8,128]{2,1,0:T(8,128)S(1)}, f32[18,8,128]{2,1,0:T(8,128)S(1)}, u32[]{:S(2)}, u32[]{:S(2)}) %collective-permute-start.7) | collective-permute-done | bytes 73760 | tf_op jit(solution)/shard_map/ppermute | solution.py:548
  29.3 0.0 collective-permute-done.6.refs_1_
  29.3 0.1 level_4.1
  29.4 1.5 %collective-permute-start.11 = (f32[18,8,128]{2,1,0:T(8,128)S(1)}, f32[18,8,128]{2,1,0:T(8,128)S(1)}, u32[]{:S(2)}, u32[]{:S(2)}) collective-permute-start(f32[18,8,128]{2,1,0:T(8,128)S(1)} %get-tuple-element.31.refs_0_), channel_id=1, source_target_pairs={{0,64},{2,66},{4,68},{6,70},{8,72},{10,74},{12,76},{14,78},{16,80}... | collective-permute-start | bytes 221192 | tf_op jit(solution)/shard_map/ppermute | solution.py:548
  30.9 1.5 %collective-permute-start.10 = (f32[18,8,128]{2,1,0:T(8,128)S(1)}, f32[18,8,128]{2,1,0:T(8,128)S(1)}, u32[]{:S(2)}, u32[]{:S(2)}) collective-permute-start(f32[18,8,128]{2,1,0:T(8,128)S(1)} %get-tuple-element.31.refs_0_), channel_id=1, source_target_pairs={{0,96},{2,98},{4,100},{6,102},{8,104},{10,106},{12,108},{14,110},{... | collective-permute-start | bytes 221192 | tf_op jit(solution)/shard_map/ppermute | solution.py:548
  32.3 0.8 %collective-permute-start.9 = (f32[18,8,128]{2,1,0:T(8,128)S(1)}, f32[18,8,128]{2,1,0:T(8,128)S(1)}, u32[]{:S(2)}, u32[]{:S(2)}) collective-permute-start(f32[18,8,128]{2,1,0:T(8,128)S(1)} %get-tuple-element.31.refs_0_), channel_id=1, source_target_pairs={{0,32},{2,34},{4,36},{6,38},{8,40},{10,42},{12,44},{14,46},{16,48}... | collective-permute-start | bytes 221192 | tf_op jit(solution)/shard_map/ppermute | solution.py:548
  33.2 2.6 %collective-permute-done.11.refs_3_ = f32[18,8,128]{2,1,0:T(8,128)S(1)} collective-permute-done((f32[18,8,128]{2,1,0:T(8,128)S(1)}, f32[18,8,128]{2,1,0:T(8,128)S(1)}, u32[]{:S(2)}, u32[]{:S(2)}) %collective-permute-start.11) | collective-permute-done | bytes 73760 | tf_op jit(solution)/shard_map/ppermute | solution.py:548
  35.8 0.8 %collective-permute-done.10.refs_2_ = f32[18,8,128]{2,1,0:T(8,128)S(1)} collective-permute-done((f32[18,8,128]{2,1,0:T(8,128)S(1)}, f32[18,8,128]{2,1,0:T(8,128)S(1)}, u32[]{:S(2)}, u32[]{:S(2)}) %collective-permute-start.10) | collective-permute-done | bytes 73760 | tf_op jit(solution)/shard_map/ppermute | solution.py:548
  36.6 0.1 collective-permute-done.9.refs_1_
  36.7 1.1 %closing.1 = f32[18,64,128]{2,1,0:T(8,128)} custom-call(f32[18,8,128]{2,1,0:T(8,128)S(1)} %get-tuple-element.31.refs_0_, f32[18,8,128]{2,1,0:T(8,128)S(1)} %collective-permute-done.9.refs_1_, f32[18,8,128]{2,1,0:T(8,128)S(1)} %collective-permute-done.10.refs_2_, f32[18,8,128]{2,1,0:T(8,128)S(1)} %collective-permute-done.11.refs_3_, ...), custom_call_target="tpu_custom_call" | custom-call | tf_op jit(solution)/shard_map/closing/pallas_call | solution.py:579
  (6 shorter events, 0.1 us)
Async XLA Ops:
  0.0 9.8 %copy-start = (f32[4,8,1,8,1024]{4,3,2,1,0:T(8,128)S(1)}, f32[4,8,1,8,1024]{4,3,2,1,0:T(8,128)}, u32[]{:S(2)}) copy-start(f32[4,8,1,8,1024]{4,3,2,1,0:T(8,128)} %param.1) | copy-start | bytes 3145732
  4.9 8.4 %collective-permute-start.1 = (f32[3,8,8,128]{3,2,1,0:T(8,128)S(1)}, f32[3,8,8,128]{3,2,1,0:T(8,128)S(1)}, u32[]{:S(2)}, u32[]{:S(2)}) collective-permute-start(f32[3,8,8,128]{3,2,1,0:T(8,128)S(1)} %get-tuple-element.26), channel_id=1, source_target_pairs={{2,0},{4,2},{6,4},{8,6},{10,8},{12,10},{14,12},{16,14},{18,16},{20... | collective-permute-start | bytes 294920 | tf_op jit(solution)/shard_map/ppermute | solution.py:478
  9.9 2.0 %collective-permute-start = (f32[2,8,64,128]{3,2,1,0:T(8,128)S(1)}, f32[2,8,64,128]{3,2,1,0:T(8,128)S(1)}, u32[]{:S(2)}, u32[]{:S(2)}) collective-permute-start(f32[2,8,64,128]{3,2,1,0:T(8,128)S(1)} %get-tuple-element.23), channel_id=1, source_target_pairs={{0,1},{1,0},{2,3},{3,2},{4,5},{5,4},{6,7},{7,6},{8,9},{9,8},{10,11... | collective-permute-start | bytes 1572872 | tf_op jit(solution)/shard_map/ppermute | solution.py:489
  13.3 1.3 %collective-permute-start.2 = (f32[8,8,128]{2,1,0:T(8,128)S(1)}, f32[8,8,128]{2,1,0:T(8,128)S(1)}, u32[]{:S(2)}, u32[]{:S(2)}) collective-permute-start(f32[8,8,128]{2,1,0:T(8,128)S(1)} %pick.1), channel_id=1, source_target_pairs={{0,1},{1,0},{2,3},{3,2},{4,5},{5,4},{6,7},{7,6},{8,9},{9,8},{10,11... | collective-permute-start | bytes 98312 | tf_op jit(solution)/shard_map/ppermute | solution.py:523
  14.8 6.7 %collective-permute-start.5 = (f32[18,8,128]{2,1,0:T(8,128)S(1)}, f32[18,8,128]{2,1,0:T(8,128)S(1)}, u32[]{:S(2)}, u32[]{:S(2)}) collective-permute-start(f32[18,8,128]{2,1,0:T(8,128)S(1)} %get-tuple-element.29.refs_0_), channel_id=1, source_target_pairs={{0,4},{2,6},{4,0},{6,2},{8,12},{10,14},{12,8},{14,10},{16,20},{18,... | collective-permute-start | bytes 221192 | tf_op jit(solution)/shard_map/ppermute | solution.py:548
  14.9 7.3 %collective-permute-start.4 = (f32[18,8,128]{2,1,0:T(8,128)S(1)}, f32[18,8,128]{2,1,0:T(8,128)S(1)}, u32[]{:S(2)}, u32[]{:S(2)}) collective-permute-start(f32[18,8,128]{2,1,0:T(8,128)S(1)} %get-tuple-element.29.refs_0_), channel_id=1, source_target_pairs={{0,6},{2,4},{4,2},{6,0},{8,14},{10,12},{12,10},{14,8},{16,22},{18,... | collective-permute-start | bytes 221192 | tf_op jit(solution)/shard_map/ppermute | solution.py:548
  15.8 6.4 %collective-permute-start.3 = (f32[18,8,128]{2,1,0:T(8,128)S(1)}, f32[18,8,128]{2,1,0:T(8,128)S(1)}, u32[]{:S(2)}, u32[]{:S(2)}) collective-permute-start(f32[18,8,128]{2,1,0:T(8,128)S(1)} %get-tuple-element.29.refs_0_), channel_id=1, source_target_pairs={{0,2},{2,0},{4,6},{6,4},{8,10},{10,8},{12,14},{14,12},{16,18},{18,... | collective-permute-start | bytes 221192 | tf_op jit(solution)/shard_map/ppermute | solution.py:548
  22.3 6.6 %collective-permute-start.8 = (f32[18,8,128]{2,1,0:T(8,128)S(1)}, f32[18,8,128]{2,1,0:T(8,128)S(1)}, u32[]{:S(2)}, u32[]{:S(2)}) collective-permute-start(f32[18,8,128]{2,1,0:T(8,128)S(1)} %get-tuple-element.30.refs_0_), channel_id=1, source_target_pairs={{0,16},{2,18},{4,20},{6,22},{8,24},{10,26},{12,28},{14,30},{16,0},... | collective-permute-start | bytes 221192 | tf_op jit(solution)/shard_map/ppermute | solution.py:548
  22.4 6.9 %collective-permute-start.7 = (f32[18,8,128]{2,1,0:T(8,128)S(1)}, f32[18,8,128]{2,1,0:T(8,128)S(1)}, u32[]{:S(2)}, u32[]{:S(2)}) collective-permute-start(f32[18,8,128]{2,1,0:T(8,128)S(1)} %get-tuple-element.30.refs_0_), channel_id=1, source_target_pairs={{0,24},{2,26},{4,28},{6,30},{8,16},{10,18},{12,20},{14,22},{16,8},... | collective-permute-start | bytes 221192 | tf_op jit(solution)/shard_map/ppermute | solution.py:548
  22.5 6.8 %collective-permute-start.6 = (f32[18,8,128]{2,1,0:T(8,128)S(1)}, f32[18,8,128]{2,1,0:T(8,128)S(1)}, u32[]{:S(2)}, u32[]{:S(2)}) collective-permute-start(f32[18,8,128]{2,1,0:T(8,128)S(1)} %get-tuple-element.30.refs_0_), channel_id=1, source_target_pairs={{0,8},{2,10},{4,12},{6,14},{8,0},{10,2},{12,4},{14,6},{16,24},{18,... | collective-permute-start | bytes 221192 | tf_op jit(solution)/shard_map/ppermute | solution.py:548
  29.4 6.4 %collective-permute-start.11 = (f32[18,8,128]{2,1,0:T(8,128)S(1)}, f32[18,8,128]{2,1,0:T(8,128)S(1)}, u32[]{:S(2)}, u32[]{:S(2)}) collective-permute-start(f32[18,8,128]{2,1,0:T(8,128)S(1)} %get-tuple-element.31.refs_0_), channel_id=1, source_target_pairs={{0,64},{2,66},{4,68},{6,70},{8,72},{10,74},{12,76},{14,78},{16,80}... | collective-permute-start | bytes 221192 | tf_op jit(solution)/shard_map/ppermute | solution.py:548
  30.9 5.7 %collective-permute-start.10 = (f32[18,8,128]{2,1,0:T(8,128)S(1)}, f32[18,8,128]{2,1,0:T(8,128)S(1)}, u32[]{:S(2)}, u32[]{:S(2)}) collective-permute-start(f32[18,8,128]{2,1,0:T(8,128)S(1)} %get-tuple-element.31.refs_0_), channel_id=1, source_target_pairs={{0,96},{2,98},{4,100},{6,102},{8,104},{10,106},{12,108},{14,110},{... | collective-permute-start | bytes 221192 | tf_op jit(solution)/shard_map/ppermute | solution.py:548
  32.3 4.4 %collective-permute-start.9 = (f32[18,8,128]{2,1,0:T(8,128)S(1)}, f32[18,8,128]{2,1,0:T(8,128)S(1)}, u32[]{:S(2)}, u32[]{:S(2)}) collective-permute-start(f32[18,8,128]{2,1,0:T(8,128)S(1)} %get-tuple-element.31.refs_0_), channel_id=1, source_target_pairs={{0,32},{2,34},{4,36},{6,38},{8,40},{10,42},{12,44},{14,46},{16,48}... | collective-permute-start | bytes 221192 | tf_op jit(solution)/shard_map/ppermute | solution.py:548

commit v6 on v5

--- a/solution.py
+++ b/solution.py
@@ -338,25 +338,29 @@
     last = NT_LOCAL - 1
     for n in range(2):
         write(other_last, link_of(slice_of(rows, n, last)), n)
-    write(other_links, read(other_last, 0), 0)
-    write(later, unit())
 
     def put(t, product):
         write(partial, product, t - SPLIT)
 
-    chain_steps(last, SPLIT, links, staple, rows, other_links, terms, later, put)
+    @pl.when(lax.axis_index("tm") != 0)
+    def _():
+        write(other_links, read(other_last, 0), 0)
+        write(later, unit())
+        chain_steps(last, SPLIT, links, staple, rows, other_links, terms, later, put)
 
 
 def early_chain_kernel(
     links, staple, rows, late, other_last, next_rows, partial, last_terms, other_links, terms, later, ahead
 ):
-    write(other_links, link_of(slice_of(rows, 0, SPLIT)), 0)
-    write(later, read(late, 0))
-
     def put(t, product):
         write(partial, product, t)
 
-    chain_steps(SPLIT, 0, links, staple, rows, other_links, terms, later, put)
+    @pl.when(lax.axis_index("tm") != 0)
+    def _():
+        write(other_links, link_of(slice_of(rows, 0, SPLIT)), 0)
+        write(later, read(late, 0))
+        chain_steps(SPLIT, 0, links, staple, rows, other_links, terms, later, put)
+
     last = NT_LOCAL - 1
     for direction in range(3):
         write(ahead, link_of([next_rows[direction, a] for a in range(8)]), direction)
@@ -370,6 +374,26 @@
         lambda: forward_term(read(links, 0, last), read(other_last, 1), read(ahead, 0)),
     ):
         write(last_terms, plus(read(last_terms), term()))
+
+
+def first_slab_kernel(
+    links, staple, rows, other_last, late_before, early_before, late, early, other_links, terms, later
+):
+    del late_before, early_before
+
+    def put_late(t, product):
+        write(late, product, t - SPLIT)
+
+    def put_early(t, product):
+        write(early, product, t)
+
+    @pl.when(lax.axis_index("tm") == 0)
+    def _():
+        write(other_links, read(other_last, 0), 0)
+        write(later, unit())
+        last = NT_LOCAL - 1
+        chain_steps(last, SPLIT, links, staple, rows, other_links, terms, later, put_late)
+        chain_steps(SPLIT, 0, links, staple, rows, other_links, terms, later, put_early)
 
 
 def pick_kernel(ahead, after, out):
@@ -541,6 +565,16 @@
         cost_estimate=cost(3_000_000),
         name="last_slice",
     )(links, other_last, last_terms, other_ahead, early)
+    late, early = pl.pallas_call(
+        first_slab_kernel,
+        out_shape=(field(NT_LOCAL - 1 - SPLIT), field(SPLIT)),
+        in_specs=[WHOLE] * 6,
+        out_specs=(WHOLE, WHOLE),
+        input_output_aliases={4: 0, 5: 1},
+        scratch_shapes=chain_scratch,
+        compiler_params=params(),
+        name="first_slab",
+    )(links, staple, other_rows, other_last, late, early)
     low = 1
     while True:
         peers = LAST_PEERS if low * 4 >= count else PEERS

time: 37.9 us -> 37.9 us (level)
  starting transfers between devices: 16 us -> 17.4 us
  waiting for transfers between devices: 12.7 us -> 11.4 us
    ppermute x9, waiting for transfers between devices: 10.7 us -> 8.68 us  [shards(): lax.ppermute(total, 'tm', [(i, i ^ low * k) for i in range(count)])]
    pallas_call x0 -> x1, Pallas kernels: none -> 1.93 us  [shards(): pl.pallas_call(first_slab_kernel, out_shape=(field(NT_LOCAL - 1 - SPLIT),...]
    ppermute x9, starting transfers between devices: 10.8 us -> 12.3 us  [shards(): lax.ppermute(total, 'tm', [(i, i ^ low * k) for i in range(count)])]
    pallas_call x1, Pallas kernels: 1.43 us -> 0.06 us  [shards(): pl.pallas_call(late_chain_kernel, out_shape=(field(NT_LOCAL - 1 - SPLIT),...]
    ppermute x1, waiting for transfers between devices: 0.11 us -> 0.71 us  [shards(): other_ahead = lax.ppermute(ahead_x, 'space', [(0, 1), (1, 0)])]
    pallas_call x1, Pallas kernels: 0.96 us -> 0.38 us  [shards(): pl.pallas_call(early_chain_kernel, out_shape=(field(SPLIT), field()), in_...]
where the time goes in v6:
time: 37.9 us; the launch traced here: 37.8 us
  starting transfers between devices  17.4 us (46%)
  waiting for transfers between devices  11.4 us (30%)
  Pallas kernels  8.87 us (23%)
    ppermute x9, starting transfers between devices, shards(): lax.ppermute(total, 'tm', [(i, i ^ low * k) for i in range(count)])  12.3 us
    ppermute x9, waiting for transfers between devices, shards(): lax.ppermute(total, 'tm', [(i, i ^ low * k) for i in range(count)])  8.68 us
    ppermute x1, starting transfers between devices, shards(): lax.ppermute(first, 'tm', [((i + 1) % count, i) for i in range(count)])  4.93 us
    pallas_call x1, Pallas kernels, shards(): pl.pallas_call(first_kernel, out_shape=(block(3, 8, ROWS, LANES), field(4...  4.9 us
    pallas_call x1, Pallas kernels, shards(): pl.pallas_call(first_slab_kernel, out_shape=(field(NT_LOCAL - 1 - SPLIT),...  1.93 us
    ppermute x1, waiting for transfers between devices, shards(): other_rows = lax.ppermute(sent, 'space', [(0, 1), (1, 0)])  1.87 us
    pallas_call x1, Pallas kernels, shards(): pl.pallas_call(closing, out_shape=block(18, ROWS * NT_LOCAL, LANES), in_s...  1.05 us
  transfers between devices with their start and end apart: 12, of which 9 were waited for; matrix products, arithmetic and copies ran while one was open for 0% of the time, Pallas kernels for 7%

profile of v6, /device:TPU:0, one launch (start us, length us, event | category | flops | bytes accessed | tf_op | source)
XLA Modules:
  0.0 37.8 jit_solution(17208163070095959932)
XLA Ops:
  0.0 4.9 %first_slice.1 = (f32[3,8,8,128]{3,2,1,0:T(8,128)S(1)}, f32[4,8,18,8,128]{4,3,2,1,0:T(8,128)S(1)}, f32[8,18,8,128]{3,2,1,0:T(8,128)S(1)}) custom-call(f32[4,8,8,8,128]{4,3,2,1,0:T(8,128)} %bitcast.11, f32[4,8,64,128]{3,2,1,0:T(8,128)} %bitcast.10), custom_call_target="tpu_custom_call" | custom-call | flops 1000000000 | bytes 1000000 | tf_op jit(solution)/shard_map/first_slice/pallas_call | solution.py:486
  4.9 4.9 %collective-permute-start.1 = (f32[3,8,8,128]{3,2,1,0:T(8,128)S(1)}, f32[3,8,8,128]{3,2,1,0:T(8,128)S(1)}, u32[]{:S(2)}, u32[]{:S(2)}) collective-permute-start(f32[3,8,8,128]{3,2,1,0:T(8,128)S(1)} %get-tuple-element.28), channel_id=1, source_target_pairs={{2,0},{4,2},{6,4},{8,6},{10,8},{12,10},{14,12},{16,14},{18,16},{20... | collective-permute-start | bytes 294920 | tf_op jit(solution)/shard_map/ppermute | solution.py:502
  9.9 0.1 collective-permute-start
  10.0 1.9 %collective-permute-done.rows = f32[2,8,64,128]{3,2,1,0:T(8,128)S(1)} collective-permute-done((f32[2,8,64,128]{3,2,1,0:T(8,128)S(1)}, f32[2,8,64,128]{3,2,1,0:T(8,128)S(1)}, u32[]{:S(2)}, u32[]{:S(2)}) %collective-permute-start) | collective-permute-done | bytes 524320 | tf_op jit(solution)/shard_map/ppermute | solution.py:513
  11.9 0.1 late_chain.1
  11.9 0.1 collective-permute-done.1.next_rows.ahead
  12.1 0.1 collective-permute-start.2
  12.2 0.4 early_chain.1
  12.6 0.7 %collective-permute-done.2.other_next = f32[8,8,128]{2,1,0:T(8,128)S(1)} collective-permute-done((f32[8,8,128]{2,1,0:T(8,128)S(1)}, f32[8,8,128]{2,1,0:T(8,128)S(1)}, u32[]{:S(2)}, u32[]{:S(2)}) %collective-permute-start.2) | collective-permute-done | bytes 32800 | tf_op jit(solution)/shard_map/ppermute | solution.py:547
  13.3 0.2 last_slice.1
  13.4 0.1 collective-permute-start.5
  13.5 2.3 %collective-permute-start.4 = (f32[18,8,128]{2,1,0:T(8,128)S(1)}, f32[18,8,128]{2,1,0:T(8,128)S(1)}, u32[]{:S(2)}, u32[]{:S(2)}) collective-permute-start(f32[18,8,128]{2,1,0:T(8,128)S(1)} %get-tuple-element.31.refs_0_), channel_id=1, source_target_pairs={{0,6},{2,4},{4,2},{6,0},{8,14},{10,12},{12,10},{14,8},{16,22},{18,... | collective-permute-start | bytes 221192 | tf_op jit(solution)/shard_map/ppermute | solution.py:582
  15.8 1.2 %collective-permute-start.3 = (f32[18,8,128]{2,1,0:T(8,128)S(1)}, f32[18,8,128]{2,1,0:T(8,128)S(1)}, u32[]{:S(2)}, u32[]{:S(2)}) collective-permute-start(f32[18,8,128]{2,1,0:T(8,128)S(1)} %get-tuple-element.31.refs_0_), channel_id=1, source_target_pairs={{0,2},{2,0},{4,6},{6,4},{8,10},{10,8},{12,14},{14,12},{16,18},{18,... | collective-permute-start | bytes 221192 | tf_op jit(solution)/shard_map/ppermute | solution.py:582
  17.0 3.0 %collective-permute-done.5.refs_3_ = f32[18,8,128]{2,1,0:T(8,128)S(1)} collective-permute-done((f32[18,8,128]{2,1,0:T(8,128)S(1)}, f32[18,8,128]{2,1,0:T(8,128)S(1)}, u32[]{:S(2)}, u32[]{:S(2)}) %collective-permute-start.5) | collective-permute-done | bytes 73760 | tf_op jit(solution)/shard_map/ppermute | solution.py:582
  20.0 0.7 %collective-permute-done.4.refs_2_ = f32[18,8,128]{2,1,0:T(8,128)S(1)} collective-permute-done((f32[18,8,128]{2,1,0:T(8,128)S(1)}, f32[18,8,128]{2,1,0:T(8,128)S(1)}, u32[]{:S(2)}, u32[]{:S(2)}) %collective-permute-start.4) | collective-permute-done | bytes 73760 | tf_op jit(solution)/shard_map/ppermute | solution.py:582
  20.7 0.0 collective-permute-done.3.refs_1_
  20.7 0.1 level_1.1
  20.9 0.1 collective-permute-start.8
  21.0 1.5 %collective-permute-start.7 = (f32[18,8,128]{2,1,0:T(8,128)S(1)}, f32[18,8,128]{2,1,0:T(8,128)S(1)}, u32[]{:S(2)}, u32[]{:S(2)}) collective-permute-start(f32[18,8,128]{2,1,0:T(8,128)S(1)} %get-tuple-element.32.refs_0_), channel_id=1, source_target_pairs={{0,24},{2,26},{4,28},{6,30},{8,16},{10,18},{12,20},{14,22},{16,8},... | collective-permute-start | bytes 221192 | tf_op jit(solution)/shard_map/ppermute | solution.py:582
  22.4 2.0 %collective-permute-start.6 = (f32[18,8,128]{2,1,0:T(8,128)S(1)}, f32[18,8,128]{2,1,0:T(8,128)S(1)}, u32[]{:S(2)}, u32[]{:S(2)}) collective-permute-start(f32[18,8,128]{2,1,0:T(8,128)S(1)} %get-tuple-element.32.refs_0_), channel_id=1, source_target_pairs={{0,8},{2,10},{4,12},{6,14},{8,0},{10,2},{12,4},{14,6},{16,24},{18,... | collective-permute-start | bytes 221192 | tf_op jit(solution)/shard_map/ppermute | solution.py:582
  24.4 3.0 %collective-permute-done.8.refs_3_ = f32[18,8,128]{2,1,0:T(8,128)S(1)} collective-permute-done((f32[18,8,128]{2,1,0:T(8,128)S(1)}, f32[18,8,128]{2,1,0:T(8,128)S(1)}, u32[]{:S(2)}, u32[]{:S(2)}) %collective-permute-start.8) | collective-permute-done | bytes 73760 | tf_op jit(solution)/shard_map/ppermute | solution.py:582
  27.4 0.4 %collective-permute-done.7.refs_2_ = f32[18,8,128]{2,1,0:T(8,128)S(1)} collective-permute-done((f32[18,8,128]{2,1,0:T(8,128)S(1)}, f32[18,8,128]{2,1,0:T(8,128)S(1)}, u32[]{:S(2)}, u32[]{:S(2)}) %collective-permute-start.7) | collective-permute-done | bytes 73760 | tf_op jit(solution)/shard_map/ppermute | solution.py:582
  27.8 0.0 collective-permute-done.6.refs_1_
  27.8 0.1 level_4.1
  28.0 2.9 %collective-permute-start.11 = (f32[18,8,128]{2,1,0:T(8,128)S(1)}, f32[18,8,128]{2,1,0:T(8,128)S(1)}, u32[]{:S(2)}, u32[]{:S(2)}) collective-permute-start(f32[18,8,128]{2,1,0:T(8,128)S(1)} %get-tuple-element.33.refs_0_), channel_id=1, source_target_pairs={{0,64},{2,66},{4,68},{6,70},{8,72},{10,74},{12,76},{14,78},{16,80}... | collective-permute-start | bytes 221192 | tf_op jit(solution)/shard_map/ppermute | solution.py:582
  30.9 1.5 %collective-permute-start.10 = (f32[18,8,128]{2,1,0:T(8,128)S(1)}, f32[18,8,128]{2,1,0:T(8,128)S(1)}, u32[]{:S(2)}, u32[]{:S(2)}) collective-permute-start(f32[18,8,128]{2,1,0:T(8,128)S(1)} %get-tuple-element.33.refs_0_), channel_id=1, source_target_pairs={{0,96},{2,98},{4,100},{6,102},{8,104},{10,106},{12,108},{14,110},{... | collective-permute-start | bytes 221192 | tf_op jit(solution)/shard_map/ppermute | solution.py:582
  32.3 0.8 %collective-permute-start.9 = (f32[18,8,128]{2,1,0:T(8,128)S(1)}, f32[18,8,128]{2,1,0:T(8,128)S(1)}, u32[]{:S(2)}, u32[]{:S(2)}) collective-permute-start(f32[18,8,128]{2,1,0:T(8,128)S(1)} %get-tuple-element.33.refs_0_), channel_id=1, source_target_pairs={{0,32},{2,34},{4,36},{6,38},{8,40},{10,42},{12,44},{14,46},{16,48}... | collective-permute-start | bytes 221192 | tf_op jit(solution)/shard_map/ppermute | solution.py:582
  33.1 1.9 %first_slab.1 = (f32[5,18,8,128]{3,2,1,0:T(8,128)S(1)}, f32[2,18,8,128]{3,2,1,0:T(8,128)S(1)}) custom-call(f32[4,8,18,8,128]{4,3,2,1,0:T(8,128)S(1)} %get-tuple-element.23.links, f32[8,18,8,128]{3,2,1,0:T(8,128)S(1)} %staple.1, f32[2,8,64,128]{3,2,1,0:T(8,128)S(1)} %collective-permute-done.rows, ...), custom_call_target="tpu_custom_call", output_to_operand_aliasing={{0}: (4, {}), {1}: (5, {})} | custom-call | tf_op jit(solution)/shard_map/first_slab/pallas_call | solution.py:568
  35.1 0.0 collective-permute-done.11.refs_3_
  35.1 1.3 %collective-permute-done.10.refs_2_ = f32[18,8,128]{2,1,0:T(8,128)S(1)} collective-permute-done((f32[18,8,128]{2,1,0:T(8,128)S(1)}, f32[18,8,128]{2,1,0:T(8,128)S(1)}, u32[]{:S(2)}, u32[]{:S(2)}) %collective-permute-start.10) | collective-permute-done | bytes 73760 | tf_op jit(solution)/shard_map/ppermute | solution.py:582
  36.4 0.3 collective-permute-done.9.refs_1_
  36.7 1.1 %closing.1 = f32[18,64,128]{2,1,0:T(8,128)} custom-call(f32[18,8,128]{2,1,0:T(8,128)S(1)} %get-tuple-element.33.refs_0_, f32[18,8,128]{2,1,0:T(8,128)S(1)} %collective-permute-done.9.refs_1_, f32[18,8,128]{2,1,0:T(8,128)S(1)} %collective-permute-done.10.refs_2_, f32[18,8,128]{2,1,0:T(8,128)S(1)} %collective-permute-done.11.refs_3_, ...), custom_call_target="tpu_custom_call" | custom-call | tf_op jit(solution)/shard_map/closing/pallas_call | solution.py:613
  (7 shorter events, 0.1 us)
Async XLA Ops:
  0.0 9.8 %copy-start = (f32[4,8,1,8,1024]{4,3,2,1,0:T(8,128)S(1)}, f32[4,8,1,8,1024]{4,3,2,1,0:T(8,128)}, u32[]{:S(2)}) copy-start(f32[4,8,1,8,1024]{4,3,2,1,0:T(8,128)} %param.1) | copy-start | bytes 3145732
  4.9 7.1 %collective-permute-start.1 = (f32[3,8,8,128]{3,2,1,0:T(8,128)S(1)}, f32[3,8,8,128]{3,2,1,0:T(8,128)S(1)}, u32[]{:S(2)}, u32[]{:S(2)}) collective-permute-start(f32[3,8,8,128]{3,2,1,0:T(8,128)S(1)} %get-tuple-element.28), channel_id=1, source_target_pairs={{2,0},{4,2},{6,4},{8,6},{10,8},{12,10},{14,12},{16,14},{18,16},{20... | collective-permute-start | bytes 294920 | tf_op jit(solution)/shard_map/ppermute | solution.py:502
  9.9 2.0 %collective-permute-start = (f32[2,8,64,128]{3,2,1,0:T(8,128)S(1)}, f32[2,8,64,128]{3,2,1,0:T(8,128)S(1)}, u32[]{:S(2)}, u32[]{:S(2)}) collective-permute-start(f32[2,8,64,128]{3,2,1,0:T(8,128)S(1)} %get-tuple-element.25), channel_id=1, source_target_pairs={{0,1},{1,0},{2,3},{3,2},{4,5},{5,4},{6,7},{7,6},{8,9},{9,8},{10,11... | collective-permute-start | bytes 1572872 | tf_op jit(solution)/shard_map/ppermute | solution.py:513
  12.1 1.2 %collective-permute-start.2 = (f32[8,8,128]{2,1,0:T(8,128)S(1)}, f32[8,8,128]{2,1,0:T(8,128)S(1)}, u32[]{:S(2)}, u32[]{:S(2)}) collective-permute-start(f32[8,8,128]{2,1,0:T(8,128)S(1)} %pick.1), channel_id=1, source_target_pairs={{0,1},{1,0},{2,3},{3,2},{4,5},{5,4},{6,7},{7,6},{8,9},{9,8},{10,11... | collective-permute-start | bytes 98312 | tf_op jit(solution)/shard_map/ppermute | solution.py:547
  13.4 6.6 %collective-permute-start.5 = (f32[18,8,128]{2,1,0:T(8,128)S(1)}, f32[18,8,128]{2,1,0:T(8,128)S(1)}, u32[]{:S(2)}, u32[]{:S(2)}) collective-permute-start(f32[18,8,128]{2,1,0:T(8,128)S(1)} %get-tuple-element.31.refs_0_), channel_id=1, source_target_pairs={{0,4},{2,6},{4,0},{6,2},{8,12},{10,14},{12,8},{14,10},{16,20},{18,... | collective-permute-start | bytes 221192 | tf_op jit(solution)/shard_map/ppermute | solution.py:582
  13.5 7.2 %collective-permute-start.4 = (f32[18,8,128]{2,1,0:T(8,128)S(1)}, f32[18,8,128]{2,1,0:T(8,128)S(1)}, u32[]{:S(2)}, u32[]{:S(2)}) collective-permute-start(f32[18,8,128]{2,1,0:T(8,128)S(1)} %get-tuple-element.31.refs_0_), channel_id=1, source_target_pairs={{0,6},{2,4},{4,2},{6,0},{8,14},{10,12},{12,10},{14,8},{16,22},{18,... | collective-permute-start | bytes 221192 | tf_op jit(solution)/shard_map/ppermute | solution.py:582
  15.8 4.9 %collective-permute-start.3 = (f32[18,8,128]{2,1,0:T(8,128)S(1)}, f32[18,8,128]{2,1,0:T(8,128)S(1)}, u32[]{:S(2)}, u32[]{:S(2)}) collective-permute-start(f32[18,8,128]{2,1,0:T(8,128)S(1)} %get-tuple-element.31.refs_0_), channel_id=1, source_target_pairs={{0,2},{2,0},{4,6},{6,4},{8,10},{10,8},{12,14},{14,12},{16,18},{18,... | collective-permute-start | bytes 221192 | tf_op jit(solution)/shard_map/ppermute | solution.py:582
  20.9 6.6 %collective-permute-start.8 = (f32[18,8,128]{2,1,0:T(8,128)S(1)}, f32[18,8,128]{2,1,0:T(8,128)S(1)}, u32[]{:S(2)}, u32[]{:S(2)}) collective-permute-start(f32[18,8,128]{2,1,0:T(8,128)S(1)} %get-tuple-element.32.refs_0_), channel_id=1, source_target_pairs={{0,16},{2,18},{4,20},{6,22},{8,24},{10,26},{12,28},{14,30},{16,0},... | collective-permute-start | bytes 221192 | tf_op jit(solution)/shard_map/ppermute | solution.py:582
  21.0 6.9 %collective-permute-start.7 = (f32[18,8,128]{2,1,0:T(8,128)S(1)}, f32[18,8,128]{2,1,0:T(8,128)S(1)}, u32[]{:S(2)}, u32[]{:S(2)}) collective-permute-start(f32[18,8,128]{2,1,0:T(8,128)S(1)} %get-tuple-element.32.refs_0_), channel_id=1, source_target_pairs={{0,24},{2,26},{4,28},{6,30},{8,16},{10,18},{12,20},{14,22},{16,8},... | collective-permute-start | bytes 221192 | tf_op jit(solution)/shard_map/ppermute | solution.py:582
  22.4 5.4 %collective-permute-start.6 = (f32[18,8,128]{2,1,0:T(8,128)S(1)}, f32[18,8,128]{2,1,0:T(8,128)S(1)}, u32[]{:S(2)}, u32[]{:S(2)}) collective-permute-start(f32[18,8,128]{2,1,0:T(8,128)S(1)} %get-tuple-element.32.refs_0_), channel_id=1, source_target_pairs={{0,8},{2,10},{4,12},{6,14},{8,0},{10,2},{12,4},{14,6},{16,24},{18,... | collective-permute-start | bytes 221192 | tf_op jit(solution)/shard_map/ppermute | solution.py:582
  28.0 7.2 %collective-permute-start.11 = (f32[18,8,128]{2,1,0:T(8,128)S(1)}, f32[18,8,128]{2,1,0:T(8,128)S(1)}, u32[]{:S(2)}, u32[]{:S(2)}) collective-permute-start(f32[18,8,128]{2,1,0:T(8,128)S(1)} %get-tuple-element.33.refs_0_), channel_id=1, source_target_pairs={{0,64},{2,66},{4,68},{6,70},{8,72},{10,74},{12,76},{14,78},{16,80}... | collective-permute-start | bytes 221192 | tf_op jit(solution)/shard_map/ppermute | solution.py:582
  30.9 5.6 %collective-permute-start.10 = (f32[18,8,128]{2,1,0:T(8,128)S(1)}, f32[18,8,128]{2,1,0:T(8,128)S(1)}, u32[]{:S(2)}, u32[]{:S(2)}) collective-permute-start(f32[18,8,128]{2,1,0:T(8,128)S(1)} %get-tuple-element.33.refs_0_), channel_id=1, source_target_pairs={{0,96},{2,98},{4,100},{6,102},{8,104},{10,106},{12,108},{14,110},{... | collective-permute-start | bytes 221192 | tf_op jit(solution)/shard_map/ppermute | solution.py:582
  32.3 4.4 %collective-permute-start.9 = (f32[18,8,128]{2,1,0:T(8,128)S(1)}, f32[18,8,128]{2,1,0:T(8,128)S(1)}, u32[]{:S(2)}, u32[]{:S(2)}) collective-permute-start(f32[18,8,128]{2,1,0:T(8,128)S(1)} %get-tuple-element.33.refs_0_), channel_id=1, source_target_pairs={{0,32},{2,34},{4,36},{6,38},{8,40},{10,42},{12,44},{14,46},{16,48}... | collective-permute-start | bytes 221192 | tf_op jit(solution)/shard_map/ppermute | solution.py:582

commit v7 on v5

--- a/solution.py
+++ b/solution.py
@@ -10,7 +10,7 @@
 ROWS = 8
 NT_LOCAL = 8
 SMEAR = 0.1
-SPLIT = 2
+SPLIT = 1
 PEERS = (1, 3, 2)
 LAST_PEERS = (1, 3, 2)
 ROOT_THIRD = 1.0 / 3.0**0.5

time: 37.9 us -> 37.9 us (level)
  transfers between devices with their start and end apart: 12 -> 12, of which waited for: 9 -> 8; matrix products, arithmetic and copies ran while one was open for 0% -> 0% of each run, Pallas kernels for 7% -> 7%
where the time goes in v7:
time: 37.9 us; the launch traced here: 37.7 us
  starting transfers between devices  15.9 us (42%)
  waiting for transfers between devices  12.9 us (34%)
  Pallas kernels  8.85 us (23%)
    ppermute x9, starting transfers between devices, shards(): lax.ppermute(total, 'tm', [(i, i ^ low * k) for i in range(count)])  10.7 us
    ppermute x9, waiting for transfers between devices, shards(): lax.ppermute(total, 'tm', [(i, i ^ low * k) for i in range(count)])  10.6 us
    ppermute x1, starting transfers between devices, shards(): lax.ppermute(first, 'tm', [((i + 1) % count, i) for i in range(count)])  4.93 us
    pallas_call x1, Pallas kernels, shards(): pl.pallas_call(first_kernel, out_shape=(block(3, 8, ROWS, LANES), field(4...  4.89 us
    ppermute x1, waiting for transfers between devices, shards(): other_rows = lax.ppermute(sent, 'space', [(0, 1), (1, 0)])  1.87 us
    pallas_call x1, Pallas kernels, shards(): pl.pallas_call(late_chain_kernel, out_shape=(field(NT_LOCAL - 1 - SPLIT),...  1.71 us
    pallas_call x1, Pallas kernels, shards(): pl.pallas_call(closing, out_shape=block(18, ROWS * NT_LOCAL, LANES), in_s...  1.05 us
  transfers between devices with their start and end apart: 12, of which 8 were waited for; matrix products, arithmetic and copies ran while one was open for 0% of the time, Pallas kernels for 7%

profile of v7, /device:TPU:0, one launch (start us, length us, event | category | flops | bytes accessed | tf_op | source)
XLA Modules:
  0.0 37.7 jit_solution(17850854786448869642)
XLA Ops:
  0.0 4.9 %first_slice.1 = (f32[3,8,8,128]{3,2,1,0:T(8,128)S(1)}, f32[4,8,18,8,128]{4,3,2,1,0:T(8,128)S(1)}, f32[8,18,8,128]{3,2,1,0:T(8,128)S(1)}) custom-call(f32[4,8,8,8,128]{4,3,2,1,0:T(8,128)} %bitcast.11, f32[4,8,64,128]{3,2,1,0:T(8,128)} %bitcast.10), custom_call_target="tpu_custom_call" | custom-call | flops 1000000000 | bytes 1000000 | tf_op jit(solution)/shard_map/first_slice/pallas_call | solution.py:462
  4.9 4.9 %collective-permute-start.1 = (f32[3,8,8,128]{3,2,1,0:T(8,128)S(1)}, f32[3,8,8,128]{3,2,1,0:T(8,128)S(1)}, u32[]{:S(2)}, u32[]{:S(2)}) collective-permute-start(f32[3,8,8,128]{3,2,1,0:T(8,128)S(1)} %get-tuple-element.26), channel_id=1, source_target_pairs={{2,0},{4,2},{6,4},{8,6},{10,8},{12,10},{14,12},{16,14},{18,16},{20... | collective-permute-start | bytes 294920 | tf_op jit(solution)/shard_map/ppermute | solution.py:478
  9.8 0.0 copy-done
  9.9 0.1 collective-permute-start
  10.0 1.9 %collective-permute-done.rows = f32[2,8,64,128]{3,2,1,0:T(8,128)S(1)} collective-permute-done((f32[2,8,64,128]{3,2,1,0:T(8,128)S(1)}, f32[2,8,64,128]{3,2,1,0:T(8,128)S(1)}, u32[]{:S(2)}, u32[]{:S(2)}) %collective-permute-start) | collective-permute-done | bytes 524320 | tf_op jit(solution)/shard_map/ppermute | solution.py:489
  11.9 1.7 %late_chain.1 = (f32[6,18,8,128]{3,2,1,0:T(8,128)S(1)}, f32[2,18,8,128]{3,2,1,0:T(8,128)S(1)}) custom-call(f32[4,8,18,8,128]{4,3,2,1,0:T(8,128)S(1)} %get-tuple-element.21.links, f32[8,18,8,128]{3,2,1,0:T(8,128)S(1)} %staple.1, f32[2,8,64,128]{3,2,1,0:T(8,128)S(1)} %collective-permute-done.rows), custom_call_target="tpu_custom_call" | custom-call | flops 8000000 | bytes 1000000 | tf_op jit(solution)/shard_map/late_chain/pallas_call | solution.py:505
  13.6 0.0 collective-permute-done.1.next_rows.ahead
  13.6 0.2 collective-permute-start.2
  13.8 0.7 %early_chain.1 = (f32[1,18,8,128]{3,2,1,0:T(8,128)S(1)}, f32[18,8,128]{2,1,0:T(8,128)S(1)}) custom-call(f32[4,8,18,8,128]{4,3,2,1,0:T(8,128)S(1)} %get-tuple-element.21.links, f32[8,18,8,128]{3,2,1,0:T(8,128)S(1)} %staple.1, f32[2,8,64,128]{3,2,1,0:T(8,128)S(1)} %collective-permute-done.rows, f32[6,18,8,128]{3,2,1,0:T(8,128)S(1)} %get-tuple-element.25.late.after.refs_6_, ...), custom_call_target="tpu_custom_call" | custom-call | flops 8000000 | bytes 1000000 | tf_op jit(solution)/shard_map/early_chain/pallas_call | solution.py:524
  14.5 0.4 %collective-permute-done.2.other_next = f32[8,8,128]{2,1,0:T(8,128)S(1)} collective-permute-done((f32[8,8,128]{2,1,0:T(8,128)S(1)}, f32[8,8,128]{2,1,0:T(8,128)S(1)}, u32[]{:S(2)}, u32[]{:S(2)}) %collective-permute-start.2) | collective-permute-done | bytes 32800 | tf_op jit(solution)/shard_map/ppermute | solution.py:523
  14.9 0.2 last_slice.1
  15.1 0.1 collective-permute-start.5
  15.2 0.8 %collective-permute-start.4 = (f32[18,8,128]{2,1,0:T(8,128)S(1)}, f32[18,8,128]{2,1,0:T(8,128)S(1)}, u32[]{:S(2)}, u32[]{:S(2)}) collective-permute-start(f32[18,8,128]{2,1,0:T(8,128)S(1)} %get-tuple-element.29.refs_0_), channel_id=1, source_target_pairs={{0,6},{2,4},{4,2},{6,0},{8,14},{10,12},{12,10},{14,8},{16,22},{18,... | collective-permute-start | bytes 221192 | tf_op jit(solution)/shard_map/ppermute | solution.py:548
  15.9 2.7 %collective-permute-start.3 = (f32[18,8,128]{2,1,0:T(8,128)S(1)}, f32[18,8,128]{2,1,0:T(8,128)S(1)}, u32[]{:S(2)}, u32[]{:S(2)}) collective-permute-start(f32[18,8,128]{2,1,0:T(8,128)S(1)} %get-tuple-element.29.refs_0_), channel_id=1, source_target_pairs={{0,2},{2,0},{4,6},{6,4},{8,10},{10,8},{12,14},{14,12},{16,18},{18,... | collective-permute-start | bytes 221192 | tf_op jit(solution)/shard_map/ppermute | solution.py:548
  18.6 3.0 %collective-permute-done.5.refs_3_ = f32[18,8,128]{2,1,0:T(8,128)S(1)} collective-permute-done((f32[18,8,128]{2,1,0:T(8,128)S(1)}, f32[18,8,128]{2,1,0:T(8,128)S(1)}, u32[]{:S(2)}, u32[]{:S(2)}) %collective-permute-start.5) | collective-permute-done | bytes 73760 | tf_op jit(solution)/shard_map/ppermute | solution.py:548
  21.6 0.7 %collective-permute-done.4.refs_2_ = f32[18,8,128]{2,1,0:T(8,128)S(1)} collective-permute-done((f32[18,8,128]{2,1,0:T(8,128)S(1)}, f32[18,8,128]{2,1,0:T(8,128)S(1)}, u32[]{:S(2)}, u32[]{:S(2)}) %collective-permute-start.4) | collective-permute-done | bytes 73760 | tf_op jit(solution)/shard_map/ppermute | solution.py:548
  22.4 0.0 collective-permute-done.3.refs_1_
  22.4 0.1 level_1.1
  22.5 0.1 collective-permute-start.8
  22.6 0.1 collective-permute-start.7
  22.7 3.4 %collective-permute-start.6 = (f32[18,8,128]{2,1,0:T(8,128)S(1)}, f32[18,8,128]{2,1,0:T(8,128)S(1)}, u32[]{:S(2)}, u32[]{:S(2)}) collective-permute-start(f32[18,8,128]{2,1,0:T(8,128)S(1)} %get-tuple-element.30.refs_0_), channel_id=1, source_target_pairs={{0,8},{2,10},{4,12},{6,14},{8,0},{10,2},{12,4},{14,6},{16,24},{18,... | collective-permute-start | bytes 221192 | tf_op jit(solution)/shard_map/ppermute | solution.py:548
  26.1 3.0 %collective-permute-done.8.refs_3_ = f32[18,8,128]{2,1,0:T(8,128)S(1)} collective-permute-done((f32[18,8,128]{2,1,0:T(8,128)S(1)}, f32[18,8,128]{2,1,0:T(8,128)S(1)}, u32[]{:S(2)}, u32[]{:S(2)}) %collective-permute-start.8) | collective-permute-done | bytes 73760 | tf_op jit(solution)/shard_map/ppermute | solution.py:548
  29.1 0.4 %collective-permute-done.7.refs_2_ = f32[18,8,128]{2,1,0:T(8,128)S(1)} collective-permute-done((f32[18,8,128]{2,1,0:T(8,128)S(1)}, f32[18,8,128]{2,1,0:T(8,128)S(1)}, u32[]{:S(2)}, u32[]{:S(2)}) %collective-permute-start.7) | collective-permute-done | bytes 73760 | tf_op jit(solution)/shard_map/ppermute | solution.py:548
  29.5 0.0 collective-permute-done.6.refs_1_
  29.5 0.1 level_4.1
  29.6 1.2 %collective-permute-start.11 = (f32[18,8,128]{2,1,0:T(8,128)S(1)}, f32[18,8,128]{2,1,0:T(8,128)S(1)}, u32[]{:S(2)}, u32[]{:S(2)}) collective-permute-start(f32[18,8,128]{2,1,0:T(8,128)S(1)} %get-tuple-element.31.refs_0_), channel_id=1, source_target_pairs={{0,64},{2,66},{4,68},{6,70},{8,72},{10,74},{12,76},{14,78},{16,80}... | collective-permute-start | bytes 221192 | tf_op jit(solution)/shard_map/ppermute | solution.py:548
  30.8 1.5 %collective-permute-start.10 = (f32[18,8,128]{2,1,0:T(8,128)S(1)}, f32[18,8,128]{2,1,0:T(8,128)S(1)}, u32[]{:S(2)}, u32[]{:S(2)}) collective-permute-start(f32[18,8,128]{2,1,0:T(8,128)S(1)} %get-tuple-element.31.refs_0_), channel_id=1, source_target_pairs={{0,96},{2,98},{4,100},{6,102},{8,104},{10,106},{12,108},{14,110},{... | collective-permute-start | bytes 221192 | tf_op jit(solution)/shard_map/ppermute | solution.py:548
  32.2 0.9 %collective-permute-start.9 = (f32[18,8,128]{2,1,0:T(8,128)S(1)}, f32[18,8,128]{2,1,0:T(8,128)S(1)}, u32[]{:S(2)}, u32[]{:S(2)}) collective-permute-start(f32[18,8,128]{2,1,0:T(8,128)S(1)} %get-tuple-element.31.refs_0_), channel_id=1, source_target_pairs={{0,32},{2,34},{4,36},{6,38},{8,40},{10,42},{12,44},{14,46},{16,48}... | collective-permute-start | bytes 221192 | tf_op jit(solution)/shard_map/ppermute | solution.py:548
  33.2 2.7 %collective-permute-done.11.refs_3_ = f32[18,8,128]{2,1,0:T(8,128)S(1)} collective-permute-done((f32[18,8,128]{2,1,0:T(8,128)S(1)}, f32[18,8,128]{2,1,0:T(8,128)S(1)}, u32[]{:S(2)}, u32[]{:S(2)}) %collective-permute-start.11) | collective-permute-done | bytes 73760 | tf_op jit(solution)/shard_map/ppermute | solution.py:548
  36.0 0.7 %collective-permute-done.10.refs_2_ = f32[18,8,128]{2,1,0:T(8,128)S(1)} collective-permute-done((f32[18,8,128]{2,1,0:T(8,128)S(1)}, f32[18,8,128]{2,1,0:T(8,128)S(1)}, u32[]{:S(2)}, u32[]{:S(2)}) %collective-permute-start.10) | collective-permute-done | bytes 73760 | tf_op jit(solution)/shard_map/ppermute | solution.py:548
  36.7 0.0 collective-permute-done.9.refs_1_
  36.7 1.1 %closing.1 = f32[18,64,128]{2,1,0:T(8,128)} custom-call(f32[18,8,128]{2,1,0:T(8,128)S(1)} %get-tuple-element.31.refs_0_, f32[18,8,128]{2,1,0:T(8,128)S(1)} %collective-permute-done.9.refs_1_, f32[18,8,128]{2,1,0:T(8,128)S(1)} %collective-permute-done.10.refs_2_, f32[18,8,128]{2,1,0:T(8,128)S(1)} %collective-permute-done.11.refs_3_, ...), custom_call_target="tpu_custom_call" | custom-call | tf_op jit(solution)/shard_map/closing/pallas_call | solution.py:579
  (6 shorter events, 0.1 us)
Async XLA Ops:
  0.0 9.8 %copy-start = (f32[4,8,1,8,1024]{4,3,2,1,0:T(8,128)S(1)}, f32[4,8,1,8,1024]{4,3,2,1,0:T(8,128)}, u32[]{:S(2)}) copy-start(f32[4,8,1,8,1024]{4,3,2,1,0:T(8,128)} %param.1) | copy-start | bytes 3145732
  4.9 8.7 %collective-permute-start.1 = (f32[3,8,8,128]{3,2,1,0:T(8,128)S(1)}, f32[3,8,8,128]{3,2,1,0:T(8,128)S(1)}, u32[]{:S(2)}, u32[]{:S(2)}) collective-permute-start(f32[3,8,8,128]{3,2,1,0:T(8,128)S(1)} %get-tuple-element.26), channel_id=1, source_target_pairs={{2,0},{4,2},{6,4},{8,6},{10,8},{12,10},{14,12},{16,14},{18,16},{20... | collective-permute-start | bytes 294920 | tf_op jit(solution)/shard_map/ppermute | solution.py:478
  9.9 2.0 %collective-permute-start = (f32[2,8,64,128]{3,2,1,0:T(8,128)S(1)}, f32[2,8,64,128]{3,2,1,0:T(8,128)S(1)}, u32[]{:S(2)}, u32[]{:S(2)}) collective-permute-start(f32[2,8,64,128]{3,2,1,0:T(8,128)S(1)} %get-tuple-element.23), channel_id=1, source_target_pairs={{0,1},{1,0},{2,3},{3,2},{4,5},{5,4},{6,7},{7,6},{8,9},{9,8},{10,11... | collective-permute-start | bytes 1572872 | tf_op jit(solution)/shard_map/ppermute | solution.py:489
  13.6 1.3 %collective-permute-start.2 = (f32[8,8,128]{2,1,0:T(8,128)S(1)}, f32[8,8,128]{2,1,0:T(8,128)S(1)}, u32[]{:S(2)}, u32[]{:S(2)}) collective-permute-start(f32[8,8,128]{2,1,0:T(8,128)S(1)} %pick.1), channel_id=1, source_target_pairs={{0,1},{1,0},{2,3},{3,2},{4,5},{5,4},{6,7},{7,6},{8,9},{9,8},{10,11... | collective-permute-start | bytes 98312 | tf_op jit(solution)/shard_map/ppermute | solution.py:523
  15.1 6.6 %collective-permute-start.5 = (f32[18,8,128]{2,1,0:T(8,128)S(1)}, f32[18,8,128]{2,1,0:T(8,128)S(1)}, u32[]{:S(2)}, u32[]{:S(2)}) collective-permute-start(f32[18,8,128]{2,1,0:T(8,128)S(1)} %get-tuple-element.29.refs_0_), channel_id=1, source_target_pairs={{0,4},{2,6},{4,0},{6,2},{8,12},{10,14},{12,8},{14,10},{16,20},{18,... | collective-permute-start | bytes 221192 | tf_op jit(solution)/shard_map/ppermute | solution.py:548
  15.2 7.2 %collective-permute-start.4 = (f32[18,8,128]{2,1,0:T(8,128)S(1)}, f32[18,8,128]{2,1,0:T(8,128)S(1)}, u32[]{:S(2)}, u32[]{:S(2)}) collective-permute-start(f32[18,8,128]{2,1,0:T(8,128)S(1)} %get-tuple-element.29.refs_0_), channel_id=1, source_target_pairs={{0,6},{2,4},{4,2},{6,0},{8,14},{10,12},{12,10},{14,8},{16,22},{18,... | collective-permute-start | bytes 221192 | tf_op jit(solution)/shard_map/ppermute | solution.py:548
  15.9 6.4 %collective-permute-start.3 = (f32[18,8,128]{2,1,0:T(8,128)S(1)}, f32[18,8,128]{2,1,0:T(8,128)S(1)}, u32[]{:S(2)}, u32[]{:S(2)}) collective-permute-start(f32[18,8,128]{2,1,0:T(8,128)S(1)} %get-tuple-element.29.refs_0_), channel_id=1, source_target_pairs={{0,2},{2,0},{4,6},{6,4},{8,10},{10,8},{12,14},{14,12},{16,18},{18,... | collective-permute-start | bytes 221192 | tf_op jit(solution)/shard_map/ppermute | solution.py:548
  22.5 6.6 %collective-permute-start.8 = (f32[18,8,128]{2,1,0:T(8,128)S(1)}, f32[18,8,128]{2,1,0:T(8,128)S(1)}, u32[]{:S(2)}, u32[]{:S(2)}) collective-permute-start(f32[18,8,128]{2,1,0:T(8,128)S(1)} %get-tuple-element.30.refs_0_), channel_id=1, source_target_pairs={{0,16},{2,18},{4,20},{6,22},{8,24},{10,26},{12,28},{14,30},{16,0},... | collective-permute-start | bytes 221192 | tf_op jit(solution)/shard_map/ppermute | solution.py:548
  22.6 6.9 %collective-permute-start.7 = (f32[18,8,128]{2,1,0:T(8,128)S(1)}, f32[18,8,128]{2,1,0:T(8,128)S(1)}, u32[]{:S(2)}, u32[]{:S(2)}) collective-permute-start(f32[18,8,128]{2,1,0:T(8,128)S(1)} %get-tuple-element.30.refs_0_), channel_id=1, source_target_pairs={{0,24},{2,26},{4,28},{6,30},{8,16},{10,18},{12,20},{14,22},{16,8},... | collective-permute-start | bytes 221192 | tf_op jit(solution)/shard_map/ppermute | solution.py:548
  22.7 6.8 %collective-permute-start.6 = (f32[18,8,128]{2,1,0:T(8,128)S(1)}, f32[18,8,128]{2,1,0:T(8,128)S(1)}, u32[]{:S(2)}, u32[]{:S(2)}) collective-permute-start(f32[18,8,128]{2,1,0:T(8,128)S(1)} %get-tuple-element.30.refs_0_), channel_id=1, source_target_pairs={{0,8},{2,10},{4,12},{6,14},{8,0},{10,2},{12,4},{14,6},{16,24},{18,... | collective-permute-start | bytes 221192 | tf_op jit(solution)/shard_map/ppermute | solution.py:548
  29.6 6.4 %collective-permute-start.11 = (f32[18,8,128]{2,1,0:T(8,128)S(1)}, f32[18,8,128]{2,1,0:T(8,128)S(1)}, u32[]{:S(2)}, u32[]{:S(2)}) collective-permute-start(f32[18,8,128]{2,1,0:T(8,128)S(1)} %get-tuple-element.31.refs_0_), channel_id=1, source_target_pairs={{0,64},{2,66},{4,68},{6,70},{8,72},{10,74},{12,76},{14,78},{16,80}... | collective-permute-start | bytes 221192 | tf_op jit(solution)/shard_map/ppermute | solution.py:548
  30.8 5.9 %collective-permute-start.10 = (f32[18,8,128]{2,1,0:T(8,128)S(1)}, f32[18,8,128]{2,1,0:T(8,128)S(1)}, u32[]{:S(2)}, u32[]{:S(2)}) collective-permute-start(f32[18,8,128]{2,1,0:T(8,128)S(1)} %get-tuple-element.31.refs_0_), channel_id=1, source_target_pairs={{0,96},{2,98},{4,100},{6,102},{8,104},{10,106},{12,108},{14,110},{... | collective-permute-start | bytes 221192 | tf_op jit(solution)/shard_map/ppermute | solution.py:548
  32.2 4.5 %collective-permute-start.9 = (f32[18,8,128]{2,1,0:T(8,128)S(1)}, f32[18,8,128]{2,1,0:T(8,128)S(1)}, u32[]{:S(2)}, u32[]{:S(2)}) collective-permute-start(f32[18,8,128]{2,1,0:T(8,128)S(1)} %get-tuple-element.31.refs_0_), channel_id=1, source_target_pairs={{0,32},{2,34},{4,36},{6,38},{8,40},{10,42},{12,44},{14,46},{16,48}... | collective-permute-start | bytes 221192 | tf_op jit(solution)/shard_map/ppermute | solution.py:548
